TPU v7x, 32 devices: a whole 2x2x4 slice. The times are simulated.
32 devices in a mesh: dp: 4 (over z), seq: 2 (over x), fsdp: 4 (over y, core).
Axes of the slice: x: 2, y: 2, z: 4, core: 2. Of those that a mesh axis runs over, the one named last changes fastest.
Arguments:
- fields: bfloat16 [3, 16, 2048, 276], P(None, ('dp', 'fsdp'), 'seq'), may hold values from -6 to 6
- targets: bfloat16 [3, 16, 2048, 276], P(None, ('dp', 'fsdp'), 'seq'), may hold values from -6 to 6
- interval: int32 [3, 16], replicated, may hold values from 0 to 2
- storm_index: int32 [3, 16], replicated, may hold values from 0 to 3
- valid_count: int32 [3, 16], replicated, may hold values from 1024 to 2048, as said below
- latitude: float32 [2048], replicated, may hold values from 0.5 to 5
- storm_scale: float32 [4], replicated, may hold values from 1 to 4
- embedding: float32 [276, 1024], P(None, ('dp', 'seq', 'fsdp')), may hold values from -0.375 to 0.375
- intervals: float32 [3, 1024], P(None, ('dp', 'seq', 'fsdp')), may hold values from -6 to 6
- modulator: float32 [1024, 6144], P(('dp', 'seq', 'fsdp')), may hold values from -0.1875 to 0.1875
- projector: float32 [1024, 3072], P(('dp', 'seq', 'fsdp')), may hold values from -0.1875 to 0.1875
- combiner: float32 [1024, 1024], P(('dp', 'seq', 'fsdp')), may hold values from -1 to 1
- feedforward: float32 [2, 1024, 4096], P(None, ('dp', 'seq', 'fsdp')), may hold values from -0.125 to 0.125
- readout: float32 [1024, 276], P(('dp', 'seq', 'fsdp')), may hold values from -0.1875 to 0.1875
- vectors: float32 [7, 1024], P(None, ('dp', 'seq', 'fsdp')), may hold values from 0.1 to 1.9
- first_embedding: float32 [276, 1024], P(None, ('dp', 'seq', 'fsdp')), may hold values from -1.9073486e-06 to 1.9073486e-06
- first_intervals: float32 [3, 1024], P(None, ('dp', 'seq', 'fsdp')), may hold values from -1.9073486e-06 to 1.9073486e-06
- first_modulator: float32 [1024, 6144], P(('dp', 'seq', 'fsdp')), may hold values from -1.9073486e-06 to 1.9073486e-06
- first_projector: float32 [1024, 3072], P(('dp', 'seq', 'fsdp')), may hold values from -1.9073486e-06 to 1.9073486e-06
- first_combiner: float32 [1024, 1024], P(('dp', 'seq', 'fsdp')), may hold values from -1.9073486e-06 to 1.9073486e-06
- first_feedforward: float32 [2, 1024, 4096], P(None, ('dp', 'seq', 'fsdp')), may hold values from -1.9073486e-06 to 1.9073486e-06
- first_readout: float32 [1024, 276], P(('dp', 'seq', 'fsdp')), may hold values from -1.9073486e-06 to 1.9073486e-06
- first_vectors: float32 [7, 1024], P(None, ('dp', 'seq', 'fsdp')), may hold values from -1.9073486e-06 to 1.9073486e-06
- second_embedding: float32 [276, 1024], P(None, ('dp', 'seq', 'fsdp')), may hold values from 1.2853565e-15 to 5.141426e-15
- second_intervals: float32 [3, 1024], P(None, ('dp', 'seq', 'fsdp')), may hold values from 1.2853565e-15 to 5.141426e-15
- second_modulator: float32 [1024, 6144], P(('dp', 'seq', 'fsdp')), may hold values from 1.2853565e-15 to 5.141426e-15
- second_projector: float32 [1024, 3072], P(('dp', 'seq', 'fsdp')), may hold values from 1.2853565e-15 to 5.141426e-15
- second_combiner: float32 [1024, 1024], P(('dp', 'seq', 'fsdp')), may hold values from 1.2853565e-15 to 5.141426e-15
- second_feedforward: float32 [2, 1024, 4096], P(None, ('dp', 'seq', 'fsdp')), may hold values from 1.2853565e-15 to 5.141426e-15
- second_readout: float32 [1024, 276], P(('dp', 'seq', 'fsdp')), may hold values from 1.2853565e-15 to 5.141426e-15
- second_vectors: float32 [7, 1024], P(None, ('dp', 'seq', 'fsdp')), may hold values from 1.2853565e-15 to 5.141426e-15
Outputs:
- updated_embedding: float32 [276, 1024], P(None, ('dp', 'seq', 'fsdp'))
- updated_intervals: float32 [3, 1024], P(None, ('dp', 'seq', 'fsdp'))
- updated_modulator: float32 [1024, 6144], P(('dp', 'seq', 'fsdp'))
- updated_projector: float32 [1024, 3072], P(('dp', 'seq', 'fsdp'))
- updated_combiner: float32 [1024, 1024], P(('dp', 'seq', 'fsdp'))
- updated_feedforward: float32 [2, 1024, 4096], P(None, ('dp', 'seq', 'fsdp'))
- updated_readout: float32 [1024, 276], P(('dp', 'seq', 'fsdp'))
- updated_vectors: float32 [7, 1024], P(None, ('dp', 'seq', 'fsdp'))
- momentum_embedding: float32 [276, 1024], P(None, ('dp', 'seq', 'fsdp'))
- momentum_intervals: float32 [3, 1024], P(None, ('dp', 'seq', 'fsdp'))
- momentum_modulator: float32 [1024, 6144], P(('dp', 'seq', 'fsdp'))
- momentum_projector: float32 [1024, 3072], P(('dp', 'seq', 'fsdp'))
- momentum_combiner: float32 [1024, 1024], P(('dp', 'seq', 'fsdp'))
- momentum_feedforward: float32 [2, 1024, 4096], P(None, ('dp', 'seq', 'fsdp'))
- momentum_readout: float32 [1024, 276], P(('dp', 'seq', 'fsdp'))
- momentum_vectors: float32 [7, 1024], P(None, ('dp', 'seq', 'fsdp'))
- variance_embedding: float32 [276, 1024], P(None, ('dp', 'seq', 'fsdp'))
- variance_intervals: float32 [3, 1024], P(None, ('dp', 'seq', 'fsdp'))
- variance_modulator: float32 [1024, 6144], P(('dp', 'seq', 'fsdp'))
- variance_projector: float32 [1024, 3072], P(('dp', 'seq', 'fsdp'))
- variance_combiner: float32 [1024, 1024], P(('dp', 'seq', 'fsdp'))
- variance_feedforward: float32 [2, 1024, 4096], P(None, ('dp', 'seq', 'fsdp'))
- variance_readout: float32 [1024, 276], P(('dp', 'seq', 'fsdp'))
- variance_vectors: float32 [7, 1024], P(None, ('dp', 'seq', 'fsdp'))
- loss_total: float32 [], replicated
- loss_weight: float32 [], replicated
- gradient_norm: float32 [], replicated
Inputs may be any that keep to these rules, and one draw needn't show every extreme that they name: `valid_count`: in every interval some sample counts all 2048 patches.
All inputs are finite; a program needn't handle non-finite values.
Results may differ from a plain program's by a relative error of at most 0.013.
Values may be sent and summed in bfloat16 or wider, within the bound.
A program may use at most 1.1875 GiB of HBM per device.

v0:
```python
import functools

import jax
import jax.numpy as jnp
from jax import lax
from jax.experimental import pallas as pl
from jax.experimental.pallas import tpu as pltpu
from jax.sharding import PartitionSpec as P

D = 1024
HD = 64
PIN = 276
WIDE = 384
DTK = 3
STEP = 10
PATCHES = 2048
ALL = ("dp", "seq", "fsdp")

beta_one = 0.9
beta_two = 0.999
decay = 0.01
epsilon = 1e-08
clip_norm = 0.005
norm_eps = 1e-06
bf16 = jnp.bfloat16
f32 = jnp.float32
LN2 = 0.6931471805599453
QUERY_SCALE = 0.125 / LN2
VMEM_BYTES = 60 * 2**20
ERF = (
    0.7978822138768258,
    0.03634467259297056,
    -4.4877727054425946e-05,
    -5.036405881894902e-05,
    3.0986869577148946e-06,
    -6.638614747540505e-08,
)
ERF_END = 21.16


def step_rates():
    factor = 1.5
    return (
        factor / PIN**0.5,
        factor,
        factor / D**0.5,
        factor / D**0.5,
        factor / max(64 * D // PATCHES, 16) ** 0.5,
        factor / (2 * D) ** 0.5,
        factor / D**0.5,
        factor,
    )


def contract(left, right, left_dim, right_dim):
    return lax.dot_general(
        left, right, (((left_dim,), (right_dim,)), ((), ())), preferred_element_type=f32
    )


def layer_norm(values):
    center = values - jnp.mean(values, -1, keepdims=True)
    inverse = lax.rsqrt(jnp.mean(center * center, -1, keepdims=True) + norm_eps)
    return (center * inverse, inverse)


def norm_back(upstream, normed, inverse):
    return inverse * (
        upstream
        - jnp.mean(upstream, -1, keepdims=True)
        - normed * jnp.mean(upstream * normed, -1, keepdims=True)
    )


def column_sum(values):
    return jnp.sum(values, 0, keepdims=True)


def gelu_pair(inner):
    square = inner * inner
    bounded = jnp.minimum(square, ERF_END)
    series = jnp.full_like(inner, ERF[-1])
    for coefficient in ERF[-2::-1]:
        series = series * bounded + coefficient
    normal = 0.5 + 0.5 * jnp.tanh(inner * series)
    density = jnp.exp2(square * (-0.5 / LN2)) * 0.3989422804014327
    return (inner * normal, normal + inner * density)


def resident(shape):
    return pl.BlockSpec(shape, lambda *place: (0,) * len(shape), pipeline_mode=pl.Buffered(1))


def entry_kernel(query_blocks, field, embed, weight, mod, stream, hidden, mixed):
    width = embed.shape[0]
    stream_zero = contract(field[...], embed[...], 1, 1)
    stream[...] = stream_zero
    normed, unused = layer_norm(stream_zero)
    low = (normed * (1.0 + mod[1:2, :]) + mod[0:1, :]).astype(bf16)
    hidden[...] = low
    for part in (1, 2):
        columns = pl.ds(part * width, width)
        mixed[:, columns] = contract(low, weight[:, columns], 1, 0).astype(bf16)

    @pl.when(pl.program_id(0) < query_blocks)
    def _():
        queries = contract(low, weight[:, 0:width], 1, 0)
        mixed[:, 0:width] = (queries * QUERY_SCALE).astype(bf16)


def entry(fields, embed, weight, mod, block, query_rows, unit_of):
    rows, pieces = fields.shape
    width = embed.shape[0]
    by_row = lambda columns: pl.BlockSpec((block, columns), lambda i: (i, 0))
    return pl.pallas_call(
        functools.partial(entry_kernel, query_rows // block),
        grid=(rows // block,),
        in_specs=[
            by_row(pieces),
            resident(embed.shape),
            resident(weight.shape),
            pl.BlockSpec((None,) + mod.shape[1:], lambda i: (unit_of(i), 0, 0)),
        ],
        out_specs=[by_row(width), by_row(width), by_row(3 * width)],
        out_shape=[
            jax.ShapeDtypeStruct((rows, width), f32),
            jax.ShapeDtypeStruct((rows, width), bf16),
            jax.ShapeDtypeStruct((rows, 3 * width), bf16),
        ],
        compiler_params=pltpu.CompilerParams(vmem_limit_bytes=VMEM_BYTES),
        name="entry",
    )(fields, embed, weight, mod)


def attend_kernel(sub, query, key, value, out, kept, inverse, value_t, key_one, stats):
    block, keys = query.shape[0], key.shape[0]
    zero, one = jnp.zeros((), bf16), jnp.ones((), bf16)

    @pl.when(pl.program_id(1) == 0)
    def _():
        turned = jnp.transpose(value[...])
        first_rows = lax.broadcasted_iota(jnp.int32, (2 * HD, keys), 0) < HD
        value_t[0] = jnp.where(first_rows, turned, one)
        value_t[1] = jnp.where(first_rows, one, turned)
        first_lanes = lax.broadcasted_iota(jnp.int32, (keys, 2 * HD), 1) < HD
        both = key[...]
        key_one[0] = jnp.where(first_lanes, both, one)
        key_one[1] = jnp.where(first_lanes, one, both)
        wide = both.astype(f32)
        mean = jnp.mean(wide, 0, keepdims=True)
        spread = (wide - mean) * (wide - mean)
        stats[0:1] = mean
        for head in range(2):
            mine = first_lanes if head == 0 else jnp.logical_not(first_lanes)
            size = jnp.sum(jnp.where(mine, spread, 0.0), 1, keepdims=True)
            far = jnp.max(size, 0, keepdims=True)
            stats[1 + head : 2 + head] = jnp.broadcast_to(0.5 * jnp.sqrt(far), (1, 2 * HD))

    lanes = lax.broadcasted_iota(jnp.int32, (block, 2 * HD), 1)
    wide = query[...].astype(f32)
    level = wide * stats[0:1]
    shifts, reaches = [], []
    for head in range(2):
        mine = (lanes < HD) if head == 0 else (lanes >= HD)
        length = jnp.sqrt(jnp.sum(jnp.where(mine, wide * wide, 0.0), 1, keepdims=True))
        reach = length * stats[1 + head : 2 + head, 0:1]
        shifts.append(jnp.sum(jnp.where(mine, level, 0.0), 1, keepdims=True) + reach)
        reaches.append(jnp.max(reach))
    near = jnp.maximum(reaches[0], reaches[1]) <= 60.0
    upper = lax.broadcasted_iota(jnp.int32, (2 * HD, sub), 0) < HD

    def run(exact):
        for part in range(block // sub):
            rows = pl.ds(part * sub, sub)
            results = []
            for head in range(2):
                spot = lanes[0:sub]
                mine = (spot < HD) if head == 0 else (spot >= HD)
                if exact:
                    moved = jnp.where(mine, query[rows, :], zero)
                    scores = contract(key_one[head], moved, 1, 1)
                    scores = scores - jnp.max(scores, 0, keepdims=True)
                else:
                    shift = (-shifts[head][part * sub : part * sub + sub]).astype(bf16)
                    free = HD if head == 0 else 0
                    rest = jnp.where(spot == free, shift, zero)
                    moved = jnp.where(mine, query[rows, :], rest)
                    scores = contract(key_one[head], moved, 1, 1)
                weights = jnp.exp2(scores).astype(bf16)
                kept[head, :, rows] = weights
                results.append(contract(value_t[head], weights, 1, 0))
            total = jnp.where(
                upper, pltpu.roll(results[0], HD, 0), pltpu.roll(results[1], HD, 0)
            )
            above = 1.0 / total
            mean = jnp.where(upper, results[0], results[1]) * above
            out[rows, :] = jnp.transpose(mean).astype(bf16)
            inverse[0:1, rows] = above[0:1]
            inverse[1:2, rows] = above[HD : HD + 1]

    @pl.when(near)
    def _():
        run(False)

    @pl.when(jnp.logical_not(near))
    def _():
        run(True)


def attend(queries, memory, places, block, sub, count, keys, width):
    pairs = width // (2 * HD)
    query_at, key_at, key_column, value_column = places
    return pl.pallas_call(
        functools.partial(attend_kernel, sub),
        grid=(pairs, count // block),
        in_specs=[
            pl.BlockSpec((block, 2 * HD), lambda h, i: (query_at // block + i, h)),
            pl.BlockSpec((keys, 2 * HD), lambda h, i: (key_at // keys, key_column * pairs + h)),
            pl.BlockSpec((keys, 2 * HD), lambda h, i: (key_at // keys, value_column * pairs + h)),
        ],
        out_specs=[
            pl.BlockSpec((block, 2 * HD), lambda h, i: (i, h)),
            pl.BlockSpec((None, None, 2, keys, block), lambda h, i: (h, i, 0, 0, 0)),
            pl.BlockSpec((None, 2, block), lambda h, i: (h, 0, i)),
        ],
        out_shape=[
            jax.ShapeDtypeStruct((count, width), bf16),
            jax.ShapeDtypeStruct((pairs, count // block, 2, keys, block), bf16),
            jax.ShapeDtypeStruct((pairs, 2, count), f32),
        ],
        scratch_shapes=[
            pltpu.VMEM((2, 2 * HD, keys), bf16),
            pltpu.VMEM((2, keys, 2 * HD), bf16),
            pltpu.VMEM((8, 2 * HD), f32),
        ],
        compiler_params=pltpu.CompilerParams(vmem_limit_bytes=VMEM_BYTES),
        name="attend",
    )(queries, memory, memory)


def attend_back_kernel(
    sub, query, key, value, grad, out, kept, inverse,
    grad_query, grad_key, grad_value, key_t, value_one, key_sum, value_sum,
):
    block, keys = query.shape[0], key.shape[0]
    step, steps = pl.program_id(1), pl.num_programs(1)
    zero = jnp.zeros((), bf16)

    @pl.when(step == 0)
    def _():
        first_rows = lax.broadcasted_iota(jnp.int32, (2 * HD, keys), 0) < HD
        turned = jnp.transpose(key[...])
        key_t[0] = jnp.where(first_rows, turned, zero)
        key_t[1] = jnp.where(first_rows, zero, turned)
        first_lanes = lax.broadcasted_iota(jnp.int32, (keys, 2 * HD), 1) < HD
        minus = jnp.full((), -1.0, bf16)
        value_one[0] = jnp.where(first_lanes, value[...], minus)
        value_one[1] = jnp.where(first_lanes, minus, value[...])
        key_sum[...] = jnp.zeros_like(key_sum)
        value_sum[...] = jnp.zeros_like(value_sum)

    lanes = lax.broadcasted_iota(jnp.int32, (sub, 2 * HD), 1)
    places = lax.broadcasted_iota(jnp.int32, (2 * HD, sub), 0)
    upper = places < HD
    for part in range(block // sub):
        rows = pl.ds(part * sub, sub)
        above = jnp.where(upper, inverse[0:1, rows], inverse[1:2, rows])
        scaled = (jnp.transpose(grad[rows, :].astype(f32)) * above).astype(bf16)
        product = scaled.astype(f32) * jnp.transpose(out[rows, :].astype(f32))
        natural = jnp.transpose(scaled)
        queries = query[rows, :]
        turned = None
        for head in range(2):
            delta = jnp.sum(product[HD * head : HD * head + HD], 0, keepdims=True)
            high = delta.astype(bf16)
            rest = (delta - high.astype(f32)).astype(bf16)
            free = HD if head == 0 else 0
            mine = upper if head == 0 else jnp.logical_not(upper)
            extra = jnp.where(places == free, high, jnp.where(places == free + 1, rest, zero))
            grad_probs = contract(value_one[head], jnp.where(mine, scaled, extra), 1, 0)
            weights = kept[head, :, rows]
            grad_scores = grad_probs.astype(bf16) * weights
            own = (lanes < HD) if head == 0 else (lanes >= HD)
            value_sum[...] += contract(weights, jnp.where(own, natural, zero), 1, 0)
            key_sum[...] += contract(grad_scores, jnp.where(own, queries, zero), 1, 0)
            term = contract(key_t[head], grad_scores, 1, 0)
            turned = term if turned is None else turned + term
        grad_query[rows, :] = (jnp.transpose(turned) * 0.125).astype(bf16)

    @pl.when(step == steps - 1)
    def _():
        grad_key[...] = (key_sum[...] * LN2).astype(bf16)
        grad_value[...] = value_sum[...].astype(bf16)


def attend_back(queries, memory, grads, out, kept, inverse, places, block, sub, count, keys, width):
    pairs = width // (2 * HD)
    query_at, key_at, key_column, value_column = places
    return pl.pallas_call(
        functools.partial(attend_back_kernel, sub),
        grid=(pairs, count // block),
        in_specs=[
            pl.BlockSpec((block, 2 * HD), lambda h, i: (query_at // block + i, h)),
            pl.BlockSpec((keys, 2 * HD), lambda h, i: (key_at // keys, key_column * pairs + h)),
            pl.BlockSpec((keys, 2 * HD), lambda h, i: (key_at // keys, value_column * pairs + h)),
            pl.BlockSpec((block, 2 * HD), lambda h, i: (query_at // block + i, h)),
            pl.BlockSpec((block, 2 * HD), lambda h, i: (i, h)),
            pl.BlockSpec((None, None, 2, keys, block), lambda h, i: (h, i, 0, 0, 0)),
            pl.BlockSpec((None, 2, block), lambda h, i: (h, 0, i)),
        ],
        out_specs=[
            pl.BlockSpec((block, 2 * HD), lambda h, i: (i, h)),
            pl.BlockSpec((keys, 2 * HD), lambda h, i: (0, h)),
            pl.BlockSpec((keys, 2 * HD), lambda h, i: (0, h)),
        ],
        out_shape=[
            jax.ShapeDtypeStruct((count, width), bf16),
            jax.ShapeDtypeStruct((keys, width), bf16),
            jax.ShapeDtypeStruct((keys, width), bf16),
        ],
        scratch_shapes=[
            pltpu.VMEM((2, 2 * HD, keys), bf16),
            pltpu.VMEM((2, keys, 2 * HD), bf16),
            pltpu.VMEM((keys, 2 * HD), f32),
            pltpu.VMEM((keys, 2 * HD), f32),
        ],
        compiler_params=pltpu.CompilerParams(vmem_limit_bytes=VMEM_BYTES),
        name="attend_back",
    )(queries, memory, memory, grads, out, kept, inverse)


def middle_kernel(
    attended, stream, target, weight_rows, mod, combine, first, second, read,
    hidden, active, grad_two, grad_inner, final, grad_read, grad_one, grad_attended, grad_stream,
    sums, losses, slopes,
):
    width, spread = first.shape
    tiles = [pl.ds(start, width) for start in range(0, spread, width)]
    gate_a, shift_b, scale_b = mod[2:3, :], mod[3:4, :], mod[4:5, :]
    gate_b, gain = mod[5:6, :], mod[6:7, :]
    branch_a = contract(attended[...], combine[...], 1, 0)
    stream_one = stream[...] + gate_a * branch_a
    norm_b, inverse_b = layer_norm(stream_one)
    low = (norm_b * (1.0 + scale_b) + shift_b).astype(bf16)
    hidden[...] = low
    branch_b = None
    for tile in tiles:
        value, slope = gelu_pair(contract(low, first[:, tile], 1, 0))
        value = value.astype(bf16)
        active[:, tile] = value
        slopes[:, tile] = slope.astype(bf16)
        term = contract(value, second[:, tile], 1, 1)
        branch_b = term if branch_b is None else branch_b + term
    norm_c, inverse_c = layer_norm(stream_one + gate_b * branch_b)
    last = (norm_c * gain).astype(bf16)
    final[...] = last
    diff = contract(last, read[...], 1, 0) - target[...].astype(f32)
    losses[...] = jnp.broadcast_to(column_sum(weight_rows[:, 0:1] * diff * diff), losses.shape)
    grad_low = (weight_rows[:, 1:2] * diff).astype(bf16)
    grad_read[...] = grad_low
    grad_final = contract(grad_low, read[...], 1, 1)
    sums[6:7, :] = column_sum(grad_final * norm_c)
    grad = norm_back(grad_final * gain, norm_c, inverse_c)
    sums[5:6, :] = column_sum(grad * branch_b)
    back = (grad * gate_b).astype(bf16)
    grad_two[...] = back
    grad_hidden = None
    for tile in tiles:
        inner = contract(back, second[:, tile], 1, 0)
        inner = (inner * slopes[:, tile].astype(f32)).astype(bf16)
        grad_inner[:, tile] = inner
        term = contract(inner, first[:, tile], 1, 1)
        grad_hidden = term if grad_hidden is None else grad_hidden + term
    sums[3:4, :] = column_sum(grad_hidden)
    sums[4:5, :] = column_sum(grad_hidden * norm_b)
    grad = grad + norm_back(grad_hidden * (1.0 + scale_b), norm_b, inverse_b)
    grad_stream[...] = grad
    sums[2:3, :] = column_sum(grad * branch_a)
    back = (grad * gate_a).astype(bf16)
    grad_one[...] = back
    grad_attended[...] = contract(back, combine[...], 1, 1).astype(bf16)
    sums[0:2, :] = jnp.zeros((2, width), f32)
    sums[7:8, :] = jnp.zeros((1, width), f32)


def middle(attended, stream, target, weight_rows, mod, combine, first, second, read, block, unit_of):
    rows, width = attended.shape
    spread, pieces = first.shape[1], read.shape[1]
    blocks = rows // block
    by_row = lambda columns: pl.BlockSpec((block, columns), lambda i: (i, 0))
    shape = lambda columns, kind: jax.ShapeDtypeStruct((rows, columns), kind)
    outs = (
        (width, bf16), (spread, bf16), (width, bf16), (spread, bf16), (width, bf16), (pieces, bf16),
        (width, bf16), (width, bf16), (width, f32),
    )
    return pl.pallas_call(
        middle_kernel,
        grid=(blocks,),
        in_specs=[
            by_row(width),
            by_row(width),
            by_row(pieces),
            by_row(2),
            pl.BlockSpec((None,) + mod.shape[1:], lambda i: (unit_of(i), 0, 0)),
            resident(combine.shape),
            resident(first.shape),
            resident(second.shape),
            resident(read.shape),
        ],
        out_specs=[by_row(columns) for columns, kind in outs]
        + [
            pl.BlockSpec((None, 8, width), lambda i: (i, 0, 0)),
            pl.BlockSpec((None, 8, pieces), lambda i: (i, 0, 0)),
        ],
        out_shape=[shape(columns, kind) for columns, kind in outs]
        + [
            jax.ShapeDtypeStruct((blocks, 8, width), f32),
            jax.ShapeDtypeStruct((blocks, 8, pieces), f32),
        ],
        scratch_shapes=[pltpu.VMEM((block, spread), bf16)],
        compiler_params=pltpu.CompilerParams(vmem_limit_bytes=VMEM_BYTES),
        name="middle",
    )(attended, stream, target, weight_rows, mod, combine, first, second, read)


def leave_kernel(query_blocks, grad_query, grad_memory, stream, grad_stream, weight, mod, out, sums, held):
    width = stream.shape[1]
    asks = pl.program_id(0) < query_blocks
    grad_hidden = contract(grad_memory[...], weight[:, width:], 1, 1)
    held[...] = grad_hidden

    @pl.when(asks)
    def _():
        held[...] += contract(grad_query[...], weight[:, 0:width], 1, 1)

    normed, inverse = layer_norm(stream[...])
    grad_hidden = held[...]
    sums[0:1, :] = column_sum(grad_hidden)
    sums[1:2, :] = column_sum(grad_hidden * normed)
    sums[2:8, :] = jnp.zeros((6, width), f32)
    grad = norm_back(grad_hidden * (1.0 + mod[1:2, :]), normed, inverse)
    grad = grad + jnp.where(asks, grad_stream[...], 0.0)
    out[...] = grad.astype(bf16)


def leave(grad_query, grad_memory, stream, grad_stream, weight, mod, block, unit_of):
    rows, width = stream.shape
    asking = grad_query.shape[0] // block
    blocks = rows // block
    by_row = lambda columns: pl.BlockSpec((block, columns), lambda i: (i, 0))
    asked = pl.BlockSpec((block, width), lambda i: (jnp.minimum(i, asking - 1), 0))
    return pl.pallas_call(
        functools.partial(leave_kernel, asking),
        grid=(blocks,),
        in_specs=[
            asked,
            by_row(2 * width),
            by_row(width),
            asked,
            resident(weight.shape),
            pl.BlockSpec((None,) + mod.shape[1:], lambda i: (unit_of(i), 0, 0)),
        ],
        out_specs=[by_row(width), pl.BlockSpec((None, 8, width), lambda i: (i, 0, 0))],
        out_shape=[
            jax.ShapeDtypeStruct((rows, width), bf16),
            jax.ShapeDtypeStruct((blocks, 8, width), f32),
        ],
        scratch_shapes=[pltpu.VMEM((block, width), f32)],
        compiler_params=pltpu.CompilerParams(vmem_limit_bytes=VMEM_BYTES),
        name="leave",
    )(grad_query, grad_memory, stream, grad_stream, weight, mod)


def adam(master, first, second, grad, factor, step_rate):
    grad = grad * factor
    first_new = beta_one * first + (1.0 - beta_one) * grad
    second_new = beta_two * second + (1.0 - beta_two) * grad * grad
    corrected = (
        first_new
        / (1.0 - beta_one**STEP)
        / (jnp.sqrt(second_new / (1.0 - beta_two**STEP)) + epsilon)
    )
    return (master - step_rate * (corrected + decay * master), first_new, second_new)


def largest(limit, *sizes):
    block = limit
    while any(size % block for size in sizes):
        block //= 2
    return block


def body(ways, *args):
    fields, targets, interval, storm_index, valid_count, latitude, storm_scale = args[:7]
    masters, firsts, seconds = args[7:15], args[15:23], args[23:31]
    embedding, intervals, modulator, projector, combiner, feedforward, readout, vectors = masters
    micros, samples_dev, part, pieces = fields.shape
    patches = latitude.shape[0]
    units = micros * samples_dev
    share, width = projector.shape[0], projector.shape[1] // 3
    place = lax.axis_index("seq")
    device = lax.axis_index(ALL)
    sample_start = lax.axis_index(("dp", "fsdp")) * samples_dev
    ring = [(index, 1 - index) for index in range(2)]
    alone = units // 2 if ways == 2 else 0
    shared = units - ways * alone
    have = alone + shared

    everywhere = jnp.arange(patches, dtype=jnp.int32)
    mask = (everywhere[None, None, :] >= patches - valid_count[:, :, None]).astype(f32)
    levels = jnp.arange(storm_scale.shape[0], dtype=jnp.int32)
    storms = jnp.sum(jnp.where(storm_index[:, :, None] == levels, storm_scale, 0.0), -1)
    row_weights = latitude[None, None, :] * storms[:, :, None] * mask
    total_weight = pieces * jnp.sum(row_weights)

    def local(values):
        cut = lax.dynamic_slice_in_dim(values, sample_start, samples_dev, 1)
        cut = cut.reshape((units,) + values.shape[2:])
        mine = [lax.dynamic_slice_in_dim(cut, place * alone, alone, 0)] if alone else []
        return jnp.concatenate(mine + [cut[ways * alone :]], 0)

    kinds = local(interval)
    weights_unit = jnp.roll(local(row_weights), -place * part, 1)
    weights_rows = jnp.concatenate(
        [weights_unit[:alone].reshape(-1), weights_unit[alone:, :part].reshape(-1)]
    )
    weight_rows = jnp.stack([weights_rows, weights_rows * (2.0 / total_weight)], 1)

    def widen(values):
        flat = values.reshape(units, part, pieces)
        return jnp.pad(flat, ((0, 0), (0, 0), (0, WIDE - pieces)))

    own, goal = widen(fields), widen(targets)
    if alone:
        away = (1 - place) * alone
        cut = lambda values, start: lax.dynamic_slice_in_dim(values, start, alone, 0)
        sent = jnp.concatenate([cut(own, away), own[2 * alone :]], 0)
        came = lax.ppermute(sent, "seq", ring)
        goal_came = lax.ppermute(cut(goal, away), "seq", ring)
        whole = jnp.concatenate([cut(own, place * alone), came[:alone]], 1)
        goal_whole = jnp.concatenate([cut(goal, place * alone), goal_came], 1)
        rows = [whole, own[2 * alone :], came[alone:]]
        goals = [goal_whole, goal[2 * alone :]]
    elif ways == 1:
        rows, goals = [own], [goal]
    else:
        everyone = lax.all_gather(own, "seq", axis=1, tiled=True)
        rows = [own, jnp.roll(everyone, -place * part, 1)[:, part:]]
        goals = [goal]
    flatten = lambda parts: jnp.concatenate([piece.reshape(-1, WIDE) for piece in parts], 0)
    all_rows, goal_rows = flatten(rows), flatten(goals)
    asking = (alone * ways + shared) * part

    def unit_of(block):
        whole_blocks = alone * patches // block
        own_blocks = shared * part // block
        other = max((patches - part) // block, 1)

        def at(i):
            late = alone + (i - whole_blocks) // (part // block)
            later = alone + (i - whole_blocks - own_blocks) // other
            late = jnp.where(i < whole_blocks + own_blocks, late, later)
            return jnp.where(i < whole_blocks, i // (patches // block), late)

        return at

    low = [master.astype(bf16) for master in masters]
    step_vec = low[1].astype(f32)
    active = jax.nn.silu(step_vec)
    active_low = active.astype(bf16)
    table = contract(active_low, low[2], 1, 0)
    spread_vectors = lax.dynamic_update_slice(
        jnp.zeros((7, width), f32), low[7].astype(f32), (0, device * share)
    )
    carried = lax.psum(jnp.concatenate([table.reshape(-1), spread_vectors.reshape(-1)]), ALL)
    table = carried[: table.size].reshape(DTK, 6, width)
    all_vectors = carried[table.size :].reshape(7, width)
    table = table + all_vectors[None, :6]
    chosen = sum(jnp.where(kinds[:, None, None] == kind, table[kind], 0.0) for kind in range(DTK))
    gain = jnp.broadcast_to(all_vectors[6], (have, 1, width))
    mod = jnp.concatenate([chosen, gain, jnp.zeros((have, 1, width), f32)], 1)

    gather = lambda values: lax.all_gather(values, ALL, axis=0, tiled=True)
    wide_readout = jnp.pad(low[6], ((0, 0), (0, WIDE - pieces)))
    embed = gather(jnp.pad(low[0].T, ((0, 0), (0, WIDE - pieces))))
    project = gather(low[3])
    combine = gather(low[4])
    first = gather(low[5][0])
    second = gather(low[5][1])
    read = gather(wide_readout)

    block = largest(512, part)
    stream, hidden_a, mixed = entry(all_rows, embed, project, mod, block, asking, unit_of(block))

    calls = []
    for unit in range(have):
        if unit < alone:
            calls.append((unit * patches, patches, mixed, unit * patches, 1, 2))
        else:
            start = alone * patches + (unit - alone) * part
            behind = asking + (unit - alone) * (patches - part)
            if shared == 1 and start % patches == 0:
                calls.append((start, part, mixed, start, 1, 2))
            else:
                pieces_of = [mixed[start : start + part, width:]]
                pieces_of.append(mixed[behind : behind + patches - part, width:])
                calls.append((start, part, jnp.concatenate(pieces_of, 0), 0, 0, 1))
    attended, saved = [], []
    for start, count, memory, key_at, key_column, value_column in calls:
        block = largest(2048, count, start if start else count)
        where = (start, key_at, key_column, value_column)
        sub = min(block, 1024)
        out, kept, inverse = attend(mixed, memory, where, block, sub, count, patches, width)
        attended.append(out)
        saved.append((out, kept, inverse, where, block))
    attended_rows = jnp.concatenate(attended, 0)

    block = largest(256, part)
    (
        hidden_b, activated, grad_two, grad_inner, final, grad_read, grad_one, grad_attended,
        grad_stream, sums, losses,
    ) = middle(
        attended_rows, stream[:asking], goal_rows, weight_rows, mod, combine, first, second, read, block,
        unit_of(block),
    )
    units_mid = [unit_of(block)(jnp.int32(i)) for i in range(sums.shape[0])]
    loss_local = jnp.sum(losses[:, 0, :])

    scatter = lambda values: lax.psum_scatter(values, ALL, scatter_dimension=0, tiled=True)
    summed = lambda left, right: contract(left, right, 0, 0).astype(bf16)
    shard_first = scatter(summed(hidden_b, grad_inner)).astype(f32)
    shard_second = scatter(summed(grad_two, activated)).astype(f32)
    shard_combine = scatter(summed(attended_rows, grad_one)).astype(f32)
    shard_read = scatter(summed(final, grad_read)).astype(f32)

    grad_queries, grad_memories = [], []
    for (start, count, memory, unused_a, unused_b, unused_c), (out, kept, inverse, where, block) in zip(
        calls, saved
    ):
        grad_query, grad_key, grad_value = attend_back(
            mixed, memory, grad_attended, out, kept, inverse, where, block, min(block, 256), count,
            patches, width,
        )
        grad_queries.append(grad_query)
        grad_memories.append(jnp.concatenate([grad_key, grad_value], 1))
    grad_query_rows = jnp.concatenate(grad_queries, 0)
    grad_memory_rows = jnp.concatenate(
        grad_memories[:alone]
        + [values[:part] for values in grad_memories[alone:]]
        + [values[part:] for values in grad_memories[alone:]],
        0,
    )
    shard_project = scatter(
        jnp.concatenate(
            [
                summed(hidden_a[:asking], grad_query_rows),
                summed(hidden_a, grad_memory_rows),
            ],
            1,
        )
    ).astype(f32)
    block = largest(512, part)
    grad_zero, sums_a = leave(
        grad_query_rows, grad_memory_rows, stream, grad_stream, project, mod, block, unit_of(block)
    )
    units_out = [unit_of(block)(jnp.int32(i)) for i in range(sums_a.shape[0])]
    shard_embed = scatter(summed(grad_zero, all_rows)).astype(f32)

    by_block = jnp.concatenate([sums, sums_a], 0)
    kind_block = kinds[jnp.stack(units_mid + units_out)]
    grad_table = jnp.stack(
        [
            jnp.sum(jnp.where((kind_block == kind)[:, None, None], by_block, 0.0), 0)
            for kind in range(DTK)
        ]
    )
    carried = lax.psum(
        jnp.concatenate([grad_table[:, :7].reshape(-1), loss_local.reshape(1)]), ALL
    )
    loss_total = carried[-1]
    grad_table = carried[:-1].reshape(DTK, 7, width)
    grad_mod = grad_table[:, :6].reshape(DTK, 6 * width)
    shard_vectors = lax.dynamic_slice_in_dim(jnp.sum(grad_table, 0), device * share, share, 1)
    active_wide = active_low.astype(f32)
    shard_modulator = sum(
        active_wide[kind][:, None] * grad_mod[kind][None, :] for kind in range(DTK)
    )
    grad_active = jnp.stack(
        [jnp.sum(low[2].astype(f32) * grad_mod[kind][None, :], 1) for kind in range(DTK)]
    )
    unused, silu_back = jax.vjp(jax.nn.silu, step_vec)
    shard_intervals = silu_back(grad_active)[0]

    shards = (
        shard_embed[:, :pieces].T,
        shard_intervals,
        shard_modulator,
        shard_project,
        shard_combine,
        jnp.stack([shard_first, shard_second]),
        shard_read[:, :pieces],
        shard_vectors,
    )
    squares = lax.psum(sum(jnp.sum(grad * grad) for grad in shards), ALL)
    norm = jnp.sqrt(squares)
    factor = clip_norm / jnp.maximum(norm, clip_norm)
    results = [
        adam(master, first_moment, second_moment, grad, factor, rate)
        for master, first_moment, second_moment, grad, rate in zip(
            masters, firsts, seconds, shards, step_rates()
        )
    ]
    return tuple(result[index] for index in range(3) for result in results) + (
        loss_total,
        total_weight,
        norm,
    )


def solution(mesh):
    data = P(None, ("dp", "fsdp"), "seq", None)
    columns, rows = P(None, ALL), P(ALL, None)
    weights = (columns, columns, rows, rows, rows, P(None, ALL, None), rows, columns)
    return jax.shard_map(
        functools.partial(body, mesh.shape["seq"]),
        mesh=mesh,
        in_specs=(data, data) + (P(),) * 5 + weights * 3,
        out_specs=weights * 3 + (P(),) * 3,
        check_vma=False,
    )
```

profile of v0, /device:TPU:0, one launch (start us, length us, event | category | flops | bytes accessed | tf_op | source)
XLA Modules:
  0.0 1862.5 jit_solution(15008200917110328212)
XLA Ops:
  22.1 2.9 collective-permute-start
  35.6 77.2 %all_gather.18.embed = bf16[1024,384]{1,0:T(8,128)(2,1)} all-gather(bf16[32,384]{1,0:T(8,128)(2,1)S(1)} %pad.15), channel_id=1, replica_groups=mesh['dp'=4,'seq'=2,'fsdp'=4] {'dp','seq','fsdp'}, dimensions={0}, use_global_device_ids=true | all-gather | bytes 811008 | tf_op jit(solution)/shard_map/all_gather | solution.py:583
  112.8 42.8 %all_gather.23.read = bf16[1024,384]{1,0:T(8,128)(2,1)} all-gather(bf16[32,384]{1,0:T(8,128)(2,1)S(1)} %pad.17), channel_id=1, replica_groups=mesh['dp'=4,'seq'=2,'fsdp'=4] {'dp','seq','fsdp'}, dimensions={0}, use_global_device_ids=true | all-gather | bytes 811008 | tf_op jit(solution)/shard_map/all_gather | solution.py:583
  168.4 43.5 %all-gather.7.cloned.1.call-done.weight = bf16[1024,3072]{1,0:T(8,128)(2,1)} async-done(((bf16[32,3072]{1,0:T(8,128)(2,1)}), bf16[1024,3072]{1,0:T(8,128)(2,1)}) %all-gather.7.cloned.1.call-update) | async-done | bytes 6291472 | tf_op jit(solution)/shard_map/all_gather | solution.py:583
  211.9 40.7 %entry.1 = (f32[4096,1024]{1,0:T(8,128)}, bf16[4096,1024]{1,0:T(8,128)(2,1)}, bf16[4096,3072]{1,0:T(8,128)(2,1)}) custom-call(bf16[4096,384]{1,0:T(8,128)(2,1)} %pad_maximum_fusion.1.field, bf16[1024,384]{1,0:T(8,128)(2,1)} %all_gather.18.embed, bf16[1024,3072]{1,0:T(8,128)(2,1)} %all-gather.7.cloned.1.call-done.weight, f32[2,8,1024]{2,1,0:T(8,128)} %maximum_maximum_fusion.1.mod), custom_call_target="tpu_custom_call" | custom-call | tf_op jit(solution)/shard_map/entry/pallas_call | solution.py:115
  252.5 116.8 %attend.2 = (bf16[2048,1024]{1,0:T(8,128)(2,1)}, bf16[8,1,2,2048,2048]{4,3,2,1,0:T(8,128)(2,1)}, f32[8,2,2048]{2,1,0:T(2,128)}) custom-call(bf16[4096,3072]{1,0:T(8,128)(2,1)} %get-tuple-element.55.query.key.value, bf16[4096,3072]{1,0:T(8,128)(2,1)} %get-tuple-element.55.query.key.value, bf16[4096,3072]{1,0:T(8,128)(2,1)} %get-tuple-element.55.query.key.value), custom_call_target="tpu_custom_call" | custom-call | tf_op jit(solution)/shard_map/attend/pallas_call | solution.py:213
  369.3 56.0 %attend.3 = (bf16[1024,1024]{1,0:T(8,128)(2,1)}, bf16[8,1,2,2048,1024]{4,3,2,1,0:T(8,128)(2,1)}, f32[8,2,1024]{2,1,0:T(2,128)}) custom-call(bf16[4096,3072]{1,0:T(8,128)(2,1)} %get-tuple-element.55.query.key.value, bf16[4096,3072]{1,0:T(8,128)(2,1)} %get-tuple-element.55.query.key.value, bf16[4096,3072]{1,0:T(8,128)(2,1)} %get-tuple-element.55.query.key.value), custom_call_target="tpu_custom_call" | custom-call | tf_op jit(solution)/shard_map/attend/pallas_call | solution.py:213
  425.4 12.4 slice.138.stream
  441.6 181.7 %middle.1 = (bf16[3072,1024]{1,0:T(8,128)(2,1)}, bf16[3072,4096]{1,0:T(8,128)(2,1)}, bf16[3072,1024]{1,0:T(8,128)(2,1)}, bf16[3072,4096]{1,0:T(8,128)(2,1)}, bf1...) custom-call(bf16[3072,1024]{1,0:T(8,128)(2,1)} %constant_dynamic-upd, ...), custom_call_target="tpu_custom_call" | custom-call | tf_op jit(solution)/shard_map/middle/pallas_call | solution.py:396
  623.4 134.1 %attend_back.2 = (bf16[2048,1024]{1,0:T(8,128)(2,1)}, bf16[2048,1024]{1,0:T(8,128)(2,1)}, bf16[2048,1024]{1,0:T(8,128)(2,1)}) custom-call(bf16[4096,3072]{1,0:T(8,128)(2,1)} %get-tuple-element.55.query.key.value, bf16[4096,3072]{1,0:T(8,128)(2,1)} %get-tuple-element.55.query.key.value, bf16[4096,3072]{1,0:T(8,128)(2,1)} %get-tuple-element.55.query.key.value, ...), custom_call_target="tpu_custom_call" | custom-call | tf_op jit(solution)/shard_map/attend_back/pallas_call | solution.py:299
  757.5 4.7 constant_dynamic-update-slice_fusion.3
  763.0 69.6 %attend_back.3 = (bf16[1024,1024]{1,0:T(8,128)(2,1)}, bf16[2048,1024]{1,0:T(8,128)(2,1)}, bf16[2048,1024]{1,0:T(8,128)(2,1)}) custom-call(bf16[4096,3072]{1,0:T(8,128)(2,1)} %get-tuple-element.55.query.key.value, bf16[4096,3072]{1,0:T(8,128)(2,1)} %get-tuple-element.55.query.key.value, bf16[4096,3072]{1,0:T(8,128)(2,1)} %get-tuple-element.55.query.key.value, ...), custom_call_target="tpu_custom_call" | custom-call | tf_op jit(solution)/shard_map/attend_back/pallas_call | solution.py:299
  832.6 3.3 constant_dynamic-update-slice_fusion.2.grad_query
  835.8 32.5 %maximum_maximum_fusion.grad_memory = bf16[4096,2048]{1,0:T(8,128)(2,1)} fusion(bf16[2048,1024]{1,0:T(8,128)(2,1)} %get-tuple-element.69, bf16[2048,1024]{1,0:T(8,128)(2,1)} %get-tuple-element.68, bf16[2048,1024]{1,0:T(8,128)(2,1)} %get-tuple-element.67, bf16[2048,1024]{1,0:T(8,128)(2,1)S(1)} %copy-done.6), kind=kLoop, calls=%fused_computation | loop fusion | flops 67108864 | bytes 33554432 | tf_op jit(solution)/shard_map/concatenate | solution.py:647
  868.4 46.2 %leave.1 = (bf16[4096,1024]{1,0:T(8,128)(2,1)}, f32[8,8,1024]{2,1,0:T(8,128)}) custom-call(bf16[3072,1024]{1,0:T(8,128)(2,1)} %constant_dynamic-update-slice_fusion.2.grad_query, bf16[4096,2048]{1,0:T(8,128)(2,1)} %maximum_maximum_fusion.grad_memory, f32[4096,1024]{1,0:T(8,128)} %get-tuple-element.58.stream, f32[3072,1024]{1,0:T(8,128)} %get-tuple-element.70.grad_stream, ...), custom_call_target="tpu_custom_call" | custom-call | tf_op jit(solution)/shard_map/leave/pallas_call | solution.py:452
  920.6 9.2 convolution_convert_fusion.5
  930.3 7.8 convolution_convert_fusion.4
  938.2 11.7 convolution_convert_fusion.3
  950.0 11.7 fusion.2
  961.6 2.9 copy.74
  964.5 28.0 %convolution_convert_fusion.2 = bf16[1024,2048]{1,0:T(8,128)(2,1)S(1)} fusion(bf16[4096,1024]{1,0:T(8,128)(2,1)} %get-tuple-element.75, bf16[2048,1024]{1,0:T(8,128)(2,1)} %get-tuple-element.69, bf16[2048,1024]{1,0:T(8,128)(2,1)} %get-tuple-element.68, bf16[2048,1024]{1,0:T(8,128)(2,1)} %get-tuple-element.67, bf16[2048,1024]{1,0:T(8,128)(2,1)} %get-tuple-element.66), kind=kOutput, calls=%fused_computation.6 | convolution fusion | flops 17249075200 | bytes 29360128 | tf_op jit(solution)/shard_map/dot_general | solution.py:56
  992.5 3.2 pad_maximum_fusion
  995.9 33.4 %convolution_convert_fusion.1 = bf16[1024,4096]{1,0:T(8,128)(2,1)} fusion(bf16[3072,1024]{1,0:T(8,128)(2,1)} %get-tuple-element.77, bf16[3072,4096]{1,0:T(8,128)(2,1)} %get-tuple-element.78), kind=kOutput, calls=%fused_computation.2 | convolution fusion | flops 25773998080 | bytes 39845888 | tf_op jit(solution)/shard_map/dot_general | solution.py:56
  1029.6 33.3 %convolution_convert_fusion = bf16[1024,4096]{1,0:T(8,128)(2,1)} fusion(bf16[3072,1024]{1,0:T(8,128)(2,1)} %get-tuple-element.79, bf16[3072,4096]{1,0:T(8,128)(2,1)} %get-tuple-element.80), kind=kOutput, calls=%fused_computation.1 | convolution fusion | flops 25773998080 | bytes 39845888 | tf_op jit(solution)/shard_map/dot_general | solution.py:56
  1067.3 79.7 %reduce-scatter.7.cloned.1.call-done = bf16[32,384]{1,0:T(8,128)(2,1)} async-done(((bf16[1024,384]{1,0:T(8,128)(2,1)}), bf16[32,384]{1,0:T(8,128)(2,1)}) %reduce-scatter.7.cloned.1.call-update) | async-done | bytes 24592 | tf_op jit(solution)/shard_map/reduce_scatter | solution.py:629
  1150.2 97.0 %reduce-scatter.17.cloned.1.call-done = bf16[32,384]{1,0:T(8,128)(2,1)} async-done(((bf16[1024,384]{1,0:T(8,128)(2,1)}), bf16[32,384]{1,0:T(8,128)(2,1)}) %reduce-scatter.17.cloned.1.call-update) | async-done | bytes 24592 | tf_op jit(solution)/shard_map/reduce_scatter | solution.py:629
  1248.7 136.6 %reduce-scatter.11.cloned.1.call-done = bf16[32,1024]{1,0:T(8,128)(2,1)} async-done(((bf16[1024,1024]{1,0:T(8,128)(2,1)}), bf16[32,1024]{1,0:T(8,128)(2,1)}) %reduce-scatter.11.cloned.1.call-update) | async-done | bytes 65552 | tf_op jit(solution)/shard_map/reduce_scatter | solution.py:629
  1386.7 115.5 %reduce-scatter.9.cloned.1.call-done = bf16[32,3072]{1,0:T(8,128)(2,1)} async-done(((bf16[1024,3072]{1,0:T(8,128)(2,1)}), bf16[32,3072]{1,0:T(8,128)(2,1)}) %reduce-scatter.9.cloned.1.call-update) | async-done | bytes 196624 | tf_op jit(solution)/shard_map/reduce_scatter | solution.py:629
  1505.2 147.4 %reduce-scatter.13.cloned.1.call-done = bf16[32,4096]{1,0:T(8,128)(2,1)} async-done(((bf16[1024,4096]{1,0:T(8,128)(2,1)}), bf16[32,4096]{1,0:T(8,128)(2,1)}) %reduce-scatter.13.cloned.1.call-update) | async-done | bytes 262160 | tf_op jit(solution)/shard_map/reduce_scatter | solution.py:629
  1652.6 146.8 %reduce-scatter.15.cloned.1.call-done = bf16[32,4096]{1,0:T(8,128)(2,1)} async-done(((bf16[1024,4096]{1,0:T(8,128)(2,1)}), bf16[32,4096]{1,0:T(8,128)(2,1)}) %reduce-scatter.15.cloned.1.call-update) | async-done | bytes 262160 | tf_op jit(solution)/shard_map/reduce_scatter | solution.py:629
  1804.4 36.8 %psum.23 = f32[]{:T(128)} all-reduce(f32[]{:T(128)S(6)} %add.342), channel_id=1, replica_groups=mesh['dp'=4,'seq'=2,'fsdp'=4] {'dp','seq','fsdp'}, use_global_device_ids=true, to_apply=%region_26.27 | all-reduce | flops 1 | bytes 8 | tf_op jit(solution)/shard_map/psum | solution.py:704
  1842.8 3.7 multiply_subtract_fusion
  (213 shorter events, 69.7 us)
Async XLA Ops:
  7.2 150.1 %all-reduce.7.cloned.1.call-start = ((), (), s32[]{:S(2)}) async-start(), calls=%async_computation.7 | async-start | bytes 204800 | tf_op jit(solution)/shard_map/psum | solution.py:575
  10.2 201.7 %all-gather.7.cloned.1.call-start = ((), (), s32[]{:S(2)}) async-start(), calls=%async_computation.6 | async-start | bytes 6488064 | tf_op jit(solution)/shard_map/all_gather | solution.py:583
  11.9 429.7 %all-gather.9.cloned.1.call-start = ((), (), s32[]{:S(2)}) async-start(), calls=%async_computation.8 | async-start | bytes 2162688 | tf_op jit(solution)/shard_map/all_gather | solution.py:583
  13.6 428.1 %all-gather.11.cloned.1.call-start = ((), (), s32[]{:S(2)}) async-start(), calls=%async_computation.16 | async-start | bytes 8650752 | tf_op jit(solution)/shard_map/all_gather | solution.py:583
  15.7 425.9 %all-gather.13.cloned.1.call-start = ((), (), s32[]{:S(2)}) async-start(), calls=%async_computation.17 | async-start | bytes 8650752 | tf_op jit(solution)/shard_map/all_gather | solution.py:583
  16.3 1047.2 %all-reduce.9.cloned.1.call-start = ((), (), s32[]{:S(2)}) async-start(), calls=%async_computation.10 | async-start | bytes 180224 | tf_op jit(solution)/shard_map/psum | solution.py:677
  20.7 13.0 copy-start.46
  22.1 141.4 %collective-permute-start = (bf16[2,1024,384]{2,1,0:T(8,128)(2,1)}, bf16[2,1024,384]{2,1,0:T(8,128)(2,1)}, u32[]{:S(2)}, u32[]{:S(2)}) collective-permute-start(bf16[2,1024,384]{2,1,0:T(8,128)(2,1)} %pad_maximum_fusion.3), channel_id=1, source_target_pairs={{0,4},{4,0},{1,5},{5,1},{2,6},{6,2},{3,7},{7,3},{8,12},{12,8},{9,1... | collective-permute-start | bytes 4718600 | tf_op jit(solution)/shard_map/ppermute | solution.py:538
  29.3 131.3 %collective-permute-start.1 = (bf16[1,1024,384]{2,1,0:T(8,128)(2,1)}, bf16[1,1024,384]{2,1,0:T(8,128)(2,1)S(1)}, u32[]{:S(2)}, u32[]{:S(2)}) collective-permute-start(bf16[1,1024,384]{2,1,0:T(8,128)(2,1)} %get-tuple-element.119), channel_id=1, source_target_pairs={{0,4},{4,0},{1,5},{5,1},{2,6},{6,2},{3,7},{7,3},{8,12},{12,8},{9,1... | collective-permute-start | bytes 2359304 | tf_op jit(solution)/shard_map/ppermute | solution.py:539
  868.3 48.0 %copy-start.40 = (pred[20]{0:T(512)(128)(4,1)S(1)}, pred[20]{0:T(512)(128)(4,1)}, u32[]{:S(2)}) copy-start(pred[20]{0:T(512)(128)(4,1)} %get-tuple-element.146) | copy-start | bytes 64
  868.3 48.0 %copy-start.41 = (pred[20]{0:T(512)(128)(4,1)S(1)}, pred[20]{0:T(512)(128)(4,1)}, u32[]{:S(2)}) copy-start(pred[20]{0:T(512)(128)(4,1)} %get-tuple-element.147) | copy-start | bytes 64
  868.4 48.0 %copy-start.42 = (pred[20]{0:T(512)(128)(4,1)S(1)}, pred[20]{0:T(512)(128)(4,1)}, u32[]{:S(2)}) copy-start(pred[20]{0:T(512)(128)(4,1)} %get-tuple-element.148) | copy-start | bytes 64
  868.4 52.2 %copy-start.4 = (bf16[2048,384]{1,0:T(8,128)(2,1)S(1)}, bf16[2048,384]{1,0:T(8,128)(2,1)}, u32[]{:S(2)}) copy-start(bf16[2048,384]{1,0:T(8,128)(2,1)} %copy-done.3) | copy-start | bytes 4718596
  868.4 52.2 %copy-start.8 = (bf16[1024,384]{1,0:T(8,128)(2,1)S(1)}, bf16[1024,384]{1,0:T(8,128)(2,1)}, u32[]{:S(2)}) copy-start(bf16[1024,384]{1,0:T(8,128)(2,1)} %copy-done.7) | copy-start | bytes 2359300
  868.4 52.2 %copy-start.10 = (bf16[1024,384]{1,0:T(8,128)(2,1)S(1)}, bf16[1024,384]{1,0:T(8,128)(2,1)}, u32[]{:S(2)}) copy-start(bf16[1024,384]{1,0:T(8,128)(2,1)} %get-tuple-element.122) | copy-start | bytes 2359300
  920.5 226.4 %reduce-scatter.7.cloned.1.call-start = ((), (), s32[]{:S(2)}) async-start(), calls=%async_computation.9 | async-start | bytes 811008 | tf_op jit(solution)/shard_map/reduce_scatter | solution.py:629
  929.8 317.4 %reduce-scatter.17.cloned.1.call-start = ((), (), s32[]{:S(2)}) async-start(), calls=%async_computation.15 | async-start | bytes 811008 | tf_op jit(solution)/shard_map/reduce_scatter | solution.py:629
  938.1 447.1 %reduce-scatter.11.cloned.1.call-start = ((), (), s32[]{:S(2)}) async-start(), calls=%async_computation.12 | async-start | bytes 2162688 | tf_op jit(solution)/shard_map/reduce_scatter | solution.py:629
  949.9 552.3 %reduce-scatter.9.cloned.1.call-start = ((), (), s32[]{:S(2)}) async-start(), calls=%async_computation.11 | async-start | bytes 6488064 | tf_op jit(solution)/shard_map/reduce_scatter | solution.py:629
  995.7 656.9 %reduce-scatter.13.cloned.1.call-start = ((), (), s32[]{:S(2)}) async-start(), calls=%async_computation.13 | async-start | bytes 8650752 | tf_op jit(solution)/shard_map/reduce_scatter | solution.py:629
  1029.3 770.0 %reduce-scatter.15.cloned.1.call-start = ((), (), s32[]{:S(2)}) async-start(), calls=%async_computation.14 | async-start | bytes 8650752 | tf_op jit(solution)/shard_map/reduce_scatter | solution.py:629
  1062.9 779.0 %copy-start.35 = (f32[7,32]{1,0:T(8,128)S(1)}, f32[7,32]{1,0:T(8,128)}, u32[]{:S(2)}) copy-start(f32[7,32]{1,0:T(8,128)} %param.45) | copy-start | bytes 2692
  1062.9 779.1 %copy-start.37 = (f32[7,32]{1,0:T(8,128)S(1)}, f32[7,32]{1,0:T(8,128)}, u32[]{:S(2)}) copy-start(f32[7,32]{1,0:T(8,128)} %param.53) | copy-start | bytes 2692
  1062.9 779.1 %copy-start.38 = (f32[7,32]{1,0:T(8,128)S(1)}, f32[7,32]{1,0:T(8,128)}, u32[]{:S(2)}) copy-start(f32[7,32]{1,0:T(8,128)} %param.61) | copy-start | bytes 2692
  1062.9 779.8 %copy-start.5 = (f32[2,32,4096]{2,1,0:T(8,128)S(1)}, f32[2,32,4096]{2,1,0:T(8,128)}, u32[]{:S(2)}) copy-start(f32[2,32,4096]{2,1,0:T(8,128)} %param.43) | copy-start | bytes 3145732
  1062.9 779.8 %copy-start.13 = (f32[2,32,4096]{2,1,0:T(8,128)S(1)}, f32[2,32,4096]{2,1,0:T(8,128)}, u32[]{:S(2)}) copy-start(f32[2,32,4096]{2,1,0:T(8,128)} %param.51) | copy-start | bytes 3145732
  1066.7 783.1 %copy-start.23 = (f32[32,276]{1,0:T(8,128)S(1)}, f32[32,276]{1,0:T(8,128)}, u32[]{:S(2)}) copy-start(f32[32,276]{1,0:T(8,128)} %param.44) | copy-start | bytes 105988
  1247.2 602.5 %copy-start.29 = (bf16[32,384]{1,0:T(8,128)(2,1)S(1)}, bf16[32,384]{1,0:T(8,128)(2,1)}, u32[]{:S(2)}) copy-start(bf16[32,384]{1,0:T(8,128)(2,1)} %reduce-scatter.17.cloned.1.call-done) | copy-start | bytes 73732
  1503.8 346.6 %copy-start.17 = (f32[32,1024]{1,0:T(8,128)S(1)}, f32[32,1024]{1,0:T(8,128)}, u32[]{:S(2)}) copy-start(f32[32,1024]{1,0:T(8,128)} %param.42) | copy-start | bytes 393220
  1503.8 346.6 %copy-start.21 = (bf16[32,1024]{1,0:T(8,128)(2,1)S(1)}, bf16[32,1024]{1,0:T(8,128)(2,1)}, u32[]{:S(2)}) copy-start(bf16[32,1024]{1,0:T(8,128)(2,1)} %reduce-scatter.11.cloned.1.call-done) | copy-start | bytes 196612
  1503.8 346.6 %copy-start.26 = (f32[32,1024]{1,0:T(8,128)S(1)}, f32[32,1024]{1,0:T(8,128)}, u32[]{:S(2)}) copy-start(f32[32,1024]{1,0:T(8,128)} %param.50) | copy-start | bytes 393220
  1503.8 346.6 %copy-start.27 = (f32[32,1024]{1,0:T(8,128)S(1)}, f32[32,1024]{1,0:T(8,128)}, u32[]{:S(2)}) copy-start(f32[32,1024]{1,0:T(8,128)} %param.58) | copy-start | bytes 393220
  (29 other events, 205.0 us)
Sparse Core Ops, SparseCore 0:
  14.2 123.7 all-reduce.6
  141.4 70.3 all-gather.6
  215.3 54.8 all-gather.8
  273.5 76.4 all-gather.10
  353.3 76.1 all-gather.12
  920.6 123.6 all-reduce.8
  1050.0 96.8 reduce-scatter.6
  1152.6 94.5 reduce-scatter.16
  1249.5 135.6 reduce-scatter.10
  1391.7 110.4 reduce-scatter.8
  1504.5 148.0 reduce-scatter.12
  1654.7 144.5 reduce-scatter.14
where the time goes:
time: 1860 us
  waiting for transfers between devices  767 us (41%)
  Pallas kernels  645 us (35%)
  blocking collectives  157 us (8%)
  matrix products  136 us (7%)
  other arithmetic  78.5 us (4%)
  local copies, waits for them, and re-layouts  50.4 us (3%)
  between operations  24.1 us (1%)
    reduce_scatter x6, waiting for transfers between devices, body(): lax.psum_scatter(values, ALL, scatter_dimension=0, tiled=True)  723 us
    pallas_call x2, Pallas kernels, attend_back(): pl.pallas_call(functools.partial(attend_back_kernel, sub), grid=(pairs, c...  204 us
    pallas_call x1, Pallas kernels, middle(): pl.pallas_call(middle_kernel, grid=(blocks,), in_specs=[by_row(width), by...  182 us
    pallas_call x2, Pallas kernels, attend(): pl.pallas_call(functools.partial(attend_kernel, sub), grid=(pairs, count...  173 us
    dot_general x8, matrix products, contract(): lax.dot_general(left, right, (((left_dim,), (right_dim,)), ((), ())), pre...  136 us
    all_gather x2, blocking collectives, body(): gather = lambda values: lax.all_gather(values, ALL, axis=0, tiled=True)  120 us
    pallas_call x1, Pallas kernels, leave(): pl.pallas_call(functools.partial(leave_kernel, asking), grid=(blocks,), i...  46.2 us
    all_gather x4, waiting for transfers between devices, body(): gather = lambda values: lax.all_gather(values, ALL, axis=0, tiled=True)  43.5 us
  transfers between devices with their start and end apart: 14, of which 7 were waited for; matrix products, arithmetic and copies ran while one was open for 11% of the time, Pallas kernels for 11%

commit v1 on v0

--- a/solution.py
+++ b/solution.py
@@ -127,6 +127,9 @@
             jax.ShapeDtypeStruct((rows, width), bf16),
             jax.ShapeDtypeStruct((rows, 3 * width), bf16),
         ],
+        cost_estimate=pl.CostEstimate(
+            flops=8 * rows * width * width, bytes_accessed=12 * rows * width, transcendentals=0
+        ),
         compiler_params=pltpu.CompilerParams(vmem_limit_bytes=VMEM_BYTES),
         name="entry",
     )(fields, embed, weight, mod)
@@ -233,6 +236,9 @@
             pltpu.VMEM((2, keys, 2 * HD), bf16),
             pltpu.VMEM((8, 2 * HD), f32),
         ],
+        cost_estimate=pl.CostEstimate(
+            flops=20 * count * keys * width, bytes_accessed=2 * count * keys, transcendentals=0
+        ),
         compiler_params=pltpu.CompilerParams(vmem_limit_bytes=VMEM_BYTES),
         name="attend",
     )(queries, memory, memory)
@@ -293,40 +299,47 @@
         grad_value[...] = value_sum[...].astype(bf16)
 
 
-def attend_back(queries, memory, grads, out, kept, inverse, places, block, sub, count, keys, width):
-    pairs = width // (2 * HD)
-    query_at, key_at, key_column, value_column = places
+def attend_back(queries, memory, grads, out, kept, inverse, places, block, sub, pairs, into, shapes):
+    query_at, key_at, key_column, value_column, grad_query_at, grad_key_at = places
+    count, keys = out.shape[0], kept.shape[3]
+    every = out.shape[1] // (2 * HD)
+    first, last = pairs
+    two = 2 * HD
+    any_place = [pl.BlockSpec(memory_space=pl.ANY)] * len(into)
+    kernel = functools.partial(attend_back_kernel, sub)
+    if into:
+        kernel = lambda *refs: attend_back_kernel(sub, *(refs[:7] + refs[10:]))
+    work = (last - first) * count * keys * two
     return pl.pallas_call(
-        functools.partial(attend_back_kernel, sub),
-        grid=(pairs, count // block),
+        kernel,
+        grid=(last - first, count // block),
         in_specs=[
-            pl.BlockSpec((block, 2 * HD), lambda h, i: (query_at // block + i, h)),
-            pl.BlockSpec((keys, 2 * HD), lambda h, i: (key_at // keys, key_column * pairs + h)),
-            pl.BlockSpec((keys, 2 * HD), lambda h, i: (key_at // keys, value_column * pairs + h)),
-            pl.BlockSpec((block, 2 * HD), lambda h, i: (query_at // block + i, h)),
-            pl.BlockSpec((block, 2 * HD), lambda h, i: (i, h)),
-            pl.BlockSpec((None, None, 2, keys, block), lambda h, i: (h, i, 0, 0, 0)),
-            pl.BlockSpec((None, 2, block), lambda h, i: (h, 0, i)),
-        ],
+            pl.BlockSpec((block, two), lambda h, i: (query_at // block + i, first + h)),
+            pl.BlockSpec((keys, two), lambda h, i: (key_at // keys, key_column * every + first + h)),
+            pl.BlockSpec((keys, two), lambda h, i: (key_at // keys, value_column * every + first + h)),
+            pl.BlockSpec((block, two), lambda h, i: (query_at // block + i, first + h)),
+            pl.BlockSpec((block, two), lambda h, i: (i, first + h)),
+            pl.BlockSpec((None, None, 2, keys, block), lambda h, i: (first + h, i, 0, 0, 0)),
+            pl.BlockSpec((None, 2, block), lambda h, i: (first + h, 0, i)),
+        ]
+        + any_place,
         out_specs=[
-            pl.BlockSpec((block, 2 * HD), lambda h, i: (i, h)),
-            pl.BlockSpec((keys, 2 * HD), lambda h, i: (0, h)),
-            pl.BlockSpec((keys, 2 * HD), lambda h, i: (0, h)),
-        ],
-        out_shape=[
-            jax.ShapeDtypeStruct((count, width), bf16),
-            jax.ShapeDtypeStruct((keys, width), bf16),
-            jax.ShapeDtypeStruct((keys, width), bf16),
-        ],
+            pl.BlockSpec((block, two), lambda h, i: (grad_query_at // block + i, h)),
+            pl.BlockSpec((keys, two), lambda h, i: (grad_key_at // keys, h)),
+            pl.BlockSpec((keys, two), lambda h, i: (grad_key_at // keys, h)),
+        ],
+        out_shape=[jax.ShapeDtypeStruct(shape, bf16) for shape in shapes],
         scratch_shapes=[
-            pltpu.VMEM((2, 2 * HD, keys), bf16),
-            pltpu.VMEM((2, keys, 2 * HD), bf16),
-            pltpu.VMEM((keys, 2 * HD), f32),
-            pltpu.VMEM((keys, 2 * HD), f32),
-        ],
+            pltpu.VMEM((2, two, keys), bf16),
+            pltpu.VMEM((2, keys, two), bf16),
+            pltpu.VMEM((keys, two), f32),
+            pltpu.VMEM((keys, two), f32),
+        ],
+        input_output_aliases={7 + index: index for index in range(len(into))},
+        cost_estimate=pl.CostEstimate(flops=32 * work, bytes_accessed=4 * work // HD, transcendentals=0),
         compiler_params=pltpu.CompilerParams(vmem_limit_bytes=VMEM_BYTES),
         name="attend_back",
-    )(queries, memory, memory, grads, out, kept, inverse)
+    )(queries, memory, memory, grads, out, kept, inverse, *into)
 
 
 def middle_kernel(
@@ -418,20 +431,31 @@
             jax.ShapeDtypeStruct((blocks, 8, pieces), f32),
         ],
         scratch_shapes=[pltpu.VMEM((block, spread), bf16)],
+        cost_estimate=pl.CostEstimate(
+            flops=60 * rows * width * width, bytes_accessed=40 * rows * width, transcendentals=0
+        ),
         compiler_params=pltpu.CompilerParams(vmem_limit_bytes=VMEM_BYTES),
         name="middle",
     )(attended, stream, target, weight_rows, mod, combine, first, second, read)
 
 
-def leave_kernel(query_blocks, grad_query, grad_memory, stream, grad_stream, weight, mod, out, sums, held):
+def leave_kernel(query_blocks, parts, *refs):
+    grads, (stream, grad_stream, weight, mod, out, sums, held) = refs[: 3 * parts], refs[3 * parts :]
     width = stream.shape[1]
+    piece = width // parts
     asks = pl.program_id(0) < query_blocks
-    grad_hidden = contract(grad_memory[...], weight[:, width:], 1, 1)
-    held[...] = grad_hidden
+    columns = lambda kind, part: pl.ds(kind * width + part * piece, piece)
+    total = None
+    for part in range(parts):
+        for kind in (1, 2):
+            term = contract(grads[3 * part + kind][...], weight[:, columns(kind, part)], 1, 1)
+            total = term if total is None else total + term
+    held[...] = total
 
     @pl.when(asks)
     def _():
-        held[...] += contract(grad_query[...], weight[:, 0:width], 1, 1)
+        for part in range(parts):
+            held[...] += contract(grads[3 * part][...], weight[:, columns(0, part)], 1, 1)
 
     normed, inverse = layer_norm(stream[...])
     grad_hidden = held[...]
@@ -443,32 +467,444 @@
     out[...] = grad.astype(bf16)
 
 
-def leave(grad_query, grad_memory, stream, grad_stream, weight, mod, block, unit_of):
-    rows, width = stream.shape
-    asking = grad_query.shape[0] // block
-    blocks = rows // block
-    by_row = lambda columns: pl.BlockSpec((block, columns), lambda i: (i, 0))
-    asked = pl.BlockSpec((block, width), lambda i: (jnp.minimum(i, asking - 1), 0))
+def leave(grads, stream, grad_stream, weight, mod, block, unit_of, start, count, query_count):
+    width = stream.shape[1]
+    parts = len(grads) // 3
+    asking = query_count // block
+    blocks, offset = count // block, start // block
+    by_row = lambda columns: pl.BlockSpec((block, columns), lambda i: (offset + i, 0))
+    asked = lambda columns: pl.BlockSpec(
+        (block, columns), lambda i: (jnp.minimum(offset + i, asking - 1), 0)
+    )
+    piece = width // parts
     return pl.pallas_call(
-        functools.partial(leave_kernel, asking),
+        functools.partial(leave_kernel, asking - offset, parts),
         grid=(blocks,),
-        in_specs=[
-            asked,
-            by_row(2 * width),
+        in_specs=[asked(piece), by_row(piece), by_row(piece)] * parts
+        + [
             by_row(width),
-            asked,
+            asked(width),
             resident(weight.shape),
-            pl.BlockSpec((None,) + mod.shape[1:], lambda i: (unit_of(i), 0, 0)),
-        ],
-        out_specs=[by_row(width), pl.BlockSpec((None, 8, width), lambda i: (i, 0, 0))],
+            pl.BlockSpec((None,) + mod.shape[1:], lambda i: (unit_of(offset + i), 0, 0)),
+        ],
+        out_specs=[
+            pl.BlockSpec((block, width), lambda i: (i, 0)),
+            pl.BlockSpec((None, 8, width), lambda i: (i, 0, 0)),
+        ],
         out_shape=[
-            jax.ShapeDtypeStruct((rows, width), bf16),
+            jax.ShapeDtypeStruct((count, width), bf16),
             jax.ShapeDtypeStruct((blocks, 8, width), f32),
         ],
         scratch_shapes=[pltpu.VMEM((block, width), f32)],
+        cost_estimate=pl.CostEstimate(
+            flops=7 * count * width * width, bytes_accessed=16 * count * width, transcendentals=0
+        ),
         compiler_params=pltpu.CompilerParams(vmem_limit_bytes=VMEM_BYTES),
         name="leave",
-    )(grad_query, grad_memory, stream, grad_stream, weight, mod)
+    )(*grads, stream, grad_stream, weight, mod)
+
+
+MESH = pl.DeviceIdType.MESH
+
+
+def where_am_i():
+    both = lax.axis_index("fsdp")
+    return (lax.axis_index("dp"), lax.axis_index("seq"), both // 2, both % 2)
+
+
+def neighbour(digit, away=1):
+    z, x, y, core = where_am_i()
+    if digit == 0:
+        return {"dp": (z + away) % 4}
+    if digit == 1:
+        return {"seq": 1 - x}
+    return {"fsdp": (1 - y) * 2 + core if digit == 2 else y * 2 + 1 - core}
+
+
+def greet():
+    barrier = pltpu.get_barrier_semaphore()
+    partners = [neighbour(1), neighbour(2), neighbour(3)] + [neighbour(0, d) for d in (1, 2, 3)]
+    for partner in partners:
+        pl.semaphore_signal(barrier, inc=1, device_id=partner, device_id_type=MESH)
+    pl.semaphore_wait(barrier, len(partners))
+
+
+class Summing:
+    steps = ((3, 1), (1, 1), (2, 1), (0, 1), (0, 2))
+
+    def __init__(self, running, came, sent, got):
+        self.running, self.came, self.sent, self.got = running, came, sent, got
+        self.copies = []
+
+    def start(self):
+        index = len(self.copies)
+        digit, bit = self.steps[index]
+        if digit == 0:
+            z = where_am_i()[0]
+            partner = {"dp": z + bit - 2 * bit * ((z // bit) % 2)}
+        else:
+            partner = neighbour(digit)
+        copy = pltpu.make_async_remote_copy(
+            src_ref=self.running.at[index],
+            dst_ref=self.came.at[index],
+            send_sem=self.sent.at[index],
+            recv_sem=self.got.at[index],
+            device_id=partner,
+            device_id_type=MESH,
+        )
+        copy.start()
+        self.copies.append(copy)
+
+    def end(self):
+        index = len(self.copies) - 1
+        self.copies[index].wait()
+        self.running[index + 1] = self.running[index] + self.came[index]
+
+
+def summing_scratch(shape):
+    return [
+        pltpu.VMEM((6,) + shape, f32),
+        pltpu.VMEM((5,) + shape, f32),
+        pltpu.SemaphoreType.DMA((5,)),
+        pltpu.SemaphoreType.DMA((5,)),
+    ]
+
+
+def small_sum_kernel(values, out, running, came, sent, got):
+    running[0] = values[...]
+    greet()
+    total = Summing(running, came, sent, got)
+    for step in range(5):
+        total.start()
+        total.end()
+    out[...] = running[5]
+
+
+def small_sum(values):
+    return pl.pallas_call(
+        small_sum_kernel,
+        out_shape=jax.ShapeDtypeStruct(values.shape, f32),
+        in_specs=[pl.BlockSpec(memory_space=pltpu.VMEM)],
+        out_specs=pl.BlockSpec(memory_space=pltpu.VMEM),
+        scratch_shapes=summing_scratch(values.shape),
+        compiler_params=pltpu.CompilerParams(collective_id=2, has_side_effects=True),
+        name="small_sum",
+    )(values)
+
+
+def spread_kernel(chunks, arrays, *refs):
+    sources, values, targets, out = refs[:arrays], refs[arrays], refs[arrays + 1 : -10], refs[-10]
+    running, came, sent, got, own_sem, z_sent, z_got, far_sent, far_got = refs[-9:]
+    z, x, y, core = where_am_i()
+    running[0] = values[...]
+    greet()
+    total = Summing(running, came, sent, got)
+    total.start()
+    own = []
+    for index in range(arrays):
+        copy = pltpu.make_async_copy(
+            sources[index], targets[index].at[z, x, y, core], own_sem.at[index]
+        )
+        copy.start()
+        own.append(copy)
+    along = {}
+    for chunk, (which, start, size, order) in enumerate(chunks):
+        columns = pl.ds(start, size)
+        for away in (1, 2, 3):
+            copy = pltpu.make_async_remote_copy(
+                src_ref=sources[which].at[:, columns],
+                dst_ref=targets[which].at[z, x, y, core, :, columns],
+                send_sem=z_sent.at[chunk, away - 1],
+                recv_sem=z_got.at[chunk, away - 1],
+                device_id=neighbour(0, away),
+                device_id_type=MESH,
+            )
+            copy.start()
+            along[chunk, away] = copy
+    for copy in own:
+        copy.wait()
+    far = {}
+    every = slice(None)
+    for time in range(len(chunks) + 2):
+        for stage in range(3):
+            chunk = time - stage
+            if not 0 <= chunk < len(chunks):
+                continue
+            which, start, size, order = chunks[chunk]
+            if stage == 0:
+                for away in (1, 2, 3):
+                    along[chunk, away].wait_recv()
+            else:
+                far[chunk, stage - 1].wait_recv()
+            at = [every, x, y, core]
+            for digit in order[:stage]:
+                at[digit] = every
+            block = targets[which].at[(*at, every, pl.ds(start, size))]
+            copy = pltpu.make_async_remote_copy(
+                src_ref=block,
+                dst_ref=block,
+                send_sem=far_sent.at[chunk, stage],
+                recv_sem=far_got.at[chunk, stage],
+                device_id=neighbour(order[stage]),
+                device_id_type=MESH,
+            )
+            copy.start()
+            far[chunk, stage] = copy
+        if time < 5:
+            total.end()
+            if time < 4:
+                total.start()
+    out[...] = running[5]
+    for chunk in range(len(chunks)):
+        far[chunk, 2].wait_recv()
+        for away in (1, 2, 3):
+            along[chunk, away].wait_send()
+        for stage in range(3):
+            far[chunk, stage].wait_send()
+
+
+def spread_start(shards, values):
+    share = shards[0].shape[0]
+    orders = ((1, 2, 3), (2, 1, 3))
+    chunks = []
+    for which, shard in enumerate(shards):
+        size = min(512, shard.shape[1])
+        for start in range(0, shard.shape[1], size):
+            chunks.append((which, start, size, orders[len(chunks) % 2]))
+    count = len(chunks)
+    grid = (4, 2, 2, 2, share)
+    anywhere = pl.BlockSpec(memory_space=pl.ANY)
+    near = pl.BlockSpec(memory_space=pltpu.VMEM)
+    results = pl.pallas_call(
+        functools.partial(spread_kernel, chunks, len(shards)),
+        out_shape=[jax.ShapeDtypeStruct(grid + (shard.shape[1],), bf16) for shard in shards]
+        + [jax.ShapeDtypeStruct(values.shape, f32)],
+        in_specs=[anywhere] * len(shards) + [near],
+        out_specs=[anywhere] * len(shards) + [near],
+        scratch_shapes=summing_scratch(values.shape)
+        + [pltpu.SemaphoreType.DMA((len(shards),))]
+        + [pltpu.SemaphoreType.DMA((count, 3))] * 4,
+        compiler_params=pltpu.CompilerParams(collective_id=0, has_side_effects=True),
+        name="spread_start",
+    )(*shards, values)
+    return [whole.reshape(32 * share, whole.shape[-1]) for whole in results[:-1]], results[-1]
+
+
+def fold_kernel(chunks, first, last, values, out_first, out_last, out, running, came, sent, got,
+                part, part_one, part_two, got_core, got_one, got_two, got_z, sents, gots):
+    place = where_am_i()
+    z, core = place[0], place[3]
+    sources, outs = (first, last), (out_first, out_last)
+    running[0] = values[...]
+    greet()
+    total = Summing(running, came, sent, got)
+    copies = {}
+    every = slice(None)
+
+    def send(chunk, stage, source, target, partner):
+        copy = pltpu.make_async_remote_copy(
+            src_ref=source,
+            dst_ref=target,
+            send_sem=sents.at[chunk, stage],
+            recv_sem=gots.at[chunk, stage],
+            device_id=partner,
+            device_id_type=MESH,
+        )
+        copy.start()
+        copies[chunk, stage] = copy
+
+    def sum_of(left, right):
+        return (left.astype(f32) + right.astype(f32)).astype(bf16)
+
+    for chunk, (which, start, size, order) in enumerate(chunks):
+        block = sources[which].at[:, :, :, 1 - core, :, pl.ds(start, size)]
+        send(chunk, 0, block, got_core.at[chunk], neighbour(3))
+    total.start()
+    for time in range(len(chunks) + 3):
+        for stage in range(1, 5):
+            chunk = time - stage + 1
+            if not 0 <= chunk < len(chunks):
+                continue
+            which, start, size, order = chunks[chunk]
+            columns = pl.ds(start, size)
+            near, far = order
+            if stage == 1:
+                copies[chunk, 0].wait_recv()
+                part[chunk] = sum_of(sources[which][:, :, :, core, :, columns], got_core[chunk])
+                at = [every, every, every]
+                at[near] = 1 - place[near]
+                send(chunk, 1, part.at[(chunk, *at)], got_one.at[chunk], neighbour(near))
+            elif stage == 2:
+                copies[chunk, 1].wait_recv()
+                at = [every, every, every]
+                at[near] = place[near]
+                part_one[chunk] = sum_of(part[(chunk, *at)], got_one[chunk])
+                send(
+                    chunk, 2, part_one.at[chunk, :, 1 - place[far]], got_two.at[chunk], neighbour(far)
+                )
+            elif stage == 3:
+                copies[chunk, 2].wait_recv()
+                part_two[chunk] = sum_of(part_one[chunk, :, place[far]], got_two[chunk])
+                for away in (1, 2, 3):
+                    source = part_two.at[chunk, (z + away) % 4]
+                    send(chunk, 2 + away, source, got_z.at[chunk, away - 1], neighbour(0, away))
+            else:
+                whole = part_two[chunk, z].astype(f32)
+                for away in (1, 2, 3):
+                    copies[chunk, 2 + away].wait_recv()
+                    whole = whole + got_z[chunk, away - 1].astype(f32)
+                outs[which][:, columns] = whole
+        if time < 5:
+            total.end()
+            if time < 4:
+                total.start()
+    for step in range(len(chunks) + 3, 5):
+        total.end()
+        if step < 4:
+            total.start()
+    out[...] = running[5]
+    for chunk in range(len(chunks)):
+        for stage in range(6):
+            copies[chunk, stage].wait_send()
+
+
+def fold_end(first, last, values):
+    rows, wide = first.shape
+    thin = last.shape[1]
+    share = rows // 32
+    size = thin
+    orders = ((1, 2), (2, 1))
+    chunks = [(0, start, size, orders[(start // size) % 2]) for start in range(0, wide, size)]
+    chunks.append((1, 0, thin, orders[len(chunks) % 2]))
+    count = len(chunks)
+    grid = (4, 2, 2, 2, share)
+    near = pl.BlockSpec(memory_space=pltpu.VMEM)
+    return pl.pallas_call(
+        functools.partial(fold_kernel, chunks),
+        out_shape=[
+            jax.ShapeDtypeStruct((share, wide), f32),
+            jax.ShapeDtypeStruct((share, thin), f32),
+            jax.ShapeDtypeStruct(values.shape, f32),
+        ],
+        in_specs=[near, near, near],
+        out_specs=[near, near, near],
+        scratch_shapes=summing_scratch(values.shape)
+        + [
+            pltpu.VMEM((count, 4, 2, 2, share, size), bf16),
+            pltpu.VMEM((count, 4, 2, share, size), bf16),
+            pltpu.VMEM((count, 4, share, size), bf16),
+            pltpu.VMEM((count, 4, 2, 2, share, size), bf16),
+            pltpu.VMEM((count, 4, 2, share, size), bf16),
+            pltpu.VMEM((count, 4, share, size), bf16),
+            pltpu.VMEM((count, 3, share, size), bf16),
+            pltpu.SemaphoreType.DMA((count, 6)),
+            pltpu.SemaphoreType.DMA((count, 6)),
+        ],
+        compiler_params=pltpu.CompilerParams(
+            collective_id=1, has_side_effects=True, vmem_limit_bytes=VMEM_BYTES
+        ),
+        name="fold_end",
+    )(first.reshape(grid + (wide,)), last.reshape(grid + (thin,)), values)
+
+
+class Links:
+    def __init__(self, sizes):
+        self.plain = sizes != (4, 2, 4)
+        swap = lambda bit, size: [(index, index ^ bit) for index in range(size)]
+        self.pairs = {
+            1: ("seq", swap(1, 2)),
+            2: ("fsdp", swap(2, 4)),
+            3: ("fsdp", swap(1, 4)),
+        }
+
+    def places(self):
+        both = lax.axis_index("fsdp")
+        return (lax.axis_index("dp"), lax.axis_index("seq"), both // 2, both % 2)
+
+    def start(self, shards, values):
+        if not self.plain:
+            return spread_start(shards, values)
+        gather = lambda shard: lax.all_gather(shard, ALL, axis=0, tiled=True)
+        return [gather(shard) for shard in shards], lax.psum(values, ALL)
+
+    def end(self, first, last, values):
+        if not self.plain:
+            return fold_end(first, last, values)
+        scatter = lambda whole: lax.psum_scatter(whole, ALL, scatter_dimension=0, tiled=True)
+        return scatter(first).astype(f32), scatter(last).astype(f32), lax.psum(values, ALL)
+
+    def total(self, values):
+        return lax.psum(values, ALL) if self.plain else small_sum(values)
+
+    def scatter(self, values):
+        if self.plain:
+            yield lax.psum_scatter(values, ALL, scatter_dimension=0, tiled=True).astype(f32)
+            return
+        rows, columns = values.shape
+        place = self.places()
+        half = columns // 2
+        blocks = values.reshape(4, 2, 2, 2, rows // 32, columns)
+        lanes = [blocks[..., :half], blocks[..., half:]]
+        for step in range(3):
+            sums = []
+            sent = []
+            for lane, order in zip(lanes, ((3, 2, 1), (3, 1, 2))):
+                digit = order[step]
+                axis, swap = self.pairs[digit]
+                pick = lambda which: lax.dynamic_slice_in_dim(lane, which, 1, digit)
+                sent.append(lax.ppermute(pick(1 - place[digit]), axis, swap))
+                sums.append(pick(place[digit]))
+            yield sent
+            lanes = [
+                (mine.astype(f32) + came.astype(f32)).astype(bf16) for mine, came in zip(sums, sent)
+            ]
+        whole = jnp.concatenate(
+            [lane.reshape(4, rows // 32, half) for lane in lanes], 2
+        )
+        came = []
+        for away in (1, 2, 3):
+            part = lax.dynamic_slice_in_dim(whole, (place[0] + away) % 4, 1, 0)
+            came.append(lax.ppermute(part, "dp", [(i, (i + away) % 4) for i in range(4)]))
+        yield came
+        total = lax.dynamic_slice_in_dim(whole, place[0], 1, 0).astype(f32)
+        for part in came:
+            total = total + part.astype(f32)
+        yield total[0]
+
+
+class Flow:
+    def __init__(self):
+        self.active = []
+        self.results = {}
+        self.pending = []
+
+    def add(self, name, chain):
+        self.active.append((name, chain))
+        self.step(only=name)
+
+    def step(self, only=None):
+        left = []
+        for name, chain in self.active:
+            if only is not None and name != only:
+                left.append((name, chain))
+                continue
+            value = next(chain)
+            if isinstance(value, list):
+                self.pending.extend(value)
+                left.append((name, chain))
+            else:
+                self.results[name] = value
+        self.active = left
+
+    def tie(self, values):
+        if not self.pending:
+            return values
+        held, self.pending = lax.optimization_barrier((values, self.pending))[0], []
+        return held
+
+    def finish(self):
+        while self.active:
+            self.step()
 
 
 def adam(master, first, second, grad, factor, step_rate):
@@ -490,7 +926,9 @@
     return block
 
 
-def body(ways, *args):
+def body(sizes, *args):
+    ways = sizes[1]
+    links = Links(sizes)
     fields, targets, interval, storm_index, valid_count, latitude, storm_scale = args[:7]
     masters, firsts, seconds = args[7:15], args[15:23], args[23:31]
     embedding, intervals, modulator, projector, combiner, feedforward, readout, vectors = masters
@@ -572,7 +1010,13 @@
     spread_vectors = lax.dynamic_update_slice(
         jnp.zeros((7, width), f32), low[7].astype(f32), (0, device * share)
     )
-    carried = lax.psum(jnp.concatenate([table.reshape(-1), spread_vectors.reshape(-1)]), ALL)
+    to_wide = lambda values: jnp.pad(values, ((0, 0), (0, WIDE - pieces)))
+    (embed, project, read), carried = links.start(
+        (to_wide(low[0].T), low[3], to_wide(low[6])),
+        jnp.concatenate([table.reshape(3 * 6 * width // 128, 128), spread_vectors.reshape(-1, 128)]),
+    )
+    nothing = carried[0, 0] * 0.0
+    carried = carried.reshape(-1)
     table = carried[: table.size].reshape(DTK, 6, width)
     all_vectors = carried[table.size :].reshape(7, width)
     table = table + all_vectors[None, :6]
@@ -581,13 +1025,8 @@
     mod = jnp.concatenate([chosen, gain, jnp.zeros((have, 1, width), f32)], 1)
 
     gather = lambda values: lax.all_gather(values, ALL, axis=0, tiled=True)
-    wide_readout = jnp.pad(low[6], ((0, 0), (0, WIDE - pieces)))
-    embed = gather(jnp.pad(low[0].T, ((0, 0), (0, WIDE - pieces))))
-    project = gather(low[3])
-    combine = gather(low[4])
-    first = gather(low[5][0])
-    second = gather(low[5][1])
-    read = gather(wide_readout)
+    late = (combiner, feedforward[0], feedforward[1])
+    combine, first, second = [gather((shard + nothing).astype(bf16)) for shard in late]
 
     block = largest(512, part)
     stream, hidden_a, mixed = entry(all_rows, embed, project, mod, block, asking, unit_of(block))
@@ -595,76 +1034,103 @@
     calls = []
     for unit in range(have):
         if unit < alone:
-            calls.append((unit * patches, patches, mixed, unit * patches, 1, 2))
+            start = unit * patches
+            calls.append((patches, mixed, (start, start, 1, 2)))
         else:
             start = alone * patches + (unit - alone) * part
             behind = asking + (unit - alone) * (patches - part)
             if shared == 1 and start % patches == 0:
-                calls.append((start, part, mixed, start, 1, 2))
+                calls.append((part, mixed, (start, start, 1, 2)))
             else:
-                pieces_of = [mixed[start : start + part, width:]]
-                pieces_of.append(mixed[behind : behind + patches - part, width:])
-                calls.append((start, part, jnp.concatenate(pieces_of, 0), 0, 0, 1))
-    attended, saved = [], []
-    for start, count, memory, key_at, key_column, value_column in calls:
-        block = largest(2048, count, start if start else count)
-        where = (start, key_at, key_column, value_column)
-        sub = min(block, 1024)
-        out, kept, inverse = attend(mixed, memory, where, block, sub, count, patches, width)
-        attended.append(out)
-        saved.append((out, kept, inverse, where, block))
-    attended_rows = jnp.concatenate(attended, 0)
+                joined = jnp.concatenate(
+                    [
+                        mixed[start : start + part, width:],
+                        mixed[behind : behind + patches - part, width:],
+                    ],
+                    0,
+                )
+                calls.append((part, joined, (start, 0, 0, 1)))
+    saved = []
+    for count, memory, where in calls:
+        block = largest(1024, count, where[0] if where[0] else count)
+        saved.append(attend(mixed, memory, where, block, block, count, patches, width))
+    attended_rows = jnp.concatenate([out for out, kept, inverse in saved], 0)
 
     block = largest(256, part)
     (
         hidden_b, activated, grad_two, grad_inner, final, grad_read, grad_one, grad_attended,
         grad_stream, sums, losses,
     ) = middle(
-        attended_rows, stream[:asking], goal_rows, weight_rows, mod, combine, first, second, read, block,
+        attended_rows, stream, goal_rows, weight_rows, mod, combine, first, second, read, block,
         unit_of(block),
     )
     units_mid = [unit_of(block)(jnp.int32(i)) for i in range(sums.shape[0])]
     loss_local = jnp.sum(losses[:, 0, :])
 
-    scatter = lambda values: lax.psum_scatter(values, ALL, scatter_dimension=0, tiled=True)
+    flow = Flow()
     summed = lambda left, right: contract(left, right, 0, 0).astype(bf16)
-    shard_first = scatter(summed(hidden_b, grad_inner)).astype(f32)
-    shard_second = scatter(summed(grad_two, activated)).astype(f32)
-    shard_combine = scatter(summed(attended_rows, grad_one)).astype(f32)
-    shard_read = scatter(summed(final, grad_read)).astype(f32)
-
-    grad_queries, grad_memories = [], []
-    for (start, count, memory, unused_a, unused_b, unused_c), (out, kept, inverse, where, block) in zip(
-        calls, saved
-    ):
-        grad_query, grad_key, grad_value = attend_back(
-            mixed, memory, grad_attended, out, kept, inverse, where, block, min(block, 256), count,
-            patches, width,
+    flow.add("first", links.scatter(summed(hidden_b, grad_inner)))
+    grad_two = flow.tie(grad_two)
+    flow.step()
+    flow.add("second", links.scatter(summed(grad_two, activated)))
+    rest = jnp.concatenate([summed(attended_rows, grad_one), summed(final, grad_read)], 1)
+    grad_attended = flow.tie((grad_attended, rest))[0]
+    flow.step()
+    flow.add("rest", links.scatter(rest))
+
+    pairs = width // (2 * HD)
+    halves = 2
+    grads = []
+    for half in range(halves):
+        reach = (half * pairs // halves, (half + 1) * pairs // halves)
+        piece = width // halves
+        shapes = ((asking, piece), (have * patches, piece), (have * patches, piece))
+        into = ()
+        for unit, ((count, memory, where), (out, kept, inverse)) in enumerate(zip(calls, saved)):
+            block = kept.shape[4]
+            into = attend_back(
+                mixed, memory, grad_attended, out, kept, inverse,
+                where + (where[0], unit * patches), block, min(block, 256), reach, into, shapes,
+            )
+            grad_attended, into = flow.tie((grad_attended, into))
+            flow.step()
+        if not (alone and shared <= 1):
+            own_part = lambda values, unit, low_row, high_row: values[
+                unit * patches + low_row : unit * patches + high_row
+            ]
+            into = (into[0],) + tuple(
+                jnp.concatenate(
+                    [values[: alone * patches]]
+                    + [own_part(values, unit, 0, part) for unit in range(alone, have)]
+                    + [own_part(values, unit, part, patches) for unit in range(alone, have)],
+                    0,
+                )
+                for values in into[1:]
+            )
+        grads.extend(into)
+        pieces_of = [summed(hidden_a[:asking], into[0])]
+        pieces_of += [summed(hidden_a, values) for values in into[1:]]
+        last_part = jnp.concatenate(pieces_of, 1)
+        if half < halves - 1:
+            flow.add("project" + str(half), links.scatter(last_part))
+    block = largest(512, part)
+    grad_zero, sums_a, units_out = [], [], []
+    for start, count in ((0, alone * patches), (alone * patches, (have - alone) * patches)):
+        if count == 0:
+            continue
+        held = flow.tie(tuple(grads))
+        flow.step()
+        value, by_block = leave(
+            held, stream, grad_stream, project, mod, block, unit_of(block), start, count, asking
         )
-        grad_queries.append(grad_query)
-        grad_memories.append(jnp.concatenate([grad_key, grad_value], 1))
-    grad_query_rows = jnp.concatenate(grad_queries, 0)
-    grad_memory_rows = jnp.concatenate(
-        grad_memories[:alone]
-        + [values[:part] for values in grad_memories[alone:]]
-        + [values[part:] for values in grad_memories[alone:]],
-        0,
-    )
-    shard_project = scatter(
-        jnp.concatenate(
-            [
-                summed(hidden_a[:asking], grad_query_rows),
-                summed(hidden_a, grad_memory_rows),
-            ],
-            1,
-        )
-    ).astype(f32)
-    block = largest(512, part)
-    grad_zero, sums_a = leave(
-        grad_query_rows, grad_memory_rows, stream, grad_stream, project, mod, block, unit_of(block)
-    )
-    units_out = [unit_of(block)(jnp.int32(i)) for i in range(sums_a.shape[0])]
-    shard_embed = scatter(summed(grad_zero, all_rows)).astype(f32)
+        grad_zero.append(value)
+        sums_a.append(by_block)
+        units_out += [unit_of(block)(jnp.int32(start // block + i)) for i in range(count // block)]
+    grad_embed = summed(jnp.concatenate(grad_zero, 0), all_rows)
+    flow.finish()
+    shard_first, shard_second = flow.results["first"], flow.results["second"]
+    shard_combine, shard_read = flow.results["rest"][:, :width], flow.results["rest"][:, width:]
+    sums_a = jnp.concatenate(sums_a, 0)
 
     by_block = jnp.concatenate([sums, sums_a], 0)
     kind_block = kinds[jnp.stack(units_mid + units_out)]
@@ -674,10 +1140,13 @@
             for kind in range(DTK)
         ]
     )
-    carried = lax.psum(
-        jnp.concatenate([grad_table[:, :7].reshape(-1), loss_local.reshape(1)]), ALL
-    )
-    loss_total = carried[-1]
+    loss_row = jnp.full((1, 128), loss_local)
+    small = jnp.concatenate([grad_table[:, :7].reshape(-1, 128), loss_row])
+    shard_last, shard_embed, carried = links.end(last_part, grad_embed, small)
+    by_half = [flow.results["project" + str(half)] for half in range(halves - 1)] + [shard_last]
+    by_half = jnp.stack(by_half, 1).reshape(share, halves, 3, width // halves)
+    shard_project = by_half.transpose(0, 2, 1, 3).reshape(share, 3 * width)
+    loss_total = carried[-1, 0]
     grad_table = carried[:-1].reshape(DTK, 7, width)
     grad_mod = grad_table[:, :6].reshape(DTK, 6 * width)
     shard_vectors = lax.dynamic_slice_in_dim(jnp.sum(grad_table, 0), device * share, share, 1)
@@ -701,7 +1170,8 @@
         shard_read[:, :pieces],
         shard_vectors,
     )
-    squares = lax.psum(sum(jnp.sum(grad * grad) for grad in shards), ALL)
+    squares = sum(jnp.sum(grad * grad) for grad in shards)
+    squares = links.total(jnp.full((8, 128), squares))[0, 0]
     norm = jnp.sqrt(squares)
     factor = clip_norm / jnp.maximum(norm, clip_norm)
     results = [
@@ -722,7 +1192,7 @@
     columns, rows = P(None, ALL), P(ALL, None)
     weights = (columns, columns, rows, rows, rows, P(None, ALL, None), rows, columns)
     return jax.shard_map(
-        functools.partial(body, mesh.shape["seq"]),
+        functools.partial(body, tuple(mesh.shape[axis] for axis in ALL)),
         mesh=mesh,
         in_specs=(data, data) + (P(),) * 5 + weights * 3,
         out_specs=weights * 3 + (P(),) * 3,

time: 1860 us -> 1220 us (0.66)
  waiting for transfers between devices: 767 us -> 87.5 us
  Pallas kernels: 645 us -> 806 us
  blocking collectives: 157 us -> 0 us
  starting transfers between devices: 4.23 us -> 45.2 us
    reduce_scatter x6 -> x0, waiting for transfers between devices: 723 us -> none  [body(): lax.psum_scatter(values, ALL, scatter_dimension=0, tiled=True)]
    pallas_call x3 -> x9, Pallas kernels: 250 us -> 387 us  [the longest x4 221 us: attend_back(): pl.pallas_call(kernel, grid=(last - first, count // block), in_specs=[pl....]
    all_gather x2 -> x0, blocking collectives: 120 us -> none  [body(): gather = lambda values: lax.all_gather(values, ALL, axis=0, tiled=True)]
    ppermute x1, waiting for transfers between devices: 0.01 us -> 43.8 us  [body(): goal_came = lax.ppermute(cut(goal, away), 'seq', ring)]
    ppermute x0 -> x36, waiting for transfers between devices: none -> 43.7 us  [the longest x24 27.5 us: scatter(): sent.append(lax.ppermute(pick(1 - place[digit]), axis, swap))]
    all_gather x4 -> x3, waiting for transfers between devices: 43.5 us -> 0.01 us  [body(): gather = lambda values: lax.all_gather(values, ALL, axis=0, tiled=True)]
    ppermute x0 -> x36, starting transfers between devices: none -> 43 us  [the longest x12 25.1 us: scatter(): lax.ppermute(part, 'dp', [(i, (i + away) % 4) for i in range(4)])]
    psum x1 -> x0, blocking collectives: 36.8 us -> none  [body(): squares = lax.psum(sum((jnp.sum(grad * grad) for grad in shards)), ALL)]
  transfers between devices with their start and end apart: 14 -> 41, of which waited for: 7 -> 12; matrix products, arithmetic and copies ran while one was open for 11% -> 12% of each run, Pallas kernels for 11% -> 34%
where the time goes in v1:
time: 1220 us; the launch traced here: 1210 us
  Pallas kernels  806 us (66%)
  matrix products  122 us (10%)
  waiting for transfers between devices  87.5 us (7%)
  local copies, waits for them, and re-layouts  64 us (5%)
  other arithmetic  60.5 us (5%)
  starting transfers between devices  45.2 us (4%)
  between operations  25.8 us (2%)
    pallas_call x4, Pallas kernels, attend_back(): pl.pallas_call(kernel, grid=(last - first, count // block), in_specs=[pl....  221 us
    pallas_call x2, Pallas kernels, attend(): pl.pallas_call(functools.partial(attend_kernel, sub), grid=(pairs, count...  197 us
    pallas_call x1, Pallas kernels, middle(): pl.pallas_call(middle_kernel, grid=(blocks,), in_specs=[by_row(width), by...  182 us
    dot_general x12, matrix products, contract(): lax.dot_general(left, right, (((left_dim,), (right_dim,)), ((), ())), pre...  122 us
    pallas_call x1, Pallas kernels, spread_start(): pl.pallas_call(functools.partial(spread_kernel, chunks, len(shards)), out...  57.3 us
    pallas_call x2, Pallas kernels, leave(): pl.pallas_call(functools.partial(leave_kernel, asking - offset, parts), g...  53.6 us
    ppermute x1, waiting for transfers between devices, body(): goal_came = lax.ppermute(cut(goal, away), 'seq', ring)  43.8 us
    pallas_call x1, Pallas kernels, entry(): pl.pallas_call(functools.partial(entry_kernel, query_rows // block), grid...  40.6 us
  transfers between devices with their start and end apart: 41, of which 12 were waited for; matrix products, arithmetic and copies ran while one was open for 12% of the time, Pallas kernels for 34%

profile of v1, /device:TPU:0, one launch (start us, length us, event | category | flops | bytes accessed | tf_op | source)
XLA Modules:
  0.0 1211.1 jit_solution(1765709280623284174)
XLA Ops:
  14.8 57.3 %spread_start.1 = (bf16[4,2,2,2,32,384]{5,4,3,2,1,0:T(8,128)(2,1)}, bf16[4,2,2,2,32,3072]{5,4,3,2,1,0:T(8,128)(2,1)}, bf16[4,2,2,2,32,384]{5,4,3,2,1,0:T(8,128)(2,1)}, f32[200,128]{1,0:T(8,128)}) custom-call(bf16[32,384]{1,0:T(8,128)(2,1)} %pad.16.refs_0_, bf16[32,3072]{1,0:T(8,128)(2,1)} %convert_element_type.355.refs_1_, bf16[32,384]{1,0:T(8,128)(2,1)} %pad.17.refs_2_, ...), custom_call_target="tpu_custom_call" | custom-call | tf_op jit(solution)/shard_map/spread_start/pallas_call | solution.py:678
  98.1 43.8 %collective-permute-done.1 = bf16[1,1024,384]{2,1,0:T(8,128)(2,1)S(1)} collective-permute-done((bf16[1,1024,384]{2,1,0:T(8,128)(2,1)}, bf16[1,1024,384]{2,1,0:T(8,128)(2,1)S(1)}, u32[]{:S(2)}, u32[]{:S(2)}) %collective-permute-start.1) | collective-permute-done | bytes 786464 | tf_op jit(solution)/shard_map/ppermute | solution.py:977
  147.9 40.6 %entry.1 = (f32[4096,1024]{1,0:T(8,128)}, bf16[4096,1024]{1,0:T(8,128)(2,1)}, bf16[4096,3072]{1,0:T(8,128)(2,1)}) custom-call(bf16[4096,384]{1,0:T(8,128)(2,1)} %pad_maximum_fusion.field, bf16[1024,384]{1,0:T(8,128)(2,1)} %bitcast.132, bf16[1024,3072]{1,0:T(8,128)(2,1)} %bitcast.109, f32[2,8,1024]{2,1,0:T(8,128)} %maximum_maximum_fusion.mod.refs_9_), custom_call_target="tpu_custom_call" | custom-call | flops 34359738368 | bytes 50331648 | tf_op jit(solution)/shard_map/entry/pallas_call | solution.py:115
  188.5 132.1 %attend.2 = (bf16[2048,1024]{1,0:T(8,128)(2,1)}, bf16[8,2,2,2048,1024]{4,3,2,1,0:T(8,128)(2,1)}, f32[8,2,2048]{2,1,0:T(2,128)}) custom-call(bf16[4096,3072]{1,0:T(8,128)(2,1)} %get-tuple-element.103.query.key.value.refs_0_.refs_1_.refs_2_, bf16[4096,3072]{1,0:T(8,128)(2,1)} %get-tuple-element.103.query.key.value.refs_0_.refs_1_.refs_2_, ...), custom_call_target="tpu_custom_call" | custom-call | flops 85899345920 | bytes 8388608 | tf_op jit(solution)/shard_map/attend/pallas_call | solution.py:216
  320.6 4.6 constant_dynamic-update-slice_fusion.1
  325.2 64.7 %attend.3 = (bf16[1024,1024]{1,0:T(8,128)(2,1)}, bf16[8,1,2,2048,1024]{4,3,2,1,0:T(8,128)(2,1)}, f32[8,2,1024]{2,1,0:T(2,128)}) custom-call(bf16[4096,3072]{1,0:T(8,128)(2,1)} %get-tuple-element.103.query.key.value.refs_0_.refs_1_.refs_2_, bf16[4096,3072]{1,0:T(8,128)(2,1)} %get-tuple-element.103.query.key.value.refs_0_.refs_1_.refs_2_, ...), custom_call_target="tpu_custom_call" | custom-call | flops 42949672960 | bytes 4194304 | tf_op jit(solution)/shard_map/attend/pallas_call | solution.py:216
  393.1 181.9 %middle.1 = (bf16[3072,1024]{1,0:T(8,128)(2,1)}, bf16[3072,4096]{1,0:T(8,128)(2,1)}, bf16[3072,1024]{1,0:T(8,128)(2,1)}, bf16[3072,4096]{1,0:T(8,128)(2,1)}, bf1...) custom-call(bf16[3072,1024]{1,0:T(8,128)(2,1)} %constant_dynamic-upd, ...), custom_call_target="tpu_custom_call" | custom-call | flops 193273528320 | bytes 125829120 | tf_op jit(solution)/shard_map/middle/pallas_call | solution.py:409
  575.0 10.8 convolution_convert_fusion.2
  596.8 30.4 %convolution_convert_fusion.1 = bf16[1024,4096]{1,0:T(8,128)(2,1)S(1)} fusion(bf16[3072,1024]{1,0:T(8,128)(2,1)S(1)} %bitcast.138, bf16[3072,4096]{1,0:T(8,128)(2,1)} %get-tuple-element.113), kind=kOutput, calls=%fused_computation.5 | convolution fusion | flops 25773998080 | bytes 39845888 | tf_op jit(solution)/shard_map/dot_general | solution.py:56
  638.6 8.5 collective-permute-done.19
  650.5 3.5 collective-permute-done.24
  658.9 3.7 collective-permute-start.29
  669.8 32.1 %convolution_convert_fusion = bf16[1024,4096]{1,0:T(8,128)(2,1)S(1)} fusion(bf16[3072,1024]{1,0:T(8,128)(2,1)} %get-tuple-element.115, bf16[3072,4096]{1,0:T(8,128)(2,1)} %get-tuple-element.116), kind=kOutput, calls=%fused_computation.4 | convolution fusion | flops 25773998080 | bytes 39845888 | tf_op jit(solution)/shard_map/dot_general | solution.py:56
  707.0 6.9 collective-permute-done.8
  721.1 5.8 collective-permute-done.14
  726.9 10.3 collective-permute-done.15
  743.8 72.7 %attend_back.4 = (bf16[3072,512]{1,0:T(8,128)(2,1)}, bf16[4096,512]{1,0:T(8,128)(2,1)}, bf16[4096,512]{1,0:T(8,128)(2,1)}) custom-call(bf16[4096,3072]{1,0:T(8,128)(2,1)} %get-tuple-element.103.query.key.value.refs_0_.refs_1_.refs_2_, bf16[4096,3072]{1,0:T(8,128)(2,1)} %get-tuple-element.103.query.key.value.refs_0_.refs_1_.refs_2_, ...), custom_call_target="tpu_custom_call" | custom-call | flops 68719476736 | bytes 134217728 | tf_op jit(solution)/shard_map/attend_back/pallas_call | solution.py:313
  823.6 37.6 %attend_back.5 = (bf16[3072,512]{1,0:T(8,128)(2,1)}, bf16[4096,512]{1,0:T(8,128)(2,1)}, bf16[4096,512]{1,0:T(8,128)(2,1)}) custom-call(bf16[4096,3072]{1,0:T(8,128)(2,1)} %get-tuple-element.103.query.key.value.refs_0_.refs_1_.refs_2_, ...), custom_call_target="tpu_custom_call", output_to_operand_aliasing={{0}: (7, {}), {1}: (8, {}), {2}: (9, {})} | custom-call | flops 34359738368 | bytes 67108864 | tf_op jit(solution)/shard_map/attend_back/pallas_call | solution.py:313
  861.2 72.7 %attend_back.6 = (bf16[3072,512]{1,0:T(8,128)(2,1)}, bf16[4096,512]{1,0:T(8,128)(2,1)}, bf16[4096,512]{1,0:T(8,128)(2,1)}) custom-call(bf16[4096,3072]{1,0:T(8,128)(2,1)} %get-tuple-element.103.query.key.value.refs_0_.refs_1_.refs_2_, bf16[4096,3072]{1,0:T(8,128)(2,1)} %get-tuple-element.103.query.key.value.refs_0_.refs_1_.refs_2_, ...), custom_call_target="tpu_custom_call" | custom-call | flops 68719476736 | bytes 134217728 | tf_op jit(solution)/shard_map/attend_back/pallas_call | solution.py:313
  935.2 5.8 collective-permute-start.21
  943.3 7.6 convolution_convert_fusion.5
  951.0 4.6 convolution_convert_fusion.6
  955.6 3.5 fusion.8
  971.2 37.8 %attend_back.7 = (bf16[3072,512]{1,0:T(8,128)(2,1)}, bf16[4096,512]{1,0:T(8,128)(2,1)}, bf16[4096,512]{1,0:T(8,128)(2,1)}) custom-call(bf16[4096,3072]{1,0:T(8,128)(2,1)} %get-tuple-element.103.query.key.value.refs_0_.refs_1_.refs_2_, ...), custom_call_target="tpu_custom_call", output_to_operand_aliasing={{0}: (7, {}), {1}: (8, {}), {2}: (9, {})} | custom-call | flops 34359738368 | bytes 67108864 | tf_op jit(solution)/shard_map/attend_back/pallas_call | solution.py:313
  1009.0 9.3 convolution_convert_fusion.3
  1018.4 7.4 convolution_convert_fusion.4
  1025.8 3.5 fusion.11
  1046.8 27.9 %leave.2 = (bf16[2048,1024]{1,0:T(8,128)(2,1)}, f32[4,8,1024]{2,1,0:T(8,128)}) custom-call(bf16[3072,512]{1,0:T(8,128)(2,1)} %get-tuple-element.149.refs_0_, bf16[4096,512]{1,0:T(8,128)(2,1)} %get-tuple-element.150.refs_1_, bf16[4096,512]{1,0:T(8,128)(2,1)} %get-tuple-element.151.refs_2_, bf16[3072,512]{1,0:T(8,128)(2,1)} %get-tuple-element.152.refs_3_, ...), custom_call_target="tpu_custom_call" | custom-call | flops 15032385536 | bytes 33554432 | tf_op jit(solution)/shard_map/leave/pallas_call | solution.py:480
  1076.3 25.8 %leave.3 = (bf16[2048,1024]{1,0:T(8,128)(2,1)}, f32[4,8,1024]{2,1,0:T(8,128)}) custom-call(bf16[3072,512]{1,0:T(8,128)(2,1)} %get-tuple-element.149.refs_0_, bf16[4096,512]{1,0:T(8,128)(2,1)} %get-tuple-element.150.refs_1_, bf16[4096,512]{1,0:T(8,128)(2,1)} %get-tuple-element.151.refs_2_, bf16[3072,512]{1,0:T(8,128)(2,1)} %get-tuple-element.152.refs_3_, ...), custom_call_target="tpu_custom_call" | custom-call | flops 15032385536 | bytes 33554432 | tf_op jit(solution)/shard_map/leave/pallas_call | solution.py:480
  1107.2 8.9 fusion.14
  1117.5 39.3 %fold_end.1 = (f32[32,1536]{1,0:T(8,128)}, f32[32,384]{1,0:T(8,128)}, f32[169,128]{1,0:T(8,128)}) custom-call(bf16[4,2,2,2,32,1536]{5,4,3,2,1,0:T(8,128)(2,1)} %bitcast.113, bf16[4,2,2,2,32,384]{5,4,3,2,1,0:T(8,128)(2,1)} %bitcast.119, f32[169,128]{1,0:T(8,128)} %concatenate.124.values), custom_call_target="tpu_custom_call" | custom-call | tf_op jit(solution)/shard_map/fold_end/pallas_call | solution.py:782
  1171.9 15.5 %small_sum.1 = f32[8,128]{1,0:T(8,128)} custom-call(f32[8,128]{1,0:T(8,128)} %broadcast_in_dim.109.values), custom_call_target="tpu_custom_call" | custom-call | tf_op jit(solution)/shard_map/small_sum/pallas_call | solution.py:584
  (430 shorter events, 168.4 us)
Async XLA Ops:
  7.2 385.8 %all-gather.6.cloned.1.call-start = ((), (), s32[]{:S(2)}) async-start(), calls=%async_computation | async-start | bytes 2162688 | tf_op jit(solution)/shard_map/all_gather | solution.py:1027
  75.5 317.6 %all-gather.8.cloned.1.call-start = ((), (), s32[]{:S(2)}) async-start(), calls=%async_computation.1 | async-start | bytes 8650752 | tf_op jit(solution)/shard_map/all_gather | solution.py:1027
  76.4 316.7 %all-gather.10.cloned.1.call-start = ((), (), s32[]{:S(2)}) async-start(), calls=%async_computation.2 | async-start | bytes 8650752 | tf_op jit(solution)/shard_map/all_gather | solution.py:1027
  82.1 61.6 %collective-permute-start = (bf16[2,1024,384]{2,1,0:T(8,128)(2,1)}, bf16[2,1024,384]{2,1,0:T(8,128)(2,1)}, u32[]{:S(2)}, u32[]{:S(2)}) collective-permute-start(bf16[2,1024,384]{2,1,0:T(8,128)(2,1)} %pad_maximum_fusion.5), channel_id=1, source_target_pairs={{0,4},{4,0},{1,5},{5,1},{2,6},{6,2},{3,7},{7,3},{8,12},{12,8},{9,1... | collective-permute-start | bytes 4718600 | tf_op jit(solution)/shard_map/ppermute | solution.py:976
  87.7 54.2 %collective-permute-start.1 = (bf16[1,1024,384]{2,1,0:T(8,128)(2,1)}, bf16[1,1024,384]{2,1,0:T(8,128)(2,1)S(1)}, u32[]{:S(2)}, u32[]{:S(2)}) collective-permute-start(bf16[1,1024,384]{2,1,0:T(8,128)(2,1)} %get-tuple-element.223), channel_id=1, source_target_pairs={{0,4},{4,0},{1,5},{5,1},{2,6},{6,2},{3,7},{7,3},{8,12},{12,8},{9,1... | collective-permute-start | bytes 2359304 | tf_op jit(solution)/shard_map/ppermute | solution.py:977
  595.0 39.1 %collective-permute-start.12 = (bf16[4,2,2,1,32,704]{5,4,0,3,2,1:T(8,128)(2,1)S(1)}, bf16[4,2,2,1,32,704]{5,4,0,3,2,1:T(8,128)(2,1)}, u32[]{:S(2)}, u32[]{:S(2)}) collective-permute-start(bf16[4,2,2,1,32,704]{5,4,0,3,2,1:T(8,128)(2,1)S(1)} %copy.142), channel_id=1, source_target_pairs={{0,1},{1,0},{2,3},{3,2},{4,5},{5,4},{6,7},{7,6},{8,9},{9,8},{10,11... | collective-permute-start | bytes 2162696 | tf_op jit(solution)/shard_map/ppermute | solution.py:855
  630.8 34.7 %collective-permute-start.2 = (bf16[4,2,2,1,32,2048]{5,4,0,3,2,1:T(8,128)(2,1)S(1)}, bf16[4,2,2,1,32,2048]{5,4,0,3,2,1:T(8,128)(2,1)S(1)}, u32[]{:S(2)}, u32[]{:S(2)}) collective-permute-start(bf16[4,2,2,1,32,2048]{5,4,0,3,2,1:T(8,128)(2,1)S(1)} %copy.131), channel_id=1, source_target_pairs={{0,1},{1,0},{2,3},{3,2},{4,5},{5,4},{6,7},{7,6},{8,9},{9,8},{10,11... | collective-permute-start | bytes 6291464 | tf_op jit(solution)/shard_map/ppermute | solution.py:855
  631.6 36.9 %collective-permute-start.4 = (bf16[4,2,2,1,32,2048]{5,4,0,3,2,1:T(8,128)(2,1)S(1)}, bf16[4,2,2,1,32,2048]{5,4,0,3,2,1:T(8,128)(2,1)S(1)}, u32[]{:S(2)}, u32[]{:S(2)}) collective-permute-start(bf16[4,2,2,1,32,2048]{5,4,0,3,2,1:T(8,128)(2,1)S(1)} %copy.134), channel_id=1, source_target_pairs={{0,1},{1,0},{2,3},{3,2},{4,5},{5,4},{6,7},{7,6},{8,9},{9,8},{10,11... | collective-permute-start | bytes 6291464 | tf_op jit(solution)/shard_map/ppermute | solution.py:855
  635.5 11.6 collective-permute-start.19
  638.4 11.4 collective-permute-start.20
  656.3 59.5 %collective-permute-start.28 = (bf16[1,32,1408]{2,1,0:T(8,128)(2,1)S(1)}, bf16[1,32,1408]{2,1,0:T(8,128)(2,1)S(1)}, u32[]{:S(2)}, u32[]{:S(2)}) collective-permute-start(bf16[1,32,1408]{2,1,0:T(8,128)(2,1)S(1)} %get-tuple-element.247), channel_id=1, source_target_pairs={{0,8},{8,16},{16,24},{24,0},{1,9},{9,17},{17,25},{25,1},{2,10},{10... | collective-permute-start | bytes 270344 | tf_op jit(solution)/shard_map/ppermute | solution.py:867
  658.9 57.0 %collective-permute-start.29 = (bf16[1,32,1408]{2,1,0:T(8,128)(2,1)S(1)}, bf16[1,32,1408]{2,1,0:T(8,128)(2,1)S(1)}, u32[]{:S(2)}, u32[]{:S(2)}) collective-permute-start(bf16[1,32,1408]{2,1,0:T(8,128)(2,1)S(1)} %get-tuple-element.248), channel_id=1, source_target_pairs={{0,16},{8,24},{16,0},{24,8},{1,17},{9,25},{17,1},{25,9},{2,18},{10... | collective-permute-start | bytes 270344 | tf_op jit(solution)/shard_map/ppermute | solution.py:867
  662.7 54.0 %collective-permute-start.30 = (bf16[1,32,1408]{2,1,0:T(8,128)(2,1)S(1)}, bf16[1,32,1408]{2,1,0:T(8,128)(2,1)S(1)}, u32[]{:S(2)}, u32[]{:S(2)}) collective-permute-start(bf16[1,32,1408]{2,1,0:T(8,128)(2,1)S(1)} %get-tuple-element.246), channel_id=1, source_target_pairs={{0,24},{8,0},{16,8},{24,16},{1,25},{9,1},{17,9},{25,17},{2,26},{10... | collective-permute-start | bytes 270344 | tf_op jit(solution)/shard_map/ppermute | solution.py:867
  666.5 36.8 %collective-permute-start.3 = (bf16[4,2,1,1,32,2048]{5,4,0,3,2,1:T(8,128)(2,1)S(1)}, bf16[4,2,1,1,32,2048]{5,4,0,3,2,1:T(8,128)(2,1)S(1)}, u32[]{:S(2)}, u32[]{:S(2)}) collective-permute-start(bf16[4,2,1,1,32,2048]{5,4,0,3,2,1:T(8,128)(2,1)S(1)} %constant_dynamic-slice_fusion.28), channel_id=1, source_target_pairs={{0,2},{1,3},{2,0},{3,1},{4,6},{5,7},{6,4},{7,5},{8,10},{9,11},{10,... | collective-permute-start | bytes 3145736 | tf_op jit(solution)/shard_map/ppermute | solution.py:855
  669.4 36.1 %collective-permute-start.5 = (bf16[4,1,2,1,32,2048]{5,4,0,3,2,1:T(8,128)(2,1)S(1)}, bf16[4,1,2,1,32,2048]{5,4,0,3,2,1:T(8,128)(2,1)S(1)}, u32[]{:S(2)}, u32[]{:S(2)}) collective-permute-start(bf16[4,1,2,1,32,2048]{5,4,0,3,2,1:T(8,128)(2,1)S(1)} %constant_dynamic-slice_fusion.25), channel_id=1, source_target_pairs={{0,4},{4,0},{1,5},{5,1},{2,6},{6,2},{3,7},{7,3},{8,12},{12,8},{9,1... | collective-permute-start | bytes 3145736 | tf_op jit(solution)/shard_map/ppermute | solution.py:855
  713.9 24.2 %collective-permute-start.6 = (bf16[4,2,2,1,32,2048]{5,4,0,3,2,1:T(8,128)(2,1)S(1)}, bf16[4,2,2,1,32,2048]{5,4,0,3,2,1:T(8,128)(2,1)S(1)}, u32[]{:S(2)}, u32[]{:S(2)}) collective-permute-start(bf16[4,2,2,1,32,2048]{5,4,0,3,2,1:T(8,128)(2,1)S(1)} %copy.136), channel_id=1, source_target_pairs={{0,1},{1,0},{2,3},{3,2},{4,5},{5,4},{6,7},{7,6},{8,9},{9,8},{10,11... | collective-permute-start | bytes 6291464 | tf_op jit(solution)/shard_map/ppermute | solution.py:855
  715.6 22.6 %collective-permute-start.7 = (bf16[4,2,2,1,32,2048]{5,4,0,3,2,1:T(8,128)(2,1)S(1)}, bf16[4,2,2,1,32,2048]{5,4,0,3,2,1:T(8,128)(2,1)S(1)}, u32[]{:S(2)}, u32[]{:S(2)}) collective-permute-start(bf16[4,2,2,1,32,2048]{5,4,0,3,2,1:T(8,128)(2,1)S(1)} %copy.138), channel_id=1, source_target_pairs={{0,1},{1,0},{2,3},{3,2},{4,5},{5,4},{6,7},{7,6},{8,9},{9,8},{10,11... | collective-permute-start | bytes 6291464 | tf_op jit(solution)/shard_map/ppermute | solution.py:855
  715.8 11.1 collective-permute-start.14
  715.9 21.3 %collective-permute-start.15 = (bf16[1,32,4096]{2,1,0:T(8,128)(2,1)S(1)}, bf16[1,32,4096]{2,1,0:T(8,128)(2,1)S(1)}, u32[]{:S(2)}, u32[]{:S(2)}) collective-permute-start(bf16[1,32,4096]{2,1,0:T(8,128)(2,1)S(1)} %get-tuple-element.240), channel_id=1, source_target_pairs={{0,16},{8,24},{16,0},{24,8},{1,17},{9,25},{17,1},{25,9},{2,18},{10... | collective-permute-start | bytes 786440 | tf_op jit(solution)/shard_map/ppermute | solution.py:867
  716.7 20.5 %collective-permute-start.16 = (bf16[1,32,4096]{2,1,0:T(8,128)(2,1)S(1)}, bf16[1,32,4096]{2,1,0:T(8,128)(2,1)S(1)}, u32[]{:S(2)}, u32[]{:S(2)}) collective-permute-start(bf16[1,32,4096]{2,1,0:T(8,128)(2,1)S(1)} %get-tuple-element.238), channel_id=1, source_target_pairs={{0,24},{8,0},{16,8},{24,16},{1,25},{9,1},{17,9},{25,17},{2,26},{10... | collective-permute-start | bytes 786440 | tf_op jit(solution)/shard_map/ppermute | solution.py:867
  739.2 77.3 %collective-permute-start.10 = (bf16[4,2,1,1,32,2048]{5,4,0,3,2,1:T(8,128)(2,1)S(1)}, bf16[4,2,1,1,32,2048]{5,4,0,3,2,1:T(8,128)(2,1)}, u32[]{:S(2)}, u32[]{:S(2)}) collective-permute-start(bf16[4,2,1,1,32,2048]{5,4,0,3,2,1:T(8,128)(2,1)S(1)} %constant_dynamic-slice_fusion.19), channel_id=1, source_target_pairs={{0,2},{1,3},{2,0},{3,1},{4,6},{5,7},{6,4},{7,5},{8,10},{9,11},{10,... | collective-permute-start | bytes 3145736 | tf_op jit(solution)/shard_map/ppermute | solution.py:855
  743.1 73.4 %collective-permute-start.11 = (bf16[4,1,2,1,32,2048]{5,4,0,3,2,1:T(8,128)(2,1)}, bf16[4,1,2,1,32,2048]{5,4,0,3,2,1:T(8,128)(2,1)}, u32[]{:S(2)}, u32[]{:S(2)}) collective-permute-start(bf16[4,1,2,1,32,2048]{5,4,0,3,2,1:T(8,128)(2,1)} %constant_dynamic-slice_fusion.17), channel_id=1, source_target_pairs={{0,4},{4,0},{1,5},{5,1},{2,6},{6,2},{3,7},{7,3},{8,12},{12,8},{9,1... | collective-permute-start | bytes 3145736 | tf_op jit(solution)/shard_map/ppermute | solution.py:855
  818.4 42.8 %collective-permute-start.17 = (bf16[4,1,1,1,32,2048]{5,4,0,3,2,1:T(8,128)(2,1)S(1)}, bf16[4,1,1,1,32,2048]{5,4,0,3,2,1:T(8,128)(2,1)S(1)}, u32[]{:S(2)}, u32[]{:S(2)}) collective-permute-start(bf16[4,1,1,1,32,2048]{5,4,0,3,2,1:T(8,128)(2,1)S(1)} %constant_dynamic-slice_fusion.14), channel_id=1, source_target_pairs={{0,4},{4,0},{1,5},{5,1},{2,6},{6,2},{3,7},{7,3},{8,12},{12,8},{9,1... | collective-permute-start | bytes 1572872 | tf_op jit(solution)/shard_map/ppermute | solution.py:855
  822.2 39.0 %collective-permute-start.18 = (bf16[4,1,1,1,32,2048]{5,4,0,3,2,1:T(8,128)(2,1)}, bf16[4,1,1,1,32,2048]{5,4,0,3,2,1:T(8,128)(2,1)S(1)}, u32[]{:S(2)}, u32[]{:S(2)}) collective-permute-start(bf16[4,1,1,1,32,2048]{5,4,0,3,2,1:T(8,128)(2,1)} %constant_dynamic-slice_fusion.13), channel_id=1, source_target_pairs={{0,2},{1,3},{2,0},{3,1},{4,6},{5,7},{6,4},{7,5},{8,10},{9,11},{10,... | collective-permute-start | bytes 1572872 | tf_op jit(solution)/shard_map/ppermute | solution.py:855
  935.2 30.4 %collective-permute-start.21 = (bf16[1,32,4096]{2,1,0:T(8,128)(2,1)}, bf16[1,32,4096]{2,1,0:T(8,128)(2,1)S(1)}, u32[]{:S(2)}, u32[]{:S(2)}) collective-permute-start(bf16[1,32,4096]{2,1,0:T(8,128)(2,1)} %get-tuple-element.236), channel_id=1, source_target_pairs={{0,8},{8,16},{16,24},{24,0},{1,9},{9,17},{17,25},{25,1},{2,10},{10... | collective-permute-start | bytes 786440 | tf_op jit(solution)/shard_map/ppermute | solution.py:867
  940.9 24.6 %collective-permute-start.22 = (bf16[1,32,4096]{2,1,0:T(8,128)(2,1)}, bf16[1,32,4096]{2,1,0:T(8,128)(2,1)}, u32[]{:S(2)}, u32[]{:S(2)}) collective-permute-start(bf16[1,32,4096]{2,1,0:T(8,128)(2,1)} %get-tuple-element.237), channel_id=1, source_target_pairs={{0,16},{8,24},{16,0},{24,8},{1,17},{9,25},{17,1},{25,9},{2,18},{10... | collective-permute-start | bytes 786440 | tf_op jit(solution)/shard_map/ppermute | solution.py:867
  940.9 24.6 %collective-permute-start.23 = (bf16[1,32,4096]{2,1,0:T(8,128)(2,1)}, bf16[1,32,4096]{2,1,0:T(8,128)(2,1)}, u32[]{:S(2)}, u32[]{:S(2)}) collective-permute-start(bf16[1,32,4096]{2,1,0:T(8,128)(2,1)} %get-tuple-element.235), channel_id=1, source_target_pairs={{0,24},{8,0},{16,8},{24,16},{1,25},{9,1},{17,9},{25,17},{2,26},{10... | collective-permute-start | bytes 786440 | tf_op jit(solution)/shard_map/ppermute | solution.py:867
  968.6 40.4 %collective-permute-start.31 = (bf16[4,2,1,1,32,768]{5,4,3,2,1,0:T(8,128)(2,1)S(1)}, bf16[4,2,1,1,32,768]{5,4,3,2,1,0:T(8,128)(2,1)S(1)}, u32[]{:S(2)}, u32[]{:S(2)}) collective-permute-start(bf16[4,2,1,1,32,768]{5,4,3,2,1,0:T(8,128)(2,1)S(1)} %constant_dynamic-slice_fusion.4), channel_id=1, source_target_pairs={{0,2},{1,3},{2,0},{3,1},{4,6},{5,7},{6,4},{7,5},{8,10},{9,11},{10,... | collective-permute-start | bytes 1179656 | tf_op jit(solution)/shard_map/ppermute | solution.py:855
  970.4 38.6 %collective-permute-start.32 = (bf16[4,1,2,1,32,768]{5,4,3,2,1,0:T(8,128)(2,1)S(1)}, bf16[4,1,2,1,32,768]{5,4,3,2,1,0:T(8,128)(2,1)S(1)}, u32[]{:S(2)}, u32[]{:S(2)}) collective-permute-start(bf16[4,1,2,1,32,768]{5,4,3,2,1,0:T(8,128)(2,1)S(1)} %constant_dynamic-slice_fusion.3), channel_id=1, source_target_pairs={{0,4},{4,0},{1,5},{5,1},{2,6},{6,2},{3,7},{7,3},{8,12},{12,8},{9,1... | collective-permute-start | bytes 1179656 | tf_op jit(solution)/shard_map/ppermute | solution.py:855
  1042.9 33.3 %collective-permute-start.35 = (bf16[1,32,1536]{2,1,0:T(8,128)(2,1)}, bf16[1,32,1536]{2,1,0:T(8,128)(2,1)S(1)}, u32[]{:S(2)}, u32[]{:S(2)}) collective-permute-start(bf16[1,32,1536]{2,1,0:T(8,128)(2,1)} %get-tuple-element.244), channel_id=1, source_target_pairs={{0,8},{8,16},{16,24},{24,0},{1,9},{9,17},{17,25},{25,1},{2,10},{10... | collective-permute-start | bytes 294920 | tf_op jit(solution)/shard_map/ppermute | solution.py:867
  1042.9 33.3 %collective-permute-start.36 = (bf16[1,32,1536]{2,1,0:T(8,128)(2,1)S(1)}, bf16[1,32,1536]{2,1,0:T(8,128)(2,1)S(1)}, u32[]{:S(2)}, u32[]{:S(2)}) collective-permute-start(bf16[1,32,1536]{2,1,0:T(8,128)(2,1)S(1)} %get-tuple-element.245), channel_id=1, source_target_pairs={{0,16},{8,24},{16,0},{24,8},{1,17},{9,25},{17,1},{25,9},{2,18},{10... | collective-permute-start | bytes 294920 | tf_op jit(solution)/shard_map/ppermute | solution.py:867
  1045.5 30.8 %collective-permute-start.37 = (bf16[1,32,1536]{2,1,0:T(8,128)(2,1)S(1)}, bf16[1,32,1536]{2,1,0:T(8,128)(2,1)S(1)}, u32[]{:S(2)}, u32[]{:S(2)}) collective-permute-start(bf16[1,32,1536]{2,1,0:T(8,128)(2,1)S(1)} %get-tuple-element.243), channel_id=1, source_target_pairs={{0,24},{8,0},{16,8},{24,16},{1,25},{9,1},{17,9},{25,17},{2,26},{10... | collective-permute-start | bytes 294920 | tf_op jit(solution)/shard_map/ppermute | solution.py:867
  (100 other events, 1164.0 us)
Sparse Core Ops, SparseCore 0:
  75.6 60.0 all-gather.5
  139.2 76.4 all-gather.7
  219.1 76.1 all-gather.9

commit v2 on v0

--- a/solution.py
+++ b/solution.py
@@ -36,6 +36,7 @@
     -6.638614747540505e-08,
 )
 ERF_END = 21.16
+TILE = 1024
 
 
 def step_rates():
@@ -89,6 +90,497 @@
 
 def resident(shape):
     return pl.BlockSpec(shape, lambda *place: (0,) * len(shape), pipeline_mode=pl.Buffered(1))
+
+
+MESH = pl.DeviceIdType.MESH
+
+
+def where_am_i():
+    both = lax.axis_index("fsdp")
+    return (lax.axis_index("dp"), lax.axis_index("seq"), both // 2, both % 2)
+
+
+def neighbour(digit, away=1):
+    z, x, y, core = where_am_i()
+    if digit == 0:
+        return {"dp": (z + away) % 4}
+    if digit == 1:
+        return {"seq": 1 - x}
+    return {"fsdp": (1 - y) * 2 + core if digit == 2 else y * 2 + 1 - core}
+
+
+def greet():
+    barrier = pltpu.get_barrier_semaphore()
+    partners = [neighbour(1), neighbour(2), neighbour(3)] + [neighbour(0, d) for d in (1, 2, 3)]
+    for partner in partners:
+        pl.semaphore_signal(barrier, inc=1, device_id=partner, device_id_type=MESH)
+    pl.semaphore_wait(barrier, len(partners))
+
+
+class Summing:
+    steps = ((3, 1), (1, 1), (2, 1), (0, 1), (0, 2))
+
+    def __init__(self, running, came, sent, got):
+        self.running, self.came, self.sent, self.got = running, came, sent, got
+        self.copies = []
+
+    def start(self):
+        index = len(self.copies)
+        digit, bit = self.steps[index]
+        if digit == 0:
+            z = where_am_i()[0]
+            partner = {"dp": z + bit - 2 * bit * ((z // bit) % 2)}
+        else:
+            partner = neighbour(digit)
+        copy = pltpu.make_async_remote_copy(
+            src_ref=self.running.at[index],
+            dst_ref=self.came.at[index],
+            send_sem=self.sent.at[index],
+            recv_sem=self.got.at[index],
+            device_id=partner,
+            device_id_type=MESH,
+        )
+        copy.start()
+        self.copies.append(copy)
+
+    def end(self):
+        index = len(self.copies) - 1
+        self.copies[index].wait()
+        self.running[index + 1] = self.running[index] + self.came[index]
+
+
+def summing_scratch(shape):
+    return [
+        pltpu.VMEM((6,) + shape, f32),
+        pltpu.VMEM((5,) + shape, f32),
+        pltpu.SemaphoreType.DMA((5,)),
+        pltpu.SemaphoreType.DMA((5,)),
+    ]
+
+
+def small_sum_kernel(values, out, running, came, sent, got):
+    running[0] = values[...]
+    greet()
+    total = Summing(running, came, sent, got)
+    for step in range(5):
+        total.start()
+        total.end()
+    out[...] = running[5]
+
+
+def small_sum(values):
+    return pl.pallas_call(
+        small_sum_kernel,
+        out_shape=jax.ShapeDtypeStruct(values.shape, f32),
+        in_specs=[pl.BlockSpec(memory_space=pltpu.VMEM)],
+        out_specs=pl.BlockSpec(memory_space=pltpu.VMEM),
+        scratch_shapes=summing_scratch(values.shape),
+        compiler_params=pltpu.CompilerParams(collective_id=2, has_side_effects=True),
+        name="small_sum",
+    )(values)
+
+
+def spread_kernel(chunks, arrays, *refs):
+    sources, values, targets, out = refs[:arrays], refs[arrays], refs[arrays + 1 : -10], refs[-10]
+    running, came, sent, got, own_sem, z_sent, z_got, far_sent, far_got = refs[-9:]
+    z, x, y, core = where_am_i()
+    running[0] = values[...]
+    greet()
+    total = Summing(running, came, sent, got)
+    total.start()
+    own = []
+    for index in range(arrays):
+        copy = pltpu.make_async_copy(
+            sources[index], targets[index].at[z, x, y, core], own_sem.at[index]
+        )
+        copy.start()
+        own.append(copy)
+    along = {}
+    for chunk, (which, start, size, order) in enumerate(chunks):
+        columns = pl.ds(start, size)
+        for away in (1, 2, 3):
+            copy = pltpu.make_async_remote_copy(
+                src_ref=sources[which].at[:, columns],
+                dst_ref=targets[which].at[z, x, y, core, :, columns],
+                send_sem=z_sent.at[chunk, away - 1],
+                recv_sem=z_got.at[chunk, away - 1],
+                device_id=neighbour(0, away),
+                device_id_type=MESH,
+            )
+            copy.start()
+            along[chunk, away] = copy
+    for copy in own:
+        copy.wait()
+    far = {}
+    every = slice(None)
+    for time in range(len(chunks) + 2):
+        for stage in range(3):
+            chunk = time - stage
+            if not 0 <= chunk < len(chunks):
+                continue
+            which, start, size, order = chunks[chunk]
+            if stage == 0:
+                for away in (1, 2, 3):
+                    along[chunk, away].wait_recv()
+            else:
+                far[chunk, stage - 1].wait_recv()
+            at = [every, x, y, core]
+            for digit in order[:stage]:
+                at[digit] = every
+            block = targets[which].at[(*at, every, pl.ds(start, size))]
+            copy = pltpu.make_async_remote_copy(
+                src_ref=block,
+                dst_ref=block,
+                send_sem=far_sent.at[chunk, stage],
+                recv_sem=far_got.at[chunk, stage],
+                device_id=neighbour(order[stage]),
+                device_id_type=MESH,
+            )
+            copy.start()
+            far[chunk, stage] = copy
+        if time < 5:
+            total.end()
+            if time < 4:
+                total.start()
+    out[...] = running[5]
+    for chunk in range(len(chunks)):
+        far[chunk, 2].wait_recv()
+        for away in (1, 2, 3):
+            along[chunk, away].wait_send()
+        for stage in range(3):
+            far[chunk, stage].wait_send()
+
+
+def spread_start(shards, values):
+    share = shards[0].shape[0]
+    orders = ((1, 2, 3), (2, 1, 3))
+    chunks = []
+    for which, shard in enumerate(shards):
+        size = min(512, shard.shape[1])
+        for start in range(0, shard.shape[1], size):
+            chunks.append((which, start, size, orders[len(chunks) % 2]))
+    count = len(chunks)
+    grid = (4, 2, 2, 2, share)
+    anywhere = pl.BlockSpec(memory_space=pl.ANY)
+    near = pl.BlockSpec(memory_space=pltpu.VMEM)
+    results = pl.pallas_call(
+        functools.partial(spread_kernel, chunks, len(shards)),
+        out_shape=[jax.ShapeDtypeStruct(grid + (shard.shape[1],), bf16) for shard in shards]
+        + [jax.ShapeDtypeStruct(values.shape, f32)],
+        in_specs=[anywhere] * len(shards) + [near],
+        out_specs=[anywhere] * len(shards) + [near],
+        scratch_shapes=summing_scratch(values.shape)
+        + [pltpu.SemaphoreType.DMA((len(shards),))]
+        + [pltpu.SemaphoreType.DMA((count, 3))] * 4,
+        compiler_params=pltpu.CompilerParams(collective_id=0, has_side_effects=True),
+        name="spread_start",
+    )(*shards, values)
+    return [whole.reshape(32 * share, whole.shape[-1]) for whole in results[:-1]], results[-1]
+
+
+def fold_kernel(chunks, last, values, out_last, out, running, came, sent, got,
+                part, part_one, part_two, got_core, got_one, got_two, got_z, sents, gots):
+    place = where_am_i()
+    z, core = place[0], place[3]
+    running[0] = values[...]
+    greet()
+    total = Summing(running, came, sent, got)
+    copies = {}
+    every = slice(None)
+
+    def send(chunk, stage, source, target, partner):
+        copy = pltpu.make_async_remote_copy(
+            src_ref=source,
+            dst_ref=target,
+            send_sem=sents.at[chunk, stage],
+            recv_sem=gots.at[chunk, stage],
+            device_id=partner,
+            device_id_type=MESH,
+        )
+        copy.start()
+        copies[chunk, stage] = copy
+
+    def sum_of(left, right):
+        return (left.astype(f32) + right.astype(f32)).astype(bf16)
+
+    for chunk, (start, size, order) in enumerate(chunks):
+        block = last.at[:, :, :, 1 - core, :, pl.ds(start, size)]
+        send(chunk, 0, block, got_core.at[chunk], neighbour(3))
+    total.start()
+    for time in range(len(chunks) + 3):
+        for stage in range(1, 5):
+            chunk = time - stage + 1
+            if not 0 <= chunk < len(chunks):
+                continue
+            start, size, order = chunks[chunk]
+            columns = pl.ds(start, size)
+            near, far = order
+            if stage == 1:
+                copies[chunk, 0].wait_recv()
+                part[chunk] = sum_of(last[:, :, :, core, :, columns], got_core[chunk])
+                at = [every, every, every]
+                at[near] = 1 - place[near]
+                send(chunk, 1, part.at[(chunk, *at)], got_one.at[chunk], neighbour(near))
+            elif stage == 2:
+                copies[chunk, 1].wait_recv()
+                at = [every, every, every]
+                at[near] = place[near]
+                part_one[chunk] = sum_of(part[(chunk, *at)], got_one[chunk])
+                send(
+                    chunk, 2, part_one.at[chunk, :, 1 - place[far]], got_two.at[chunk], neighbour(far)
+                )
+            elif stage == 3:
+                copies[chunk, 2].wait_recv()
+                part_two[chunk] = sum_of(part_one[chunk, :, place[far]], got_two[chunk])
+                for away in (1, 2, 3):
+                    source = part_two.at[chunk, (z + away) % 4]
+                    send(chunk, 2 + away, source, got_z.at[chunk, away - 1], neighbour(0, away))
+            else:
+                whole = part_two[chunk, z].astype(f32)
+                for away in (1, 2, 3):
+                    copies[chunk, 2 + away].wait_recv()
+                    whole = whole + got_z[chunk, away - 1].astype(f32)
+                out_last[:, columns] = whole
+        if time < 5:
+            total.end()
+            if time < 4:
+                total.start()
+    for step in range(len(chunks) + 3, 5):
+        total.end()
+        if step < 4:
+            total.start()
+    out[...] = running[5]
+    for chunk in range(len(chunks)):
+        for stage in range(6):
+            copies[chunk, stage].wait_send()
+
+
+def fold_end(last, values):
+    rows, wide = last.shape
+    share = rows // 32
+    size = 128
+    orders = ((1, 2), (2, 1))
+    chunks = [(start, size, orders[(start // size) % 2]) for start in range(0, wide, size)]
+    count = len(chunks)
+    near = pl.BlockSpec(memory_space=pltpu.VMEM)
+    return pl.pallas_call(
+        functools.partial(fold_kernel, chunks),
+        out_shape=[
+            jax.ShapeDtypeStruct((share, wide), f32),
+            jax.ShapeDtypeStruct(values.shape, f32),
+        ],
+        in_specs=[near, near],
+        out_specs=[near, near],
+        scratch_shapes=summing_scratch(values.shape)
+        + [
+            pltpu.VMEM((count, 4, 2, 2, share, size), bf16),
+            pltpu.VMEM((count, 4, 2, share, size), bf16),
+            pltpu.VMEM((count, 4, share, size), bf16),
+            pltpu.VMEM((count, 4, 2, 2, share, size), bf16),
+            pltpu.VMEM((count, 4, 2, share, size), bf16),
+            pltpu.VMEM((count, 4, share, size), bf16),
+            pltpu.VMEM((count, 3, share, size), bf16),
+            pltpu.SemaphoreType.DMA((count, 6)),
+            pltpu.SemaphoreType.DMA((count, 6)),
+        ],
+        compiler_params=pltpu.CompilerParams(
+            collective_id=1, has_side_effects=True, vmem_limit_bytes=VMEM_BYTES
+        ),
+        name="fold_end",
+    )(last.reshape(4, 2, 2, 2, share, wide), values)
+
+
+class Ride:
+    def __init__(self, arrays, lanes, columns, steps, collective):
+        rows = arrays[0].shape[0]
+        self.share = rows // 32
+        self.arrays = [array.reshape(4, 2, 2, 2, self.share, array.shape[1]) for array in arrays]
+        self.lanes, self.columns, self.steps, self.collective = lanes, columns, steps, collective
+        self.size = 128
+        while columns % self.size or columns // self.size + 4 > steps:
+            self.size += 128
+        self.chunks = columns // self.size
+
+    def in_specs(self):
+        return [pl.BlockSpec(memory_space=pl.ANY)] * len(self.arrays)
+
+    def out_specs(self):
+        return [pl.BlockSpec((self.share, self.columns), lambda *place: (0, 0))] * 2
+
+    def out_shape(self):
+        return [jax.ShapeDtypeStruct((self.share, self.columns), f32)] * 2
+
+    def scratch(self):
+        tail = (self.share, self.size)
+        whole, half, quarter = (4, 2, 2) + tail, (4, 2) + tail, (4,) + tail
+        every = (2, self.chunks)
+        return [
+            pltpu.VMEM((2, 2) + whole, bf16),
+            pltpu.VMEM(every + whole, bf16),
+            pltpu.VMEM(every + half, bf16),
+            pltpu.VMEM(every + quarter, bf16),
+            pltpu.VMEM(every + (3,) + tail, bf16),
+            pltpu.VMEM((2, 2) + whole, bf16),
+            pltpu.VMEM((2, 2) + half, bf16),
+            pltpu.VMEM((2, 2) + quarter, bf16),
+            pltpu.SemaphoreType.DMA((2, 2)),
+            pltpu.SemaphoreType.DMA(every + (6,)),
+            pltpu.SemaphoreType.DMA(every + (6,)),
+        ]
+
+    def step(self, time, sources, outs, scratch):
+        own, got_core, got_one, got_two, got_z, part, part_one, part_two, own_sem, sents, gots = scratch
+        place = where_am_i()
+        z, core = place[0], place[3]
+        count, size = self.chunks, self.size
+        every = slice(None)
+
+        def sum_of(left, right):
+            return (left.astype(f32) + right.astype(f32)).astype(bf16)
+
+        def copy_of(lane, chunk, stage):
+            array, base = self.lanes[lane]
+            near, far = ((1, 2), (2, 1))[lane]
+            slot = chunk % 2
+            if stage == 0:
+                columns = pl.ds(pl.multiple_of(base + chunk * size, 128), size)
+                source = sources[array].at[:, :, :, 1 - core, :, columns]
+                target, partner = got_core.at[lane, chunk], neighbour(3)
+            elif stage == 1:
+                at = [every, every, every]
+                at[near] = 1 - place[near]
+                source, target = part.at[(lane, slot, *at)], got_one.at[lane, chunk]
+                partner = neighbour(near)
+            elif stage == 2:
+                source = part_one.at[lane, slot, :, 1 - place[far]]
+                target, partner = got_two.at[lane, chunk], neighbour(far)
+            else:
+                away = stage - 2
+                source = part_two.at[lane, slot, (z + away) % 4]
+                target, partner = got_z.at[lane, chunk, away - 1], neighbour(0, away)
+            return pltpu.make_async_remote_copy(
+                src_ref=source,
+                dst_ref=target,
+                send_sem=sents.at[lane, chunk, stage],
+                recv_sem=gots.at[lane, chunk, stage],
+                device_id=partner,
+                device_id_type=MESH,
+            )
+
+        def own_copy(lane, chunk):
+            array, base = self.lanes[lane]
+            columns = pl.ds(pl.multiple_of(base + chunk * size, 128), size)
+            source = sources[array].at[:, :, :, core, :, columns]
+            slot = chunk % 2
+            return pltpu.make_async_copy(source, own.at[lane, slot], own_sem.at[lane, slot])
+
+        @pl.when(time == 0)
+        def _():
+            greet()
+
+        for lane in range(2):
+            near, far = ((1, 2), (2, 1))[lane]
+
+            @pl.when(time < count)
+            def _():
+                copy_of(lane, time, 0).start()
+                own_copy(lane, time).start()
+
+            @pl.when((time >= 1) & (time < count + 1))
+            def _():
+                chunk = time - 1
+                own_copy(lane, chunk).wait()
+                copy_of(lane, chunk, 0).wait()
+
+                @pl.when(chunk >= 2)
+                def _():
+                    copy_of(lane, chunk - 2, 1).wait_send()
+
+                part[lane, chunk % 2] = sum_of(own[lane, chunk % 2], got_core[lane, chunk])
+                copy_of(lane, chunk, 1).start()
+
+            @pl.when((time >= 2) & (time < count + 2))
+            def _():
+                chunk = time - 2
+                copy_of(lane, chunk, 1).wait_recv()
+
+                @pl.when(chunk >= 2)
+                def _():
+                    copy_of(lane, chunk - 2, 2).wait_send()
+
+                at = [every, every, every]
+                at[near] = place[near]
+                mine = part[(lane, chunk % 2, *at)]
+                part_one[lane, chunk % 2] = sum_of(mine, got_one[lane, chunk])
+                copy_of(lane, chunk, 2).start()
+
+            @pl.when((time >= 3) & (time < count + 3))
+            def _():
+                chunk = time - 3
+                copy_of(lane, chunk, 2).wait_recv()
+
+                @pl.when(chunk >= 2)
+                def _():
+                    for away in (1, 2, 3):
+                        copy_of(lane, chunk - 2, 2 + away).wait_send()
+
+                mine = part_one[lane, chunk % 2, :, place[far]]
+                part_two[lane, chunk % 2] = sum_of(mine, got_two[lane, chunk])
+                for away in (1, 2, 3):
+                    copy_of(lane, chunk, 2 + away).start()
+
+            @pl.when((time >= 4) & (time < count + 4))
+            def _():
+                chunk = time - 4
+                whole = part_two[lane, chunk % 2, z].astype(f32)
+                for away in (1, 2, 3):
+                    copy_of(lane, chunk, 2 + away).wait_recv()
+                    whole = whole + got_z[lane, chunk, away - 1].astype(f32)
+                outs[lane][:, pl.ds(pl.multiple_of(chunk * size, 128), size)] = whole
+
+        @pl.when(time == self.steps - 1)
+        def _():
+            for lane in range(2):
+                for chunk in range(max(count - 2, 0), count):
+                    for stage in range(1, 6):
+                        copy_of(lane, chunk, stage).wait_send()
+
+
+class NoRide:
+    arrays = ()
+    collective = None
+    in_specs = out_specs = out_shape = scratch = lambda self: []
+
+    def step(self, *unused):
+        pass
+
+
+class Links:
+    def __init__(self, sizes):
+        self.plain = sizes != (4, 2, 4)
+
+    def start(self, shards, values):
+        if not self.plain:
+            return spread_start(shards, values)
+        gather = lambda shard: lax.all_gather(shard, ALL, axis=0, tiled=True)
+        return [gather(shard) for shard in shards], lax.psum(values, ALL)
+
+    def ride(self, arrays, lanes, columns, steps, collective):
+        return NoRide() if self.plain else Ride(arrays, lanes, columns, steps, collective)
+
+    def scatter(self, values, done):
+        if not self.plain:
+            return jnp.concatenate(done, 1)
+        return lax.psum_scatter(values, ALL, scatter_dimension=0, tiled=True).astype(f32)
+
+    def end(self, last, values):
+        if not self.plain:
+            return fold_end(last, values)
+        total = lax.psum_scatter(last, ALL, scatter_dimension=0, tiled=True).astype(f32)
+        return total, lax.psum(values, ALL)
+
+    def total(self, values):
+        return lax.psum(values, ALL) if self.plain else small_sum(values)
 
 
 def entry_kernel(query_blocks, field, embed, weight, mod, stream, hidden, mixed):
@@ -127,9 +619,18 @@
             jax.ShapeDtypeStruct((rows, width), bf16),
             jax.ShapeDtypeStruct((rows, 3 * width), bf16),
         ],
+        cost_estimate=pl.CostEstimate(
+            flops=8 * rows * width * width, bytes_accessed=12 * rows * width, transcendentals=0
+        ),
         compiler_params=pltpu.CompilerParams(vmem_limit_bytes=VMEM_BYTES),
         name="entry",
     )(fields, embed, weight, mod)
+
+
+def crossed():
+    row = lax.broadcasted_iota(jnp.int32, (2 * HD, 2 * HD), 0) < HD
+    column = lax.broadcasted_iota(jnp.int32, (2 * HD, 2 * HD), 1) < HD
+    return jnp.where(row != column, 1.0, 0.0).astype(bf16)
 
 
 def attend_kernel(sub, query, key, value, out, kept, inverse, value_t, key_one, stats):
@@ -148,25 +649,17 @@
         key_one[1] = jnp.where(first_lanes, one, both)
         wide = both.astype(f32)
         mean = jnp.mean(wide, 0, keepdims=True)
-        spread = (wide - mean) * (wide - mean)
+        spread = ((wide - mean) * (wide - mean)).astype(bf16)
         stats[0:1] = mean
-        for head in range(2):
-            mine = first_lanes if head == 0 else jnp.logical_not(first_lanes)
-            size = jnp.sum(jnp.where(mine, spread, 0.0), 1, keepdims=True)
-            far = jnp.max(size, 0, keepdims=True)
-            stats[1 + head : 2 + head] = jnp.broadcast_to(0.5 * jnp.sqrt(far), (1, 2 * HD))
-
-    lanes = lax.broadcasted_iota(jnp.int32, (block, 2 * HD), 1)
+        far = jnp.max(contract(spread, crossed(), 1, 0), 0, keepdims=True)
+        stats[1:2] = 0.5 * jnp.sqrt(far)
+
+    lanes = lax.broadcasted_iota(jnp.int32, (sub, 2 * HD), 1)
     wide = query[...].astype(f32)
-    level = wide * stats[0:1]
-    shifts, reaches = [], []
-    for head in range(2):
-        mine = (lanes < HD) if head == 0 else (lanes >= HD)
-        length = jnp.sqrt(jnp.sum(jnp.where(mine, wide * wide, 0.0), 1, keepdims=True))
-        reach = length * stats[1 + head : 2 + head, 0:1]
-        shifts.append(jnp.sum(jnp.where(mine, level, 0.0), 1, keepdims=True) + reach)
-        reaches.append(jnp.max(reach))
-    near = jnp.maximum(reaches[0], reaches[1]) <= 60.0
+    length = jnp.sqrt(contract((wide * wide).astype(bf16), crossed(), 1, 0))
+    reach = length * stats[1:2]
+    shifts = (-contract((wide * stats[0:1]).astype(bf16), crossed(), 1, 0) - reach).astype(bf16)
+    near = jnp.max(reach) <= 60.0
     upper = lax.broadcasted_iota(jnp.int32, (2 * HD, sub), 0) < HD
 
     def run(exact):
@@ -174,16 +667,14 @@
             rows = pl.ds(part * sub, sub)
             results = []
             for head in range(2):
-                spot = lanes[0:sub]
-                mine = (spot < HD) if head == 0 else (spot >= HD)
+                mine = (lanes < HD) if head == 0 else (lanes >= HD)
                 if exact:
                     moved = jnp.where(mine, query[rows, :], zero)
                     scores = contract(key_one[head], moved, 1, 1)
                     scores = scores - jnp.max(scores, 0, keepdims=True)
                 else:
-                    shift = (-shifts[head][part * sub : part * sub + sub]).astype(bf16)
                     free = HD if head == 0 else 0
-                    rest = jnp.where(spot == free, shift, zero)
+                    rest = jnp.where(lanes == free, shifts[part * sub : part * sub + sub], zero)
                     moved = jnp.where(mine, query[rows, :], rest)
                     scores = contract(key_one[head], moved, 1, 1)
                 weights = jnp.exp2(scores).astype(bf16)
@@ -233,6 +724,9 @@
             pltpu.VMEM((2, keys, 2 * HD), bf16),
             pltpu.VMEM((8, 2 * HD), f32),
         ],
+        cost_estimate=pl.CostEstimate(
+            flops=20 * count * keys * width, bytes_accessed=2 * count * keys, transcendentals=0
+        ),
         compiler_params=pltpu.CompilerParams(vmem_limit_bytes=VMEM_BYTES),
         name="attend",
     )(queries, memory, memory)
@@ -293,92 +787,143 @@
         grad_value[...] = value_sum[...].astype(bf16)
 
 
-def attend_back(queries, memory, grads, out, kept, inverse, places, block, sub, count, keys, width):
-    pairs = width // (2 * HD)
-    query_at, key_at, key_column, value_column = places
-    return pl.pallas_call(
-        functools.partial(attend_back_kernel, sub),
-        grid=(pairs, count // block),
+def attend_back(queries, memory, grads, out, kept, inverse, places, block, sub, into, shapes, ride):
+    query_at, key_at, key_column, value_column, grad_query_at, grad_key_at = places
+    count, keys = out.shape[0], kept.shape[3]
+    pairs = out.shape[1] // (2 * HD)
+    two = 2 * HD
+    steps = count // block
+    given, riding = len(into), len(ride.arrays)
+
+    def kernel(*refs):
+        ins, refs = refs[:7], refs[7 + given :]
+        sources, refs = refs[:riding], refs[riding:]
+        outs, refs = refs[:3], refs[3:]
+        sums, refs = refs[: 2 * bool(riding)], refs[2 * bool(riding) :]
+        ride.step(pl.program_id(0) * steps + pl.program_id(1), sources, sums, refs[4:])
+        attend_back_kernel(sub, *ins, *outs, *refs[:4])
+
+    work = pairs * count * keys * two
+    results = pl.pallas_call(
+        kernel,
+        grid=(pairs, steps),
         in_specs=[
-            pl.BlockSpec((block, 2 * HD), lambda h, i: (query_at // block + i, h)),
-            pl.BlockSpec((keys, 2 * HD), lambda h, i: (key_at // keys, key_column * pairs + h)),
-            pl.BlockSpec((keys, 2 * HD), lambda h, i: (key_at // keys, value_column * pairs + h)),
-            pl.BlockSpec((block, 2 * HD), lambda h, i: (query_at // block + i, h)),
-            pl.BlockSpec((block, 2 * HD), lambda h, i: (i, h)),
+            pl.BlockSpec((block, two), lambda h, i: (query_at // block + i, h)),
+            pl.BlockSpec((keys, two), lambda h, i: (key_at // keys, key_column * pairs + h)),
+            pl.BlockSpec((keys, two), lambda h, i: (key_at // keys, value_column * pairs + h)),
+            pl.BlockSpec((block, two), lambda h, i: (query_at // block + i, h)),
+            pl.BlockSpec((block, two), lambda h, i: (i, h)),
             pl.BlockSpec((None, None, 2, keys, block), lambda h, i: (h, i, 0, 0, 0)),
             pl.BlockSpec((None, 2, block), lambda h, i: (h, 0, i)),
-        ],
+        ]
+        + [pl.BlockSpec(memory_space=pl.ANY)] * given
+        + ride.in_specs(),
         out_specs=[
-            pl.BlockSpec((block, 2 * HD), lambda h, i: (i, h)),
-            pl.BlockSpec((keys, 2 * HD), lambda h, i: (0, h)),
-            pl.BlockSpec((keys, 2 * HD), lambda h, i: (0, h)),
-        ],
-        out_shape=[
-            jax.ShapeDtypeStruct((count, width), bf16),
-            jax.ShapeDtypeStruct((keys, width), bf16),
-            jax.ShapeDtypeStruct((keys, width), bf16),
-        ],
+            pl.BlockSpec((block, two), lambda h, i: (grad_query_at // block + i, h)),
+            pl.BlockSpec((keys, two), lambda h, i: (grad_key_at // keys, h)),
+            pl.BlockSpec((keys, two), lambda h, i: (grad_key_at // keys, h)),
+        ]
+        + ride.out_specs(),
+        out_shape=[jax.ShapeDtypeStruct(shape, bf16) for shape in shapes] + ride.out_shape(),
         scratch_shapes=[
-            pltpu.VMEM((2, 2 * HD, keys), bf16),
-            pltpu.VMEM((2, keys, 2 * HD), bf16),
-            pltpu.VMEM((keys, 2 * HD), f32),
-            pltpu.VMEM((keys, 2 * HD), f32),
-        ],
-        compiler_params=pltpu.CompilerParams(vmem_limit_bytes=VMEM_BYTES),
+            pltpu.VMEM((2, two, keys), bf16),
+            pltpu.VMEM((2, keys, two), bf16),
+            pltpu.VMEM((keys, two), f32),
+            pltpu.VMEM((keys, two), f32),
+        ]
+        + ride.scratch(),
+        input_output_aliases={7 + index: index for index in range(given)},
+        cost_estimate=pl.CostEstimate(flops=32 * work, bytes_accessed=4 * work // HD, transcendentals=0),
+        compiler_params=pltpu.CompilerParams(
+            vmem_limit_bytes=VMEM_BYTES,
+            collective_id=ride.collective,
+            has_side_effects=riding > 0,
+        ),
         name="attend_back",
-    )(queries, memory, memory, grads, out, kept, inverse)
+    )(queries, memory, memory, grads, out, kept, inverse, *into, *ride.arrays)
+    return results[:3], results[3:]
 
 
 def middle_kernel(
-    attended, stream, target, weight_rows, mod, combine, first, second, read,
+    parts, attended, stream, target, weight_rows, mod, combine, first, second, read,
     hidden, active, grad_two, grad_inner, final, grad_read, grad_one, grad_attended, grad_stream,
     sums, losses, slopes,
 ):
+    block = attended.shape[0]
     width, spread = first.shape
-    tiles = [pl.ds(start, width) for start in range(0, spread, width)]
+    size_tile = min(TILE, spread)
+    tiles = [pl.ds(start, size_tile) for start in range(0, spread, size_tile)]
     gate_a, shift_b, scale_b = mod[2:3, :], mod[3:4, :], mod[4:5, :]
     gate_b, gain = mod[5:6, :], mod[6:7, :]
-    branch_a = contract(attended[...], combine[...], 1, 0)
-    stream_one = stream[...] + gate_a * branch_a
-    norm_b, inverse_b = layer_norm(stream_one)
-    low = (norm_b * (1.0 + scale_b) + shift_b).astype(bf16)
-    hidden[...] = low
-    branch_b = None
-    for tile in tiles:
-        value, slope = gelu_pair(contract(low, first[:, tile], 1, 0))
-        value = value.astype(bf16)
-        active[:, tile] = value
-        slopes[:, tile] = slope.astype(bf16)
-        term = contract(value, second[:, tile], 1, 1)
-        branch_b = term if branch_b is None else branch_b + term
-    norm_c, inverse_c = layer_norm(stream_one + gate_b * branch_b)
-    last = (norm_c * gain).astype(bf16)
-    final[...] = last
-    diff = contract(last, read[...], 1, 0) - target[...].astype(f32)
-    losses[...] = jnp.broadcast_to(column_sum(weight_rows[:, 0:1] * diff * diff), losses.shape)
-    grad_low = (weight_rows[:, 1:2] * diff).astype(bf16)
-    grad_read[...] = grad_low
-    grad_final = contract(grad_low, read[...], 1, 1)
-    sums[6:7, :] = column_sum(grad_final * norm_c)
-    grad = norm_back(grad_final * gain, norm_c, inverse_c)
-    sums[5:6, :] = column_sum(grad * branch_b)
-    back = (grad * gate_b).astype(bf16)
-    grad_two[...] = back
-    grad_hidden = None
-    for tile in tiles:
-        inner = contract(back, second[:, tile], 1, 0)
-        inner = (inner * slopes[:, tile].astype(f32)).astype(bf16)
-        grad_inner[:, tile] = inner
-        term = contract(inner, first[:, tile], 1, 1)
-        grad_hidden = term if grad_hidden is None else grad_hidden + term
-    sums[3:4, :] = column_sum(grad_hidden)
-    sums[4:5, :] = column_sum(grad_hidden * norm_b)
-    grad = grad + norm_back(grad_hidden * (1.0 + scale_b), norm_b, inverse_b)
-    grad_stream[...] = grad
-    sums[2:3, :] = column_sum(grad * branch_a)
-    back = (grad * gate_a).astype(bf16)
-    grad_one[...] = back
-    grad_attended[...] = contract(back, combine[...], 1, 1).astype(bf16)
+
+    def run(rows, found):
+        branch_a = contract(attended[rows, :], combine[...], 1, 0)
+        yield
+        stream_one = stream[rows, :] + gate_a * branch_a
+        norm_b, inverse_b = layer_norm(stream_one)
+        low = (norm_b * (1.0 + scale_b) + shift_b).astype(bf16)
+        hidden[rows, :] = low
+        yield
+        branch_b = None
+        ahead = contract(low, first[:, tiles[0]], 1, 0)
+        for index, tile in enumerate(tiles):
+            inner = ahead
+            if index + 1 < len(tiles):
+                ahead = contract(low, first[:, tiles[index + 1]], 1, 0)
+            yield
+            value, slope = gelu_pair(inner)
+            value = value.astype(bf16)
+            active[rows, tile] = value
+            slopes[rows, tile] = slope.astype(bf16)
+            term = contract(value, second[:, tile], 1, 1)
+            branch_b = term if branch_b is None else branch_b + term
+            yield
+        norm_c, inverse_c = layer_norm(stream_one + gate_b * branch_b)
+        last = (norm_c * gain).astype(bf16)
+        final[rows, :] = last
+        yield
+        diff = contract(last, read[...], 1, 0) - target[rows, :].astype(f32)
+        found[0] = column_sum(weight_rows[rows, 0:1] * diff * diff)
+        grad_low = (weight_rows[rows, 1:2] * diff).astype(bf16)
+        grad_read[rows, :] = grad_low
+        grad_final = contract(grad_low, read[...], 1, 1)
+        yield
+        found[6] = column_sum(grad_final * norm_c)
+        grad = norm_back(grad_final * gain, norm_c, inverse_c)
+        found[5] = column_sum(grad * branch_b)
+        back = (grad * gate_b).astype(bf16)
+        grad_two[rows, :] = back
+        yield
+        grad_hidden = None
+        ahead = contract(back, second[:, tiles[0]], 1, 0)
+        for index, tile in enumerate(tiles):
+            inner = ahead
+            if index + 1 < len(tiles):
+                ahead = contract(back, second[:, tiles[index + 1]], 1, 0)
+            yield
+            inner = (inner * slopes[rows, tile].astype(f32)).astype(bf16)
+            grad_inner[rows, tile] = inner
+            term = contract(inner, first[:, tile], 1, 1)
+            grad_hidden = term if grad_hidden is None else grad_hidden + term
+            yield
+        found[3] = column_sum(grad_hidden)
+        found[4] = column_sum(grad_hidden * norm_b)
+        grad = grad + norm_back(grad_hidden * (1.0 + scale_b), norm_b, inverse_b)
+        grad_stream[rows, :] = grad
+        found[2] = column_sum(grad * branch_a)
+        back = (grad * gate_a).astype(bf16)
+        grad_one[rows, :] = back
+        yield
+        grad_attended[rows, :] = contract(back, combine[...], 1, 1).astype(bf16)
+
+    size = block // parts
+    found = [{} for part in range(parts)]
+    runs = [run(pl.ds(part * size, size), found[part]) for part in range(parts)]
+    while runs:
+        runs = [one for one in runs if next(one, runs) is not runs]
+    losses[...] = jnp.broadcast_to(sum(one[0] for one in found), losses.shape)
+    for row in (2, 3, 4, 5, 6):
+        sums[row : row + 1, :] = sum(one[row] for one in found)
     sums[0:2, :] = jnp.zeros((2, width), f32)
     sums[7:8, :] = jnp.zeros((1, width), f32)
 
@@ -394,7 +939,7 @@
         (width, bf16), (width, bf16), (width, f32),
     )
     return pl.pallas_call(
-        middle_kernel,
+        functools.partial(middle_kernel, 1),
         grid=(blocks,),
         in_specs=[
             by_row(width),
@@ -418,20 +963,24 @@
             jax.ShapeDtypeStruct((blocks, 8, pieces), f32),
         ],
         scratch_shapes=[pltpu.VMEM((block, spread), bf16)],
+        cost_estimate=pl.CostEstimate(
+            flops=60 * rows * width * width, bytes_accessed=40 * rows * width, transcendentals=0
+        ),
         compiler_params=pltpu.CompilerParams(vmem_limit_bytes=VMEM_BYTES),
         name="middle",
     )(attended, stream, target, weight_rows, mod, combine, first, second, read)
 
 
-def leave_kernel(query_blocks, grad_query, grad_memory, stream, grad_stream, weight, mod, out, sums, held):
+def leave_kernel(query_blocks, grad_query, grad_key, grad_value, stream, grad_stream, weight, mod, out, sums, held):
     width = stream.shape[1]
     asks = pl.program_id(0) < query_blocks
-    grad_hidden = contract(grad_memory[...], weight[:, width:], 1, 1)
-    held[...] = grad_hidden
+    columns = lambda kind: pl.ds(kind * width, width)
+    held[...] = contract(grad_key[...], weight[:, columns(1)], 1, 1)
+    held[...] += contract(grad_value[...], weight[:, columns(2)], 1, 1)
 
     @pl.when(asks)
     def _():
-        held[...] += contract(grad_query[...], weight[:, 0:width], 1, 1)
+        held[...] += contract(grad_query[...], weight[:, columns(0)], 1, 1)
 
     normed, inverse = layer_norm(stream[...])
     grad_hidden = held[...]
@@ -443,32 +992,52 @@
     out[...] = grad.astype(bf16)
 
 
-def leave(grad_query, grad_memory, stream, grad_stream, weight, mod, block, unit_of):
+def leave(grads, stream, grad_stream, weight, mod, block, unit_of, ride):
     rows, width = stream.shape
-    asking = grad_query.shape[0] // block
-    blocks = rows // block
-    by_row = lambda columns: pl.BlockSpec((block, columns), lambda i: (i, 0))
+    asking = grads[0].shape[0] // block
+    blocks, riding = rows // block, len(ride.arrays)
+    by_row = pl.BlockSpec((block, width), lambda i: (i, 0))
     asked = pl.BlockSpec((block, width), lambda i: (jnp.minimum(i, asking - 1), 0))
-    return pl.pallas_call(
-        functools.partial(leave_kernel, asking),
+
+    def kernel(*refs):
+        ins, refs = refs[:7], refs[7:]
+        sources, refs = refs[:riding], refs[riding:]
+        outs, refs = refs[:2], refs[2:]
+        shards, refs = refs[: 2 * bool(riding)], refs[2 * bool(riding) :]
+        ride.step(pl.program_id(0), sources, shards, refs[1:])
+        leave_kernel(asking, *ins, *outs, refs[0])
+
+    results = pl.pallas_call(
+        kernel,
         grid=(blocks,),
         in_specs=[
             asked,
-            by_row(2 * width),
-            by_row(width),
+            by_row,
+            by_row,
+            by_row,
             asked,
             resident(weight.shape),
             pl.BlockSpec((None,) + mod.shape[1:], lambda i: (unit_of(i), 0, 0)),
-        ],
-        out_specs=[by_row(width), pl.BlockSpec((None, 8, width), lambda i: (i, 0, 0))],
+        ]
+        + ride.in_specs(),
+        out_specs=[by_row, pl.BlockSpec((None, 8, width), lambda i: (i, 0, 0))] + ride.out_specs(),
         out_shape=[
             jax.ShapeDtypeStruct((rows, width), bf16),
             jax.ShapeDtypeStruct((blocks, 8, width), f32),
-        ],
-        scratch_shapes=[pltpu.VMEM((block, width), f32)],
-        compiler_params=pltpu.CompilerParams(vmem_limit_bytes=VMEM_BYTES),
+        ]
+        + ride.out_shape(),
+        scratch_shapes=[pltpu.VMEM((block, width), f32)] + ride.scratch(),
+        cost_estimate=pl.CostEstimate(
+            flops=7 * rows * width * width, bytes_accessed=16 * rows * width, transcendentals=0
+        ),
+        compiler_params=pltpu.CompilerParams(
+            vmem_limit_bytes=VMEM_BYTES,
+            collective_id=ride.collective,
+            has_side_effects=riding > 0,
+        ),
         name="leave",
-    )(grad_query, grad_memory, stream, grad_stream, weight, mod)
+    )(*grads, stream, grad_stream, weight, mod, *ride.arrays)
+    return results[:2], results[2:]
 
 
 def adam(master, first, second, grad, factor, step_rate):
@@ -490,7 +1059,9 @@
     return block
 
 
-def body(ways, *args):
+def body(sizes, *args):
+    ways = sizes[1]
+    links = Links(sizes)
     fields, targets, interval, storm_index, valid_count, latitude, storm_scale = args[:7]
     masters, firsts, seconds = args[7:15], args[15:23], args[23:31]
     embedding, intervals, modulator, projector, combiner, feedforward, readout, vectors = masters
@@ -572,7 +1143,13 @@
     spread_vectors = lax.dynamic_update_slice(
         jnp.zeros((7, width), f32), low[7].astype(f32), (0, device * share)
     )
-    carried = lax.psum(jnp.concatenate([table.reshape(-1), spread_vectors.reshape(-1)]), ALL)
+    to_wide = lambda values: jnp.pad(values, ((0, 0), (0, WIDE - pieces)))
+    (embed, project, read), carried = links.start(
+        (to_wide(low[0].T), low[3], to_wide(low[6])),
+        jnp.concatenate([table.reshape(3 * 6 * width // 128, 128), spread_vectors.reshape(-1, 128)]),
+    )
+    nothing = carried[0, 0] * 0.0
+    carried = carried.reshape(-1)
     table = carried[: table.size].reshape(DTK, 6, width)
     all_vectors = carried[table.size :].reshape(7, width)
     table = table + all_vectors[None, :6]
@@ -581,13 +1158,8 @@
     mod = jnp.concatenate([chosen, gain, jnp.zeros((have, 1, width), f32)], 1)
 
     gather = lambda values: lax.all_gather(values, ALL, axis=0, tiled=True)
-    wide_readout = jnp.pad(low[6], ((0, 0), (0, WIDE - pieces)))
-    embed = gather(jnp.pad(low[0].T, ((0, 0), (0, WIDE - pieces))))
-    project = gather(low[3])
-    combine = gather(low[4])
-    first = gather(low[5][0])
-    second = gather(low[5][1])
-    read = gather(wide_readout)
+    late = (combiner, feedforward[0], feedforward[1])
+    combine, first, second = [gather((shard + nothing).astype(bf16)) for shard in late]
 
     block = largest(512, part)
     stream, hidden_a, mixed = entry(all_rows, embed, project, mod, block, asking, unit_of(block))
@@ -595,76 +1167,87 @@
     calls = []
     for unit in range(have):
         if unit < alone:
-            calls.append((unit * patches, patches, mixed, unit * patches, 1, 2))
+            start = unit * patches
+            calls.append((patches, mixed, (start, start, 1, 2)))
         else:
             start = alone * patches + (unit - alone) * part
             behind = asking + (unit - alone) * (patches - part)
             if shared == 1 and start % patches == 0:
-                calls.append((start, part, mixed, start, 1, 2))
+                calls.append((part, mixed, (start, start, 1, 2)))
             else:
-                pieces_of = [mixed[start : start + part, width:]]
-                pieces_of.append(mixed[behind : behind + patches - part, width:])
-                calls.append((start, part, jnp.concatenate(pieces_of, 0), 0, 0, 1))
-    attended, saved = [], []
-    for start, count, memory, key_at, key_column, value_column in calls:
-        block = largest(2048, count, start if start else count)
-        where = (start, key_at, key_column, value_column)
-        sub = min(block, 1024)
-        out, kept, inverse = attend(mixed, memory, where, block, sub, count, patches, width)
-        attended.append(out)
-        saved.append((out, kept, inverse, where, block))
-    attended_rows = jnp.concatenate(attended, 0)
+                joined = jnp.concatenate(
+                    [
+                        mixed[start : start + part, width:],
+                        mixed[behind : behind + patches - part, width:],
+                    ],
+                    0,
+                )
+                calls.append((part, joined, (start, 0, 0, 1)))
+    saved = []
+    for count, memory, where in calls:
+        block = largest(1024, count, where[0] if where[0] else count)
+        saved.append(attend(mixed, memory, where, block, block, count, patches, width))
+    attended_rows = jnp.concatenate([out for out, kept, inverse in saved], 0)
 
     block = largest(256, part)
     (
         hidden_b, activated, grad_two, grad_inner, final, grad_read, grad_one, grad_attended,
         grad_stream, sums, losses,
     ) = middle(
-        attended_rows, stream[:asking], goal_rows, weight_rows, mod, combine, first, second, read, block,
+        attended_rows, stream, goal_rows, weight_rows, mod, combine, first, second, read, block,
         unit_of(block),
     )
     units_mid = [unit_of(block)(jnp.int32(i)) for i in range(sums.shape[0])]
     loss_local = jnp.sum(losses[:, 0, :])
 
-    scatter = lambda values: lax.psum_scatter(values, ALL, scatter_dimension=0, tiled=True)
     summed = lambda left, right: contract(left, right, 0, 0).astype(bf16)
-    shard_first = scatter(summed(hidden_b, grad_inner)).astype(f32)
-    shard_second = scatter(summed(grad_two, activated)).astype(f32)
-    shard_combine = scatter(summed(attended_rows, grad_one)).astype(f32)
-    shard_read = scatter(summed(final, grad_read)).astype(f32)
-
-    grad_queries, grad_memories = [], []
-    for (start, count, memory, unused_a, unused_b, unused_c), (out, kept, inverse, where, block) in zip(
-        calls, saved
-    ):
-        grad_query, grad_key, grad_value = attend_back(
-            mixed, memory, grad_attended, out, kept, inverse, where, block, min(block, 256), count,
-            patches, width,
+    grad_first, grad_second = summed(hidden_b, grad_inner), summed(grad_two, activated)
+    grad_combine, grad_readout = summed(attended_rows, grad_one), summed(final, grad_read)
+    rest = jnp.concatenate([grad_combine, grad_readout, jnp.zeros((width, WIDE // 3), bf16)], 1)
+    rides = [((grad_first, grad_second), ((0, 0), (1, 0)), grad_first.shape[1])]
+    rides += [((rest,), ((0, 0), (0, rest.shape[1] // 2)), rest.shape[1] // 2)]
+    shapes = ((asking, width), (have * patches, width), (have * patches, width))
+    into, done = (), []
+    for unit, ((count, memory, where), (out, kept, inverse)) in enumerate(zip(calls, saved)):
+        block = kept.shape[4]
+        ride = NoRide()
+        if unit < len(rides):
+            steps = width // (2 * HD) * (count // block)
+            ride = links.ride(*rides[unit], steps, 3 + unit)
+        into, ridden = attend_back(
+            mixed, memory, grad_attended, out, kept, inverse, where + (where[0], unit * patches),
+            block, min(block, 256), into, shapes, ride,
         )
-        grad_queries.append(grad_query)
-        grad_memories.append(jnp.concatenate([grad_key, grad_value], 1))
-    grad_query_rows = jnp.concatenate(grad_queries, 0)
-    grad_memory_rows = jnp.concatenate(
-        grad_memories[:alone]
-        + [values[:part] for values in grad_memories[alone:]]
-        + [values[part:] for values in grad_memories[alone:]],
-        0,
-    )
-    shard_project = scatter(
-        jnp.concatenate(
-            [
-                summed(hidden_a[:asking], grad_query_rows),
-                summed(hidden_a, grad_memory_rows),
-            ],
-            1,
+        done.append(ridden)
+    shard_first = links.scatter(grad_first, done[0][:1])
+    shard_second = links.scatter(grad_second, done[0][1:])
+    shard_rest = links.scatter(rest, done[1])
+    shard_combine, shard_read = shard_rest[:, :width], shard_rest[:, width : width + WIDE]
+    if not (alone and shared <= 1):
+        own_part = lambda values, unit, low_row, high_row: values[
+            unit * patches + low_row : unit * patches + high_row
+        ]
+        into = (into[0],) + tuple(
+            jnp.concatenate(
+                [values[: alone * patches]]
+                + [own_part(values, unit, 0, part) for unit in range(alone, have)]
+                + [own_part(values, unit, part, patches) for unit in range(alone, have)],
+                0,
+            )
+            for values in into[1:]
         )
-    ).astype(f32)
+    grad_project = jnp.concatenate(
+        [summed(hidden_a[:asking], into[0])] + [summed(hidden_a, values) for values in into[1:]], 1
+    )
     block = largest(512, part)
-    grad_zero, sums_a = leave(
-        grad_query_rows, grad_memory_rows, stream, grad_stream, project, mod, block, unit_of(block)
-    )
+    lane = grad_project.shape[1] // 2
+    ride = links.ride((grad_project,), ((0, 0), (0, lane)), lane, stream.shape[0] // block, 5)
+    (grad_zero, sums_a), ridden = leave(
+        into, stream, grad_stream, project, mod, block, unit_of(block), ride
+    )
+    shard_project = links.scatter(grad_project, ridden)
     units_out = [unit_of(block)(jnp.int32(i)) for i in range(sums_a.shape[0])]
-    shard_embed = scatter(summed(grad_zero, all_rows)).astype(f32)
+    grad_embed = summed(grad_zero, all_rows)
 
     by_block = jnp.concatenate([sums, sums_a], 0)
     kind_block = kinds[jnp.stack(units_mid + units_out)]
@@ -674,10 +1257,10 @@
             for kind in range(DTK)
         ]
     )
-    carried = lax.psum(
-        jnp.concatenate([grad_table[:, :7].reshape(-1), loss_local.reshape(1)]), ALL
-    )
-    loss_total = carried[-1]
+    loss_row = jnp.full((1, 128), loss_local)
+    small = jnp.concatenate([grad_table[:, :7].reshape(-1, 128), loss_row])
+    shard_embed, carried = links.end(grad_embed, small)
+    loss_total = carried[-1, 0]
     grad_table = carried[:-1].reshape(DTK, 7, width)
     grad_mod = grad_table[:, :6].reshape(DTK, 6 * width)
     shard_vectors = lax.dynamic_slice_in_dim(jnp.sum(grad_table, 0), device * share, share, 1)
@@ -701,7 +1284,8 @@
         shard_read[:, :pieces],
         shard_vectors,
     )
-    squares = lax.psum(sum(jnp.sum(grad * grad) for grad in shards), ALL)
+    squares = sum(jnp.sum(grad * grad) for grad in shards)
+    squares = links.total(jnp.full((8, 128), squares))[0, 0]
     norm = jnp.sqrt(squares)
     factor = clip_norm / jnp.maximum(norm, clip_norm)
     results = [
@@ -722,7 +1306,7 @@
     columns, rows = P(None, ALL), P(ALL, None)
     weights = (columns, columns, rows, rows, rows, P(None, ALL, None), rows, columns)
     return jax.shard_map(
-        functools.partial(body, mesh.shape["seq"]),
+        functools.partial(body, tuple(mesh.shape[axis] for axis in ALL)),
         mesh=mesh,
         in_specs=(data, data) + (P(),) * 5 + weights * 3,
         out_specs=weights * 3 + (P(),) * 3,

time: 1860 us -> 1090 us (0.59)
  waiting for transfers between devices: 767 us -> 43.3 us
  blocking collectives: 157 us -> 0 us
  Pallas kernels: 645 us -> 784 us
    reduce_scatter x6 -> x0, waiting for transfers between devices: 723 us -> none  [body(): lax.psum_scatter(values, ALL, scatter_dimension=0, tiled=True)]
    pallas_call x4 -> x7, Pallas kernels: 432 us -> 553 us  [the longest x2 226 us: attend_back(): pl.pallas_call(kernel, grid=(pairs, steps), in_specs=[pl.BlockSpec((block...]
    all_gather x2 -> x0, blocking collectives: 120 us -> none  [body(): gather = lambda values: lax.all_gather(values, ALL, axis=0, tiled=True)]
    all_gather x4 -> x3, waiting for transfers between devices: 43.5 us -> 0.01 us  [body(): gather = lambda values: lax.all_gather(values, ALL, axis=0, tiled=True)]
    ppermute x1, waiting for transfers between devices: 0.01 us -> 43.3 us  [body(): goal_came = lax.ppermute(cut(goal, away), 'seq', ring)]
    psum x1 -> x0, blocking collectives: 36.8 us -> none  [body(): squares = lax.psum(sum((jnp.sum(grad * grad) for grad in shards)), ALL)]
    concatenate x4 -> x3, other arithmetic: 37.6 us -> 16 us  [the longest x1 13.4 us: body(): jnp.concatenate([summed(hidden_a[:asking], into[0])] + [summed(hidden_a,...]
    dot_general x8 -> x9, matrix products: 136 us -> 124 us  [contract(): lax.dot_general(left, right, (((left_dim,), (right_dim,)), ((), ())), pre...]
  transfers between devices with their start and end apart: 14 -> 5, of which waited for: 7 -> 1; matrix products, arithmetic and copies ran while one was open for 11% -> 3% of each run, Pallas kernels for 11% -> 21%
where the time goes in v2:
time: 1090 us; the launch traced here: 1080 us
  Pallas kernels  784 us (72%)
  matrix products  124 us (11%)
  other arithmetic  60.3 us (6%)
  local copies, waits for them, and re-layouts  45.8 us (4%)
  waiting for transfers between devices  43.3 us (4%)
  between operations  24.6 us (2%)
    pallas_call x2, Pallas kernels, attend_back(): pl.pallas_call(kernel, grid=(pairs, steps), in_specs=[pl.BlockSpec((block...  226 us
    pallas_call x2, Pallas kernels, attend(): pl.pallas_call(functools.partial(attend_kernel, sub), grid=(pairs, count...  191 us
    pallas_call x1, Pallas kernels, middle(): pl.pallas_call(functools.partial(middle_kernel, 1), grid=(blocks,), in_sp...  176 us
    dot_general x9, matrix products, contract(): lax.dot_general(left, right, (((left_dim,), (right_dim,)), ((), ())), pre...  124 us
    pallas_call x1, Pallas kernels, spread_start(): pl.pallas_call(functools.partial(spread_kernel, chunks, len(shards)), out...  57.3 us
    pallas_call x1, Pallas kernels, leave(): pl.pallas_call(kernel, grid=(blocks,), in_specs=[asked, by_row, by_row, b...  55.1 us
    ppermute x1, waiting for transfers between devices, body(): goal_came = lax.ppermute(cut(goal, away), 'seq', ring)  43.3 us
    pallas_call x1, Pallas kernels, entry(): pl.pallas_call(functools.partial(entry_kernel, query_rows // block), grid...  40.6 us
  transfers between devices with their start and end apart: 5, of which 1 were waited for; matrix products, arithmetic and copies ran while one was open for 3% of the time, Pallas kernels for 21%

profile of v2, /device:TPU:0, one launch (start us, length us, event | category | flops | bytes accessed | tf_op | source)
XLA Modules:
  0.0 1084.9 jit_solution(18039415189589631699)
XLA Ops:
  14.7 57.3 %spread_start.1 = (bf16[4,2,2,2,32,384]{5,4,3,2,1,0:T(8,128)(2,1)}, bf16[4,2,2,2,32,3072]{5,4,3,2,1,0:T(8,128)(2,1)}, bf16[4,2,2,2,32,384]{5,4,3,2,1,0:T(8,128)(2,1)}, f32[200,128]{1,0:T(8,128)}) custom-call(bf16[32,384]{1,0:T(8,128)(2,1)} %pad.16.refs_0_, bf16[32,3072]{1,0:T(8,128)(2,1)} %convert_element_type.82.refs_1_, bf16[32,384]{1,0:T(8,128)(2,1)} %pad.17.refs_2_, ...), custom_call_target="tpu_custom_call" | custom-call | tf_op jit(solution)/shard_map/spread_start/pallas_call | solution.py:266
  75.5 2.1 add_convert_fusion
  77.6 2.8 copy.77
  84.5 2.8 copy.78
  99.7 43.3 %collective-permute-done.1 = bf16[1,1024,384]{2,1,0:T(8,128)(2,1)S(1)} collective-permute-done((bf16[1,1024,384]{2,1,0:T(8,128)(2,1)}, bf16[1,1024,384]{2,1,0:T(8,128)(2,1)S(1)}, u32[]{:S(2)}, u32[]{:S(2)}) %collective-permute-start.1) | collective-permute-done | bytes 786464 | tf_op jit(solution)/shard_map/ppermute | solution.py:1110
  148.9 1.9 pad_maximum_fusion.1.field
  150.9 40.6 %entry.1 = (f32[4096,1024]{1,0:T(8,128)}, bf16[4096,1024]{1,0:T(8,128)(2,1)}, bf16[4096,3072]{1,0:T(8,128)(2,1)}) custom-call(bf16[4096,384]{1,0:T(8,128)(2,1)} %pad_maximum_fusion.1.field, bf16[1024,384]{1,0:T(8,128)(2,1)} %bitcast.109, bf16[1024,3072]{1,0:T(8,128)(2,1)} %bitcast.106, f32[2,8,1024]{2,1,0:T(8,128)} %maximum_maximum_fusion.1.mod.refs_6_), custom_call_target="tpu_custom_call" | custom-call | flops 34359738368 | bytes 50331648 | tf_op jit(solution)/shard_map/entry/pallas_call | solution.py:607
  191.5 124.2 %attend.2 = (bf16[2048,1024]{1,0:T(8,128)(2,1)}, bf16[8,2,2,2048,1024]{4,3,2,1,0:T(8,128)(2,1)}, f32[8,2,2048]{2,1,0:T(2,128)}) custom-call(bf16[4096,3072]{1,0:T(8,128)(2,1)} %get-tuple-element.70.query.key.value.refs_0_.refs_1_.refs_2_, bf16[4096,3072]{1,0:T(8,128)(2,1)} %get-tuple-element.70.query.key.value.refs_0_.refs_1_.refs_2_, ...), custom_call_target="tpu_custom_call" | custom-call | flops 85899345920 | bytes 8388608 | tf_op jit(solution)/shard_map/attend/pallas_call | solution.py:704
  315.6 4.6 constant_dynamic-update-slice_fusion.1
  320.2 67.0 %attend.3 = (bf16[1024,1024]{1,0:T(8,128)(2,1)}, bf16[8,1,2,2048,1024]{4,3,2,1,0:T(8,128)(2,1)}, f32[8,2,1024]{2,1,0:T(2,128)}) custom-call(bf16[4096,3072]{1,0:T(8,128)(2,1)} %get-tuple-element.70.query.key.value.refs_0_.refs_1_.refs_2_, bf16[4096,3072]{1,0:T(8,128)(2,1)} %get-tuple-element.70.query.key.value.refs_0_.refs_1_.refs_2_, ...), custom_call_target="tpu_custom_call" | custom-call | flops 42949672960 | bytes 4194304 | tf_op jit(solution)/shard_map/attend/pallas_call | solution.py:704
  387.3 3.1 constant_dynamic-update-slice_fusion.attended
  390.3 175.8 %middle.1 = (bf16[3072,1024]{1,0:T(8,128)(2,1)}, bf16[3072,4096]{1,0:T(8,128)(2,1)}, bf16[3072,1024]{1,0:T(8,128)(2,1)}, bf16[3072,4096]{1,0:T(8,128)(2,1)}, bf1...) custom-call(bf16[3072,1024]{1,0:T(8,128)(2,1)} %constant_dynamic-upd, ...), custom_call_target="tpu_custom_call" | custom-call | flops 193273528320 | bytes 125829120 | tf_op jit(solution)/shard_map/middle/pallas_call | solution.py:941
  566.2 10.8 convolution_convert_fusion.4
  577.1 2.7 convolution_convert_fusion.6
  579.8 1.9 maximum_maximum_fusion
  581.7 3.0 copy.80
  584.7 33.4 %convolution_convert_fusion = bf16[1024,4096]{1,0:T(8,128)(2,1)} fusion(bf16[3072,1024]{1,0:T(8,128)(2,1)} %get-tuple-element.82, bf16[3072,4096]{1,0:T(8,128)(2,1)} %get-tuple-element.83), kind=kOutput, calls=%fused_computation | convolution fusion | flops 25773998080 | bytes 39845888 | tf_op jit(solution)/shard_map/dot_general | solution.py:57
  618.0 33.4 %convolution_convert_fusion.1 = bf16[1024,4096]{1,0:T(8,128)(2,1)} fusion(bf16[3072,1024]{1,0:T(8,128)(2,1)} %get-tuple-element.80, bf16[3072,4096]{1,0:T(8,128)(2,1)} %get-tuple-element.81), kind=kOutput, calls=%fused_computation.1 | convolution fusion | flops 25773998080 | bytes 39845888 | tf_op jit(solution)/shard_map/dot_general | solution.py:57
  651.5 152.3 %attend_back.2 = (bf16[3072,1024]{1,0:T(8,128)(2,1)}, bf16[4096,1024]{1,0:T(8,128)(2,1)}, bf16[4096,1024]{1,0:T(8,128)(2,1)}, f32[32,4096]{1,0:T(8,128)}, f32[32,4096]{1,0:T(8,128)}) custom-call(bf16[4096,3072]{1,0:T(8,128)(2,1)} %get-tuple-element.70.query.key.value.refs_0_.refs_1_.refs_2_, ...), custom_call_target="tpu_custom_call" | custom-call | flops 137438953472 | bytes 268435456 | tf_op jit(solution)/shard_map/attend_back/pallas_call | solution.py:807
  803.7 74.0 %attend_back.3 = (bf16[3072,1024]{1,0:T(8,128)(2,1)}, bf16[4096,1024]{1,0:T(8,128)(2,1)}, bf16[4096,1024]{1,0:T(8,128)(2,1)}, f32[32,768]{1,0:T(8,128)}, f32[32,768]{1,0:T(8,128)}) custom-call(bf16[4096,3072]{1,0:T(8,128)(2,1)} %get-tuple-element.70.query.key.value.refs_0_.refs_1_.refs_2_, ...), custom_call_target="tpu_custom_call", output_to_operand_aliasing={{0}: (7, {}), {1}: (8, {}), {2}: (9, {})} | custom-call | flops 68719476736 | bytes 134217728 | tf_op jit(solution)/shard_map/attend_back/pallas_call | solution.py:807
  877.8 10.8 fusion.2
  888.6 11.6 %convolution_convert_fusion.3 = bf16[1024,1024]{0,1:T(8,128)(2,1)S(1)} fusion(bf16[4096,1024]{1,0:T(8,128)(2,1)} %get-tuple-element.94, bf16[4096,1024]{1,0:T(8,128)(2,1)S(1)} %copy-done.43), kind=kOutput, calls=%fused_computation.9 | convolution fusion | flops 8590983168 | bytes 18874368 | tf_op jit(solution)/shard_map/dot_general | solution.py:57
  900.2 11.3 %convolution_convert_fusion.2 = bf16[1024,1024]{0,1:T(8,128)(2,1)S(1)} fusion(bf16[4096,1024]{1,0:T(8,128)(2,1)} %get-tuple-element.94, bf16[4096,1024]{1,0:T(8,128)(2,1)S(1)} %bitcast.113), kind=kOutput, calls=%fused_computation.8 | convolution fusion | flops 8590983168 | bytes 18874368 | tf_op jit(solution)/shard_map/dot_general | solution.py:57
  911.5 13.4 %pad_maximum_fusion = bf16[1024,3072]{0,1:T(8,128)(2,1)} fusion(bf16[1024,1024]{0,1:T(8,128)(2,1)S(1)} %convolution_convert_fusion.2, bf16[1024,1024]{0,1:T(8,128)(2,1)S(1)} %convolution_convert_fusion.3, bf16[1024,1024]{0,1:T(8,128)(2,1)S(1)} %fusion.2), kind=kLoop, calls=%fused_computation.2 | loop fusion | flops 18874368 | bytes 12582912 | tf_op jit(solution)/shard_map/concatenate | solution.py:1239
  924.9 8.7 copy.81
  933.7 55.1 %leave.1 = (bf16[4096,1024]{1,0:T(8,128)(2,1)}, f32[8,8,1024]{2,1,0:T(8,128)}, f32[32,1536]{1,0:T(8,128)}, f32[32,1536]{1,0:T(8,128)}) custom-call(bf16[3072,1024]{1,0:T(8,128)(2,1)} %get-tuple-element.90.refs_0_, bf16[4096,1024]{1,0:T(8,128)(2,1)} %get-tuple-element.91.refs_1_, bf16[4096,1024]{1,0:T(8,128)(2,1)} %get-tuple-element.92.refs_2_, ...), custom_call_target="tpu_custom_call" | custom-call | flops 30064771072 | bytes 67108864 | tf_op jit(solution)/shard_map/leave/pallas_call | solution.py:1010
  991.8 9.0 convolution_convert_fusion.5
  1002.1 23.0 %fold_end.1 = (f32[32,384]{1,0:T(8,128)}, f32[169,128]{1,0:T(8,128)}) custom-call(bf16[4,2,2,2,32,384]{5,4,3,2,1,0:T(8,128)(2,1)} %bitcast.94, f32[169,128]{1,0:T(8,128)} %concatenate.105.values), custom_call_target="tpu_custom_call" | custom-call | tf_op jit(solution)/shard_map/fold_end/pallas_call | solution.py:366
  1034.6 2.1 multiply_reduce_fusion
  1044.8 15.1 %small_sum.1 = f32[8,128]{1,0:T(8,128)} custom-call(f32[8,128]{1,0:T(8,128)} %broadcast_in_dim.113.values), custom_call_target="tpu_custom_call" | custom-call | tf_op jit(solution)/shard_map/small_sum/pallas_call | solution.py:172
  1064.9 4.1 multiply_subtract_fusion
  1071.1 3.3 multiply_subtract_fusion.1
  (190 shorter events, 55.8 us)
Async XLA Ops:
  7.2 383.1 %all-gather.6.cloned.1.call-start = ((), (), s32[]{:S(2)}) async-start(), calls=%async_computation | async-start | bytes 2162688 | tf_op jit(solution)/shard_map/all_gather | solution.py:1160
  75.4 314.9 %all-gather.8.cloned.1.call-start = ((), (), s32[]{:S(2)}) async-start(), calls=%async_computation.1 | async-start | bytes 8650752 | tf_op jit(solution)/shard_map/all_gather | solution.py:1160
  77.5 312.8 %all-gather.10.cloned.1.call-start = ((), (), s32[]{:S(2)}) async-start(), calls=%async_computation.2 | async-start | bytes 8650752 | tf_op jit(solution)/shard_map/all_gather | solution.py:1160
  81.9 11.4 %copy-start.40 = (pred[20]{0:T(512)(128)(4,1)S(1)}, pred[20]{0:T(512)(128)(4,1)}, u32[]{:S(2)}) copy-start(pred[20]{0:T(512)(128)(4,1)} %constant.698) | copy-start | bytes 64
  83.3 62.7 %collective-permute-start = (bf16[2,1024,384]{2,1,0:T(8,128)(2,1)}, bf16[2,1024,384]{2,1,0:T(8,128)(2,1)}, u32[]{:S(2)}, u32[]{:S(2)}) collective-permute-start(bf16[2,1024,384]{2,1,0:T(8,128)(2,1)} %pad_maximum_fusion.3), channel_id=1, source_target_pairs={{0,4},{4,0},{1,5},{5,1},{2,6},{6,2},{3,7},{7,3},{8,12},{12,8},{9,1... | collective-permute-start | bytes 4718600 | tf_op jit(solution)/shard_map/ppermute | solution.py:1109
  88.7 54.2 %collective-permute-start.1 = (bf16[1,1024,384]{2,1,0:T(8,128)(2,1)}, bf16[1,1024,384]{2,1,0:T(8,128)(2,1)S(1)}, u32[]{:S(2)}, u32[]{:S(2)}) collective-permute-start(bf16[1,1024,384]{2,1,0:T(8,128)(2,1)} %get-tuple-element.143), channel_id=1, source_target_pairs={{0,4},{4,0},{1,5},{5,1},{2,6},{6,2},{3,7},{7,3},{8,12},{12,8},{9,1... | collective-permute-start | bytes 2359304 | tf_op jit(solution)/shard_map/ppermute | solution.py:1110
  96.5 51.0 %copy-start.7 = (bf16[1,1024,384]{2,1,0:T(8,128)(2,1)S(1)}, bf16[1,1024,384]{2,1,0:T(8,128)(2,1)}, u32[]{:S(2)}) copy-start(bf16[1,1024,384]{2,1,0:T(8,128)(2,1)} %get-tuple-element.145) | copy-start | bytes 2359300
  566.2 10.8 copy-start.41
  566.2 10.8 copy-start.42
  877.7 10.8 copy-start.43
  877.7 22.5 %slice-start = ((s8[8388608]{0:T(1024)(128)(4,1)}), s8[4194304]{0:T(1024)(128)(4,1)S(1)}, s32[]{:S(2)}) async-start(s8[8388608]{0:T(1024)(128)(4,1)} %bitcast.112), calls=%async_computation.3 | async-start | bytes 8388608
  888.6 11.6 %slice-start.1 = ((s8[8388608]{0:T(1024)(128)(4,1)}), s8[4194304]{0:T(1024)(128)(4,1)S(1)}, s32[]{:S(2)}) async-start(s8[8388608]{0:T(1024)(128)(4,1)} %bitcast.112), calls=%async_computation.4 | async-start | bytes 8388608
  933.7 56.2 %copy-start.32 = (pred[20]{0:T(512)(128)(4,1)S(1)}, pred[20]{0:T(512)(128)(4,1)}, u32[]{:S(2)}) copy-start(pred[20]{0:T(512)(128)(4,1)} %get-tuple-element.170) | copy-start | bytes 64
  933.7 56.2 %copy-start.33 = (pred[20]{0:T(512)(128)(4,1)S(1)}, pred[20]{0:T(512)(128)(4,1)}, u32[]{:S(2)}) copy-start(pred[20]{0:T(512)(128)(4,1)} %get-tuple-element.171) | copy-start | bytes 64
  933.7 56.2 %copy-start.34 = (pred[20]{0:T(512)(128)(4,1)S(1)}, pred[20]{0:T(512)(128)(4,1)}, u32[]{:S(2)}) copy-start(pred[20]{0:T(512)(128)(4,1)} %get-tuple-element.172) | copy-start | bytes 64
  933.7 58.0 %copy-start.2 = (bf16[2048,384]{1,0:T(8,128)(2,1)S(1)}, bf16[2048,384]{1,0:T(8,128)(2,1)}, u32[]{:S(2)}) copy-start(bf16[2048,384]{1,0:T(8,128)(2,1)} %copy-done.1) | copy-start | bytes 4718596
  933.7 58.0 %copy-start.5 = (bf16[1024,384]{1,0:T(8,128)(2,1)S(1)}, bf16[1024,384]{1,0:T(8,128)(2,1)}, u32[]{:S(2)}) copy-start(bf16[1024,384]{1,0:T(8,128)(2,1)} %copy-done.4) | copy-start | bytes 2359300
  991.7 36.3 %copy-start.9 = (f32[32,768]{1,0:T(8,128)S(1)}, f32[32,768]{1,0:T(8,128)}, u32[]{:S(2)}) copy-start(f32[32,768]{1,0:T(8,128)} %get-tuple-element.104) | copy-start | bytes 294916
  991.7 36.9 %copy-start.12 = (f32[32,768]{1,0:T(8,128)S(1)}, f32[32,768]{1,0:T(8,128)}, u32[]{:S(2)}) copy-start(f32[32,768]{1,0:T(8,128)} %get-tuple-element.103) | copy-start | bytes 294916
  991.7 45.0 %copy-start = (f32[32,6144]{1,0:T(8,128)S(1)}, f32[32,6144]{1,0:T(8,128)}, u32[]{:S(2)}) copy-start(f32[32,6144]{1,0:T(8,128)} %param.40) | copy-start | bytes 2359300
  991.7 45.0 %copy-start.28 = (f32[32]{0:T(128)S(1)}, f32[32]{0:T(128)}, u32[]{:S(2)}) copy-start(f32[32]{0:T(128)} %get-tuple-element.167) | copy-start | bytes 388
  991.7 46.7 %copy-start.24 = (f32[3,32]{1,0:T(4,128)S(1)}, f32[3,32]{1,0:T(4,128)}, u32[]{:S(2)}) copy-start(f32[3,32]{1,0:T(4,128)} %param.39) | copy-start | bytes 1156
  991.7 70.1 %copy-start.26 = (f32[7,32]{1,0:T(8,128)S(1)}, f32[7,32]{1,0:T(8,128)}, u32[]{:S(2)}) copy-start(f32[7,32]{1,0:T(8,128)} %param.45) | copy-start | bytes 2692
  991.7 71.6 %copy-start.15 = (f32[32,276]{1,0:T(8,128)S(1)}, f32[32,276]{1,0:T(8,128)}, u32[]{:S(2)}) copy-start(f32[32,276]{1,0:T(8,128)} %param.44) | copy-start | bytes 105988
  1000.7 64.1 %copy-start.3 = (f32[2,32,4096]{2,1,0:T(8,128)S(1)}, f32[2,32,4096]{2,1,0:T(8,128)}, u32[]{:S(2)}) copy-start(f32[2,32,4096]{2,1,0:T(8,128)} %param.43) | copy-start | bytes 3145732
  1002.1 66.9 %copy-start.10 = (f32[32,1024]{1,0:T(8,128)S(1)}, f32[32,1024]{1,0:T(8,128)}, u32[]{:S(2)}) copy-start(f32[32,1024]{1,0:T(8,128)} %param.42) | copy-start | bytes 393220
  1026.1 43.8 %copy-start.8 = (f32[32,3072]{1,0:T(8,128)S(1)}, f32[32,3072]{1,0:T(8,128)}, u32[]{:S(2)}) copy-start(f32[32,3072]{1,0:T(8,128)} %param.41) | copy-start | bytes 1179652
  1026.1 43.7 %copy-start.13 = (f32[32,3072]{1,0:T(8,128)S(1)}, f32[32,3072]{1,0:T(8,128)}, u32[]{:S(2)}) copy-start(f32[32,3072]{1,0:T(8,128)} %param.49) | copy-start | bytes 1179652
  1036.7 34.4 %copy-start.29 = (f32[32]{0:T(128)S(1)}, f32[32]{0:T(128)}, u32[]{:S(2)}) copy-start(f32[32]{0:T(128)} %get-tuple-element.168) | copy-start | bytes 388
  1036.7 34.4 %copy-start.30 = (f32[32]{0:T(128)S(1)}, f32[32]{0:T(128)}, u32[]{:S(2)}) copy-start(f32[32]{0:T(128)} %get-tuple-element.169) | copy-start | bytes 388
  1064.9 10.2 copy-start.37
  1064.9 10.2 copy-start.38
  (19 other events, 139.7 us)
Sparse Core Ops, SparseCore 0:
  75.5 60.0 all-gather.5
  139.1 76.4 all-gather.7
  219.0 75.8 all-gather.9
